TPU v7x, 256 devices: a whole 4x4x8 slice. The times are simulated.
256 devices in a mesh: sx: 16 (over z, core), sy: 16 (over x, y).
Axes of the slice: x: 4, y: 4, z: 8, core: 2. Of those that a mesh axis runs over, the one named last changes fastest.
Arguments:
- factor_inv: bfloat16 [32, 16, 1024, 1024], P('sx', 'sy'), as said below
- dirichlet: bfloat16 [32, 16, 1024, 1024], P('sx', 'sy')
- coarse_inv: bfloat16 [4096, 4096], P('sy'), as said below
- domain_sizes: int32 [32, 16], P('sx', 'sy'), may hold values from 32 to 256, as said below
- corner_map: int32 [32, 16, 32], P('sx', 'sy'), may hold values from 0 to 4095
- snow_level: int32 [32, 16, 1024], P('sx', 'sy'), may hold values from 0 to 7
- pressure: bfloat16 [32, 16, 1024, 128], P('sx', 'sy'), may hold values from -6 to 6
Outputs:
- multiplier: float32 [32, 16, 1024, 128], P('sx', 'sy')
- residual: float32 [32, 16, 1024, 128], P('sx', 'sy')
Inputs may be any that keep to these rules, and one draw needn't show every extreme that they name: `domain_sizes`: each edge's active unknowns are its first ones; some subdomain has all 256. `factor_inv`: lower triangular. `coarse_inv`: Symmetric.
All inputs are finite; a program needn't handle non-finite values.
Results may differ from a plain program's by a relative error of at most 0.0034.
Values may be sent and summed in bfloat16 or wider, within the bound.
No kernel may reach another device: no remote copies, remote signals or barrier semaphores. Data moves between devices by JAX's collectives and lax.ppermute only.
A program may use at most 128 MiB of HBM per device.

v0:
```python
import jax
import jax.numpy as jnp
from jax import lax
from jax.sharding import PartitionSpec as P

B = 1024
E = 256
K = 128
CORN = 32
NC = 4096
SUB_DEV = 2
ITERS = 2


def padded(shard, sides, width):
    for axis, dim in sides:
        peers, length = (lax.axis_size(axis), shard.shape[dim])
        up = [(i, (i + 1) % peers) for i in range(peers - 1)]
        down = [(j, i) for i, j in up]
        last = lax.slice_in_dim(shard, length - width, length, axis=dim)
        first = lax.slice_in_dim(shard, 0, width, axis=dim)
        before = lax.ppermute(last, axis, up)
        after = lax.ppermute(first, axis, down)
        shard = jnp.concatenate([before, shard, after], axis=dim)
    return shard


def dense_apply(method, matrix, vector):
    if method == "back":
        return lax.dot_general(
            matrix, vector, (((0,), (0,)), ((), ())), preferred_element_type=jnp.float32
        )
    return jnp.dot(matrix, vector, preferred_element_type=jnp.float32)


def panel_apply(method, matrices, vectors):
    results = []
    for number in range(SUB_DEV):
        matrix = matrices[number, 0]
        vector = vectors[number, 0]
        result = dense_apply(method, matrix, vector)
        results.append(result)
    return jnp.stack(results)[:, None]


def coarse_solve(corners, corner_map, coarse_inv):
    local_terms = jax.ops.segment_sum(
        corners.reshape(-1, K), corner_map.reshape(-1), num_segments=NC
    )
    total = lax.psum(local_terms, ("sx", "sy"))
    solved = jnp.dot(
        coarse_inv, total.astype(jnp.bfloat16), preferred_element_type=jnp.float32
    ).astype(jnp.bfloat16)
    return lax.all_gather(solved, "sy", axis=0, tiled=True)


def jump(interface):
    own_rows = interface[:, 0]
    north_edge = own_rows[:, 0:E]
    south_edge = own_rows[:, E : 2 * E]
    west_edge = own_rows[:, 2 * E : 3 * E]
    east_edge = own_rows[:, 3 * E : 4 * E]
    row_ends = jnp.stack([north_edge[0], south_edge[-1]], axis=0)
    row_rims = padded(row_ends, (("sx", 0),), 1)
    from_above = jnp.concatenate([row_rims[0:1], south_edge[:-1]], axis=0)
    from_below = jnp.concatenate([north_edge[1:], row_rims[3:4]], axis=0)
    side_edges = jnp.stack([west_edge, east_edge], axis=1)
    side_rims = padded(side_edges, (("sy", 1),), 1)
    from_left = side_rims[:, 0]
    from_right = side_rims[:, 3]
    jumped = jnp.concatenate(
        [
            north_edge - from_above,
            south_edge - from_below,
            west_edge - from_left,
            east_edge - from_right,
        ],
        axis=1,
    )
    return jumped[:, None]


def local(factor_inv, dirichlet, coarse_inv, domain_sizes, corner_map, snow_level, pressure):
    offsets = jnp.arange(B, dtype=jnp.int32) % E
    active = (offsets[None, None, :] < domain_sizes[:, :, None]).astype(jnp.float32)[..., None]
    grid_rows = lax.axis_size("sx") * SUB_DEV
    grid_cols = lax.axis_size("sy")
    row_index = (lax.axis_index("sx") * SUB_DEV + jnp.arange(SUB_DEV, dtype=jnp.int32)).astype(
        jnp.float32
    )[:, None]
    col_index = lax.axis_index("sy").astype(jnp.float32)
    drift_factor = 1.0 + 2.0 * (row_index + col_index) / (grid_rows + grid_cols - 2)
    depth = 0.5 + 0.25 * snow_level.astype(jnp.float32)
    loading = (
        pressure.astype(jnp.float32) * depth[..., None] * drift_factor[:, :, None, None] * active
    )
    stride = B // CORN
    multiplier = jnp.zeros_like(loading)
    residual = loading
    for iteration in range(ITERS):
        search = active * panel_apply("pre", dirichlet, residual.astype(jnp.bfloat16))
        inner_term = panel_apply("forward", factor_inv, search.astype(jnp.bfloat16)).astype(
            jnp.bfloat16
        )
        interface = active * panel_apply("back", factor_inv, inner_term)
        corners = interface[:, 0, ::stride]
        coarse_sol = coarse_solve(corners, corner_map, coarse_inv)
        picked = jnp.take(coarse_sol, corner_map[:, 0], axis=0)
        lifted = jnp.stack(
            [
                jnp.dot(
                    factor_inv[number, 0][:, ::stride],
                    picked[number],
                    preferred_element_type=jnp.float32,
                )
                for number in range(SUB_DEV)
            ]
        )
        lifted = lifted[:, None].astype(jnp.bfloat16)
        interface = active * (interface + panel_apply("back", factor_inv, lifted))
        jumped = active * jump(interface)
        cross_term = jnp.sum(residual * jumped, axis=(0, 1, 2))
        energy = jnp.sum(jumped * jumped, axis=(0, 1, 2))
        cross_term, energy = lax.psum((cross_term, energy), ("sx", "sy"))
        step_size = cross_term / (energy + 1e-06)
        multiplier = multiplier + step_size * search
        residual = residual - step_size * jumped
    return (multiplier, residual)


def solution(mesh):
    return jax.shard_map(
        local,
        mesh=mesh,
        in_specs=(
            P("sx", "sy", None, None),
            P("sx", "sy", None, None),
            P("sy", None),
            P("sx", "sy"),
            P("sx", "sy", None),
            P("sx", "sy", None),
            P("sx", "sy", None, None),
        ),
        out_specs=(P("sx", "sy", None, None), P("sx", "sy", None, None)),
        check_vma=False,
    )
```

profile of v0, /device:TPU:1, one launch (start us, length us, event | category | flops | bytes accessed | tf_op | source)
XLA Modules:
  0.0 555.4 jit_solution(17608292898015703791)
XLA Ops:
  10.4 2.6 fusion.18
  15.5 3.4 fusion.25
  19.0 3.6 fusion.24
  25.0 2.3 slice.150
  29.6 88.3 %all-reduce.4 = bf16[4096,128]{1,0:T(8,128)(2,1)S(1)} all-reduce(f32[4096,128]{1,0:T(8,128)} %scatter_custom_fusion), channel_id=1, replica_groups=mesh['sx'=16,'sy'=16] {'sx','sy'}, use_global_device_ids=true, to_apply=%region_1.2 | all-reduce | flops 524288 | bytes 3145728 | tf_op jit(solution)/shard_map/psum | solution.py:50
  119.5 4.6 slice_bitcast_fusion.1
  124.1 4.8 slice.152
  129.0 5.4 slice.154
  134.4 28.9 %all-gather.3.cloned.1.call-done = bf16[4096,128]{0,1:T(8,128)(2,1)} async-done(((bf16[256,128]{0,1:T(8,128)(2,1)}), bf16[4096,128]{0,1:T(8,128)(2,1)}) %all-gather.3.cloned.1.call-update) | async-done | bytes 1048592 | tf_op jit(solution)/shard_map/all_gather | solution.py:54
  165.6 3.1 convolution_bitcast_fusion.2
  168.7 3.0 convolution_bitcast_fusion.3
  173.5 5.1 collective-permute-start
  180.6 4.3 collective-permute-done.1
  186.4 4.0 collective-permute-start.2
  195.1 80.6 %all-reduce.1 = (f32[128]{0:T(128)S(1)}, f32[128]{0:T(128)S(1)}) all-reduce(f32[128]{0:T(128)S(1)} %get-tuple-element.10, f32[128]{0:T(128)S(1)} %get-tuple-element.9), channel_id=1, replica_groups=mesh['sx'=16,'sy'=16] {'sx','sy'}, use_global_device_ids=true, to_apply=%region_3.5 | all-reduce | flops 256 | bytes 2048 | tf_op jit(solution)/shard_map/psum | solution.py:124
  277.5 2.4 fusion.21
  282.5 4.2 fusion.27
  286.7 4.2 fusion.26
  291.0 2.3 maximum_multiply_fusion.6
  293.3 2.3 slice.167
  297.8 81.9 %all-reduce.5 = bf16[4096,128]{1,0:T(8,128)(2,1)} all-reduce(f32[4096,128]{1,0:T(8,128)} %scatter_custom_fusion.1), channel_id=1, replica_groups=mesh['sx'=16,'sy'=16] {'sx','sy'}, use_global_device_ids=true, to_apply=%region_7.9 | all-reduce | flops 524288 | bytes 3145728 | tf_op jit(solution)/shard_map/psum | solution.py:50
  379.8 2.7 fusion.29
  382.5 44.4 %all-gather.5.cloned.1.call-done = bf16[4096,128]{0,1:T(8,128)(2,1)} async-done(((bf16[256,128]{0,1:T(8,128)(2,1)}), bf16[4096,128]{0,1:T(8,128)(2,1)}) %all-gather.5.cloned.1.call-update) | async-done | bytes 1048592 | tf_op jit(solution)/shard_map/all_gather | solution.py:54
  426.9 2.3 copy.25
  431.2 3.1 convolution_bitcast_fusion
  434.3 3.0 convolution_bitcast_fusion.1
  439.1 5.1 collective-permute-start.4
  446.1 4.3 collective-permute-done.5
  451.9 4.0 collective-permute-start.6
  460.6 80.5 %all-reduce = (f32[128]{0:T(128)S(1)}, f32[128]{0:T(128)S(1)}) all-reduce(f32[128]{0:T(128)S(1)} %get-tuple-element.8, f32[128]{0:T(128)S(1)} %get-tuple-element.7), channel_id=1, replica_groups=mesh['sx'=16,'sy'=16] {'sx','sy'}, use_global_device_ids=true, to_apply=%region_9.11 | all-reduce | flops 256 | bytes 2048 | tf_op jit(solution)/shard_map/psum | solution.py:124
  541.0 3.5 multiply_subtract_fusion
  544.6 2.6 copy.28
  (99 shorter events, 44.0 us)
Async XLA Ops:
  7.2 110.7 %copy-start = (bf16[256,4096]{1,0:T(8,128)(2,1)S(1)}, bf16[256,4096]{1,0:T(8,128)(2,1)}, u32[]{:S(2)}) copy-start(bf16[256,4096]{1,0:T(8,128)(2,1)} %param.11) | copy-start | bytes 6291460
  7.2 156.1 %all-gather.3.cloned.1.call-start = ((), (), s32[]{:S(2)}) async-start(), calls=%async_computation | async-start | bytes 1114112 | tf_op jit(solution)/shard_map/all_gather | solution.py:54
  9.4 3.6 copy-start.1
  10.2 2.8 copy-start.19
  13.0 2.5 copy-start.10
  13.8 0.8 copy-start.11
  18.9 5.0 copy-start.14
  19.0 4.2 copy-start.18
  22.6 4.8 copy-start.15
  119.4 307.5 %all-gather.5.cloned.1.call-start = ((), (), s32[]{:S(2)}) async-start(), calls=%async_computation.1 | async-start | bytes 1114112 | tf_op jit(solution)/shard_map/all_gather | solution.py:54
  129.0 39.7 %copy-start.16 = (bf16[1024,32]{1,0:T(8,128)(2,1)}, bf16[1024,32]{1,0:T(8,128)(2,1)S(1)}, u32[]{:S(2)}) copy-start(bf16[1024,32]{1,0:T(8,128)(2,1)S(1)} %slice.152) | copy-start | bytes 196612
  173.5 7.1 %collective-permute-start = (f32[1,256,128]{1,2,0:T(8,128)S(1)}, f32[1,256,128]{1,2,0:T(8,128)S(1)}, u32[]{:S(2)}, u32[]{:S(2)}) collective-permute-start(f32[1,256,128]{1,2,0:T(8,128)S(1)} %get-tuple-element.33), channel_id=1, source_target_pairs={{0,16},{16,32},{32,48},{48,64},{64,80},{80,96},{96,112},{112,128},... | collective-permute-start | bytes 393224 | tf_op jit(solution)/shard_map/ppermute | solution.py:22
  178.6 6.3 %collective-permute-start.1 = (f32[1,256,128]{1,2,0:T(8,128)S(1)}, f32[1,256,128]{1,2,0:T(8,128)S(1)}, u32[]{:S(2)}, u32[]{:S(2)}) collective-permute-start(f32[1,256,128]{1,2,0:T(8,128)S(1)} %get-tuple-element.34), channel_id=1, source_target_pairs={{16,0},{32,16},{48,32},{64,48},{80,64},{96,80},{112,96},{128,112},... | collective-permute-start | bytes 393224 | tf_op jit(solution)/shard_map/ppermute | solution.py:23
  184.9 9.5 %copy-start.2 = (bf16[2,1,1024,128]{2,3,1,0:T(8,128)(2,1)S(1)}, bf16[2,1,1024,128]{2,3,1,0:T(8,128)(2,1)}, u32[]{:S(2)}) copy-start(bf16[2,1,1024,128]{2,3,1,0:T(8,128)(2,1)} %copy-done.1) | copy-start | bytes 1572868
  185.0 9.8 %copy-start.4 = (f32[2,1,256,128]{2,3,1,0:T(8,128)}, f32[2,1,256,128]{2,3,1,0:T(8,128)S(1)}, u32[]{:S(2)}) copy-start(f32[2,1,256,128]{2,3,1,0:T(8,128)S(1)} %get-tuple-element.32) | copy-start | bytes 786436
  185.0 7.5 %collective-permute-start.3 = (f32[2,1,256,128]{2,3,0,1:T(8,128)S(1)}, f32[2,1,256,128]{2,3,0,1:T(8,128)S(1)}, u32[]{:S(2)}, u32[]{:S(2)}) collective-permute-start(f32[2,1,256,128]{2,3,0,1:T(8,128)S(1)} %get-tuple-element.30), channel_id=1, source_target_pairs={{1,0},{2,1},{3,2},{4,3},{5,4},{6,5},{7,6},{8,7},{9,8},{10,9},{11,1... | collective-permute-start | bytes 786440 | tf_op jit(solution)/shard_map/ppermute | solution.py:23
  186.4 7.8 %collective-permute-start.2 = (f32[2,1,256,128]{2,3,0,1:T(8,128)S(1)}, f32[2,1,256,128]{2,3,0,1:T(8,128)S(1)}, u32[]{:S(2)}, u32[]{:S(2)}) collective-permute-start(f32[2,1,256,128]{2,3,0,1:T(8,128)S(1)} %get-tuple-element.31), channel_id=1, source_target_pairs={{0,1},{1,2},{2,3},{3,4},{4,5},{5,6},{6,7},{7,8},{8,9},{9,10},{10,1... | collective-permute-start | bytes 786440 | tf_op jit(solution)/shard_map/ppermute | solution.py:22
  194.3 0.7 copy-start.5
  194.3 0.8 copy-start.6
  275.8 4.2 copy-start.20
  279.9 0.9 copy-start.12
  280.8 0.8 copy-start.13
  429.2 5.2 copy-start.17
  439.1 7.0 %collective-permute-start.4 = (f32[1,256,128]{1,2,0:T(8,128)S(1)}, f32[1,256,128]{1,2,0:T(8,128)S(1)}, u32[]{:S(2)}, u32[]{:S(2)}) collective-permute-start(f32[1,256,128]{1,2,0:T(8,128)S(1)} %get-tuple-element.23), channel_id=1, source_target_pairs={{0,16},{16,32},{32,48},{48,64},{64,80},{80,96},{96,112},{112,128},... | collective-permute-start | bytes 393224 | tf_op jit(solution)/shard_map/ppermute | solution.py:22
  444.2 6.3 %collective-permute-start.5 = (f32[1,256,128]{1,2,0:T(8,128)S(1)}, f32[1,256,128]{1,2,0:T(8,128)S(1)}, u32[]{:S(2)}, u32[]{:S(2)}) collective-permute-start(f32[1,256,128]{1,2,0:T(8,128)S(1)} %get-tuple-element.24), channel_id=1, source_target_pairs={{16,0},{32,16},{48,32},{64,48},{80,64},{96,80},{112,96},{128,112},... | collective-permute-start | bytes 393224 | tf_op jit(solution)/shard_map/ppermute | solution.py:23
  450.6 9.2 %copy-start.7 = (f32[2,1,256,128]{2,3,0,1:T(8,128)}, f32[2,1,256,128]{2,3,0,1:T(8,128)S(1)}, u32[]{:S(2)}) copy-start(f32[2,1,256,128]{2,3,0,1:T(8,128)S(1)} %get-tuple-element.22) | copy-start | bytes 786436
  450.6 7.4 %collective-permute-start.7 = (f32[2,1,256,128]{2,3,0,1:T(8,128)S(1)}, f32[2,1,256,128]{2,3,0,1:T(8,128)S(1)}, u32[]{:S(2)}, u32[]{:S(2)}) collective-permute-start(f32[2,1,256,128]{2,3,0,1:T(8,128)S(1)} %get-tuple-element.20), channel_id=1, source_target_pairs={{1,0},{2,1},{3,2},{4,3},{5,4},{6,5},{7,6},{8,7},{9,8},{10,9},{11,1... | collective-permute-start | bytes 786440 | tf_op jit(solution)/shard_map/ppermute | solution.py:23
  451.9 7.8 %collective-permute-start.6 = (f32[2,1,256,128]{2,3,0,1:T(8,128)S(1)}, f32[2,1,256,128]{2,3,0,1:T(8,128)S(1)}, u32[]{:S(2)}, u32[]{:S(2)}) collective-permute-start(f32[2,1,256,128]{2,3,0,1:T(8,128)S(1)} %get-tuple-element.21), channel_id=1, source_target_pairs={{0,1},{1,2},{2,3},{3,4},{4,5},{5,6},{6,7},{7,8},{8,9},{9,10},{10,1... | collective-permute-start | bytes 786440 | tf_op jit(solution)/shard_map/ppermute | solution.py:22
  459.8 0.7 copy-start.8
  459.8 0.8 copy-start.9
  544.6 2.6 copy-start.3
Sparse Core Ops, SparseCore 0:
  119.5 43.7 all-gather.2
  382.6 44.2 all-gather.4
where the time goes:
time: 557 us; the launch traced here: 555 us
  blocking collectives  331 us (59%)
  waiting for transfers between devices  89.6 us (16%)
  matrix products  38.4 us (7%)
  local copies, waits for them, and re-layouts  34.5 us (6%)
  starting transfers between devices  24.9 us (4%)
  other arithmetic  22.2 us (4%)
  between operations  14.5 us (3%)
    psum x2, blocking collectives, coarse_solve(): total = lax.psum(local_terms, ('sx', 'sy'))  170 us
    psum x2, blocking collectives, local(): cross_term, energy = lax.psum((cross_term, energy), ('sx', 'sy'))  161 us
    all_gather x2, waiting for transfers between devices, coarse_solve(): return lax.all_gather(solved, 'sy', axis=0, tiled=True)  73.3 us
    dot_general x8, matrix products, dense_apply(): lax.dot_general(matrix, vector, (((0,), (0,)), ((), ())), preferred_eleme...  27.6 us
    ppermute x4, starting transfers between devices, padded(): before = lax.ppermute(last, axis, up)  18.2 us
    ppermute x4, waiting for transfers between devices, padded(): after = lax.ppermute(first, axis, down)  12.8 us
  transfers between devices with their start and end apart: 10, of which 8 were waited for; matrix products, arithmetic and copies ran while one was open for 3% of the time, Pallas kernels for 0%

commit v1 on v0

v1 whole, which is shorter than its diff:
```python
import jax
import jax.numpy as jnp
from jax import lax
from jax.experimental import pallas as pl
from jax.experimental.pallas import tpu as pltpu
from jax.sharding import Mesh
from jax.sharding import PartitionSpec as P

B = 1024
E = 256
K = 128
CORN = 32
NC = 4096
GR = 32
GC = 16
ZS = 8
CS = 2
XS = 4
YS = 4
SY = XS * YS
STRIDE = B // CORN
ROWS = 80
HALF = 128
F32 = jnp.float32
BF16 = jnp.bfloat16
VMEM_LIMIT = 48 * 1024 * 1024

VM = pl.BlockSpec(memory_space=pltpu.VMEM)
SM = pl.BlockSpec(memory_space=pltpu.SMEM)
HB = pl.BlockSpec(memory_space=pl.ANY)


def dot(a, b):
    return jnp.dot(a, b, preferred_element_type=F32)


def iota(shape, dim):
    return lax.broadcasted_iota(jnp.int32, shape, dim)


def call(kernel, outs, in_specs, scratch=()):
    return pl.pallas_call(
        kernel,
        out_shape=[jax.ShapeDtypeStruct(shape, dtype) for shape, dtype in outs],
        in_specs=in_specs,
        out_specs=[VM] * len(outs),
        scratch_shapes=list(scratch),
        compiler_params=pltpu.CompilerParams(vmem_limit_bytes=VMEM_LIMIT),
    )


def split2(value):
    high = value.astype(BF16)
    low = (value - high.astype(F32)).astype(BF16)
    return high, low


def split3(value):
    high, _ = split2(value)
    rest = value - high.astype(F32)
    mid, low = split2(rest)
    return high, mid, low


def active_mask(size):
    return ((iota((B, K), 0) & (E - 1)) < size).astype(F32)


def rows_of(shape, rows):
    index = iota(shape, 0)
    result = jnp.zeros(shape, F32)
    for number, row in enumerate(rows):
        result = jnp.where(index == number, jnp.broadcast_to(row.astype(F32), shape), result)
    return result


def write_payload(pay, interface, tail):
    corners = [interface[s, pl.ds(0, CORN, stride=STRIDE), :].astype(BF16) for s in range(2)]
    block = jnp.concatenate(corners + [tail.astype(BF16)], axis=0)
    for dest in range(SY):
        pay[dest] = block


def write_edges(refs, interface, extra):
    north, south, west, east = refs

    def packed(s, edge):
        rows = pl.ds(edge * E, E)
        parts = list(split2(interface[s, rows, :]))
        if extra is not None:
            parts.append(extra[s, rows, :])
        return jnp.concatenate(parts, axis=1)

    north[...] = packed(0, 0)
    south[...] = packed(1, 1)
    for s in range(2):
        west[s] = packed(s, 2)
        east[s] = packed(s, 3)


def first_kernel(sizes, snow, cmap, press, dir_hbm, fac_hbm,
                 res, search, inter, gram, pay, north, south, west, east,
                 dbuf, lbuf, sems):
    copies = []
    for s in range(2):
        copies.append(pltpu.make_async_copy(dir_hbm.at[s], dbuf.at[s], sems.at[s]))
        copies.append(pltpu.make_async_copy(fac_hbm.at[s], lbuf.at[s], sems.at[2 + s]))
    copies[0].start()
    copies[2].start()
    copies[1].start()
    copies[3].start()
    grid_row = lax.axis_index("z") * (2 * CS) + lax.axis_index("core") * 2
    grid_col = lax.axis_index("x") * YS + lax.axis_index("y")
    lane = iota((B, K), 1)
    masks = [active_mask(sizes[s]) for s in range(2)]
    pick_col = jnp.where((iota((B, K), 0) == lane * STRIDE) & (lane < CORN), 1.0, 0.0).astype(BF16)
    for s in range(2):
        place = jnp.full((K, B), grid_row + s + grid_col, jnp.int32).astype(F32)
        drift = 1.0 + 2.0 * place / (GR + GC - 2)
        depth = 0.5 + 0.25 * jnp.broadcast_to(snow[s : s + 1, :], (K, B)).astype(F32)
        res[s] = press[s].astype(F32) * jnp.transpose(depth) * jnp.transpose(drift) * masks[s]
    cm = cmap[...]
    for s in range(2):
        copies[2 * s].wait()
        found = masks[s] * dot(dbuf[s], res[s].astype(BF16))
        search[s] = found
    for s in range(2):
        copies[2 * s + 1].wait()
        right = jnp.concatenate([search[s].astype(BF16), pick_col], axis=1)
        inner = jnp.transpose(dot(lbuf[s], right)).astype(BF16)
        back = jnp.transpose(dot(inner, lbuf[s]))
        inter[s] = masks[s] * back[:, :K]
        ghigh, glow = split2(masks[s] * back[:, K:])
        square = jnp.transpose(jnp.broadcast_to(cm[s : s + 1, :], (K, K)))
        column = jnp.concatenate([square] * (B // K), axis=0)
        digits = jnp.where(lane < 96, column >> 8, column & 255).astype(F32)
        low_moved = pltpu.roll(glow.astype(F32), CORN, axis=1)
        gram[s] = jnp.where(
            lane < CORN, ghigh.astype(F32), jnp.where(lane < 2 * CORN, low_moved, digits)
        ).astype(BF16)
    both = cm[2:3, :]
    tail = rows_of((16, K), [(both >> 8).astype(F32), (both & 255).astype(F32)])
    write_payload(pay, inter, tail)
    write_edges((north, south, west, east), inter, gram)


def coarse_rows(rec):
    return jnp.concatenate([rec[b, 0:64, :] for b in range(SY)], axis=0)


def halves(value, stats, own, snd):
    mine = lax.axis_index("core") == 0
    tail = rows_of((8, K), stats)
    own[0:HALF] = jnp.where(mine, value[:HALF], value[HALF:])
    snd[0:HALF] = jnp.where(mine, value[HALF:], value[:HALF])
    own[HALF : HALF + 8] = tail
    snd[HALF : HALF + 8] = tail


def coarse_first_kernel(rec, coarse, own, snd, picked_inv, acc):
    lane = iota((1, K), 1)
    tails = [rec[b, 64:80, :].astype(F32) for b in range(SY)]

    def row(number):
        parts = [
            jnp.where(lane < 64, tails[2 * m][number : number + 1], tails[2 * m + 1][number : number + 1])
            for m in range(SY // 2)
        ]
        return jnp.concatenate(parts, axis=1)

    high, low = row(0), row(1)
    low_hot = jnp.where(iota((E, B), 0) == low.astype(jnp.int32), 1.0, 0.0).astype(BF16)
    for digit in range(NC // E):
        part = dot(coarse[:, digit * E : (digit + 1) * E], low_hot)
        part = jnp.where(high == digit, part, 0.0)
        if digit == 0:
            acc[...] = part
        else:
            acc[...] += part
    matrix = acc[...].astype(BF16)
    picked_inv[...] = matrix
    halves(dot(matrix, coarse_rows(rec)), [], own, snd)


def coarse_next_kernel(rec, picked_inv, own, snd):
    value = dot(picked_inv[...], coarse_rows(rec))
    tails = sum(rec[b, 64:80, :].astype(F32) for b in range(SY))
    stats = [tails[q : q + 1] + tails[q + 1 : q + 2] + tails[q + 2 : q + 3] for q in (2, 5)]
    halves(value, stats, own, snd)


def pair_sum_kernel(own, rcv, pay):
    total = own[...] + rcv[...]
    rows = []
    for q in range(2):
        rows += list(split3(total[HALF + q : HALF + q + 1]))
    tail = rows_of((16, K), rows).astype(BF16)
    block = jnp.concatenate([total[:HALF].astype(BF16), tail], axis=0)
    for dest in range(ZS):
        pay[dest] = block


def z_sum_kernel(rec, pay, stats):
    total = sum(rec[z].astype(F32) for z in range(ZS))
    block = total[:HALF].astype(BF16)
    for dest in range(SY):
        pay[dest] = block
    rows = total[HALF:]
    stats[...] = rows_of(
        (8, K), [rows[q : q + 1] + rows[q + 1 : q + 2] + rows[q + 2 : q + 3] for q in (0, 3)]
    )


def jumps(sizes, sol_own, sol_other, inter, gram, edges, grams):
    core = lax.axis_index("core")
    in_north, in_south, in_west, in_east = edges
    gram_edges = [gram[0, 0:CORN, :], gram[1, 0:CORN, :]]
    gram_edges += [g[0:CORN, :] for g in grams[:2]]
    gram_edges += [g[s, 0:CORN, :] for g in grams[2:] for s in range(2)]
    digits = jnp.concatenate(gram_edges, axis=0).astype(F32)
    cm = digits[:, 64:65].astype(jnp.int32) * 256 + digits[:, 96:97].astype(jnp.int32)
    half = ((cm >> 7) & 1) ^ core
    place = half * 2048 + (cm >> 8) * HALF + (cm & (HALF - 1))
    hot = jnp.where(iota((8 * CORN, NC), 1) == place, 1.0, 0.0).astype(BF16)
    picks = (dot(hot[:, :2048], sol_own[...]) + dot(hot[:, 2048:], sol_other[...])).astype(BF16)
    zero = jnp.zeros((2 * CORN, K), BF16)

    def stacked(number):
        rows = picks[number * CORN : (number + 1) * CORN]
        return jnp.concatenate([rows, rows, zero], axis=0)

    full = [inter[s] + dot(gram[s], stacked(s)) for s in range(2)]

    def arrived(edge, gedge, number):
        return edge[:, :K].astype(F32) + edge[:, K : 2 * K].astype(F32) + dot(gedge, stacked(number))

    above = [arrived(in_north[...], grams[0], 2), full[0][E : 2 * E]]
    below = [full[1][0:E], arrived(in_south[...], grams[1], 3)]
    left = [arrived(in_west[s], grams[2][s], 4 + s) for s in range(2)]
    right = [arrived(in_east[s], grams[3][s], 6 + s) for s in range(2)]
    return [
        active_mask(sizes[s]) * (full[s] - jnp.concatenate([above[s], below[s], left[s], right[s]], axis=0))
        for s in range(2)
    ]


def second_kernel(sizes, sol_own, sol_other, inter, gram, in_north, in_south, in_west, in_east,
                  res, dir_hbm, fac_hbm,
                  jump0, prod, inter1, pay, north, south, west, east,
                  dbuf, lbuf, sems):
    copies = []
    for s in range(2):
        copies.append(pltpu.make_async_copy(dir_hbm.at[s], dbuf.at[s], sems.at[s]))
        copies.append(pltpu.make_async_copy(fac_hbm.at[s], lbuf.at[s], sems.at[2 + s]))
    copies[0].start()
    copies[2].start()
    copies[1].start()
    copies[3].start()
    grams = [in_north[:, 2 * K :], in_south[:, 2 * K :], in_west[:, :, 2 * K :], in_east[:, :, 2 * K :]]
    jumped = jumps(sizes, sol_own, sol_other, inter, gram, (in_north, in_south, in_west, in_east), grams)
    cross = jnp.zeros((1, K), F32)
    energy = jnp.zeros((1, K), F32)
    for s in range(2):
        jump0[s] = jumped[s]
        cross += jnp.sum(res[s] * jumped[s], axis=0, keepdims=True)
        energy += jnp.sum(jumped[s] * jumped[s], axis=0, keepdims=True)
    masks = [active_mask(sizes[s]) for s in range(2)]
    for s in range(2):
        copies[2 * s].wait()
        wide = dot(dbuf[s], jnp.concatenate(split2(jump0[s]), axis=1))
        prod[s] = masks[s] * (wide[:, :K] + wide[:, K:])
    for s in range(2):
        copies[2 * s + 1].wait()
        wide = dot(lbuf[s], jnp.concatenate(split2(prod[s]), axis=1))
        inner = jnp.transpose(wide[:, :K] + wide[:, K:])
        wide = dot(jnp.concatenate(split2(inner), axis=0), lbuf[s])
        inter1[s] = masks[s] * jnp.transpose(wide[:K] + wide[K:])
    rows = [jnp.zeros((1, K), F32)] * 2 + list(split3(cross)) + list(split3(energy))
    write_payload(pay, inter1, rows_of((16, K), rows))
    write_edges((north, south, west, east), inter1, None)


def third_kernel(sizes, sol_own, sol_other, inter, gram, in_north, in_south, in_west, in_east,
                 old_north, old_south, old_west, old_east, stats, res, search, jump0, prod,
                 res1, jump1, mult1, search1, pay):
    grams = [old_north[:, 2 * K :], old_south[:, 2 * K :], old_west[:, :, 2 * K :], old_east[:, :, 2 * K :]]
    again = jumps(sizes, sol_own, sol_other, inter, gram, (in_north, in_south, in_west, in_east), grams)
    step = stats[0:1] / (stats[1:2] + 1e-06)
    cross = jnp.zeros((1, K), F32)
    energy = jnp.zeros((1, K), F32)
    for s in range(2):
        res1[s] = res[s] - step * jump0[s]
        jumped = jump0[s] - step * again[s]
        jump1[s] = jumped
        mult1[s] = step * search[s]
        search1[s] = search[s] - step * prod[s]
        cross += jnp.sum(res1[s] * jumped, axis=0, keepdims=True)
        energy += jnp.sum(jumped * jumped, axis=0, keepdims=True)
    block = rows_of((8, K), [cross, energy])
    for dest in range(CS * XS):
        pay[dest] = block


def partial_kernel(rec, pay):
    total = sum(rec[b] for b in range(CS * XS))
    for dest in range(ZS * YS):
        pay[dest] = total


def last_kernel(rec, res1, jump1, mult1, search1, mult, res):
    total = sum(rec[b] for b in range(ZS * YS))
    step = total[0:1] / (total[1:2] + 1e-06)
    for s in range(2):
        mult[s] = mult1[s] + step * search1[s]
        res[s] = res1[s] - step * jump1[s]


def all_to_all(value, axes):
    return lax.all_to_all(value, axes, split_axis=0, concat_axis=0)


def swap(value):
    return lax.ppermute(value, "core", [(0, 1), (1, 0)])


def exchange(north, south, west, east):
    rows_up = [(i, i + 1) for i in range(ZS * CS - 1)]
    cols_up = [(j, j + 1) for j in range(SY - 1)]
    down = lambda pairs: [(b, a) for a, b in pairs]
    in_north = lax.ppermute(south, ("z", "core"), rows_up)
    in_south = lax.ppermute(north, ("z", "core"), down(rows_up))
    in_west = lax.ppermute(east, ("x", "y"), cols_up)
    in_east = lax.ppermute(west, ("x", "y"), down(cols_up))
    return in_north, in_south, in_west, in_east


def coarse_solution(own, snd):
    rcv = swap(snd)
    (pay,) = call(pair_sum_kernel, [((ZS, HALF + 16, K), BF16)], [VM] * 2)(own, rcv)
    rec = all_to_all(pay, "z")
    pay, stats = call(z_sum_kernel, [((SY, HALF, K), BF16), ((8, K), F32)], [VM])(rec)
    sol = all_to_all(pay, ("x", "y")).reshape(SY * HALF, K)
    return sol, swap(sol), stats


def local(factor_inv, dirichlet, coarse_inv, domain_sizes, corner_map, snow_level, pressure):
    factor = factor_inv.reshape(2, B, B)
    pre = dirichlet.reshape(2, B, B)
    sizes = domain_sizes.reshape(2)
    cm = corner_map.reshape(2, CORN)
    cmap = jnp.concatenate(
        [jnp.tile(cm, (1, 4)), jnp.tile(cm.reshape(1, 2 * CORN), (1, 2)), jnp.zeros((5, K), jnp.int32)], axis=0
    )
    whole = ((2, B, K), F32)
    bufs = [pltpu.VMEM((2, B, B), BF16), pltpu.VMEM((2, B, B), BF16), pltpu.SemaphoreType.DMA((4,))]

    def edge_outs(width):
        return [((E, width), BF16)] * 2 + [((2, E, width), BF16)] * 2

    res, search, inter, gram, pay, *edges = call(
        first_kernel,
        [whole, whole, whole, ((2, B, K), BF16), ((SY, ROWS, K), BF16)] + edge_outs(3 * K),
        [SM, VM, VM, VM, HB, HB],
        bufs,
    )(sizes, snow_level.reshape(2, B), cmap, pressure.reshape(2, B, K), pre, factor)
    arrived = exchange(*edges)
    rec = all_to_all(pay, ("x", "y"))
    own, snd, picked_inv = call(
        coarse_first_kernel,
        [((HALF + 8, K), F32)] * 2 + [((E, B), BF16)],
        [VM] * 2,
        [pltpu.VMEM((E, B), F32)],
    )(rec, coarse_inv)
    sol_own, sol_other, _ = coarse_solution(own, snd)
    jump0, prod, inter1, pay, *edges = call(
        second_kernel,
        [whole, whole, whole, ((SY, ROWS, K), BF16)] + edge_outs(2 * K),
        [SM] + [VM] * 9 + [HB] * 2,
        bufs,
    )(sizes, sol_own, sol_other, inter, gram, *arrived, res, pre, factor)
    arrived1 = exchange(*edges)
    rec = all_to_all(pay, ("x", "y"))
    own, snd = call(coarse_next_kernel, [((HALF + 8, K), F32)] * 2, [VM] * 2)(rec, picked_inv)
    sol_own, sol_other, stats = coarse_solution(own, snd)
    res1, jump1, mult1, search1, pay = call(
        third_kernel, [whole] * 4 + [((CS * XS, 8, K), F32)], [SM] + [VM] * 17
    )(sizes, sol_own, sol_other, inter1, gram, *arrived1, *arrived, stats, res, search, jump0, prod)
    rec = all_to_all(pay, ("core", "x"))
    (pay,) = call(partial_kernel, [((ZS * YS, 8, K), F32)], [VM])(rec)
    rec = all_to_all(pay, ("z", "y"))
    mult, res = call(last_kernel, [whole] * 2, [VM] * 5)(rec, res1, jump1, mult1, search1)
    return mult.reshape(2, 1, B, K), res.reshape(2, 1, B, K)


def solution(mesh):
    fine = Mesh(mesh.devices.reshape(ZS, CS, XS, YS), ("z", "core", "x", "y"))
    rows, cols = ("z", "core"), ("x", "y")
    return jax.shard_map(
        local,
        mesh=fine,
        in_specs=(
            P(rows, cols, None, None),
            P(rows, cols, None, None),
            P(cols, None),
            P(rows, cols),
            P(rows, cols, None),
            P(rows, cols, None),
            P(rows, cols, None, None),
        ),
        out_specs=(P(rows, cols, None, None), P(rows, cols, None, None)),
        check_vma=False,
    )
```

time: 557 us -> 200 us (0.36)
  blocking collectives: 331 us -> 115 us
  waiting for transfers between devices: 89.6 us -> 12.9 us
  matrix products: 38.4 us -> 0 us
  Pallas kernels: 0 us -> 33.4 us
  local copies, waits for them, and re-layouts: 34.5 us -> 9.34 us
  other arithmetic: 22.2 us -> 1.41 us
  between operations: 14.5 us -> 0.82 us
    psum x4 -> x0, blocking collectives: 331 us -> none  [the longest x2 170 us: coarse_solve(): total = lax.psum(local_terms, ('sx', 'sy'))]
    all_to_all x0 -> x8, blocking collectives: none -> 115 us  [all_to_all(): return lax.all_to_all(value, axes, split_axis=0, concat_axis=0)]
    all_gather x2 -> x0, waiting for transfers between devices: 73.3 us -> none  [coarse_solve(): return lax.all_gather(solved, 'sy', axis=0, tiled=True)]
    dot_general x14 -> x0, matrix products: 38.4 us -> none  [the longest x8 27.6 us: dense_apply(): lax.dot_general(matrix, vector, (((0,), (0,)), ((), ())), preferred_eleme...]
    pallas_call x0 -> x11, Pallas kernels: none -> 33.4 us  [the longest x1 12.6 us: local(): call(second_kernel, [whole, whole, whole, ((SY, ROWS, K), BF16)] + edge_o...]
    slice x8 -> x0, local copies, waits for them, and re-layouts: 14.9 us -> none  [the longest x2 10.2 us: local(): factor_inv[number, 0][:, ::stride]]
    mul x4 -> x0, other arithmetic: 6.92 us -> none  [the longest x2 3.47 us: local(): interface = active * (interface + panel_apply('back', factor_inv, lifted))]
    ppermute x8 -> x12, waiting for transfers between devices: 16.3 us -> 12.9 us  [the longest x2 9.21 us: exchange(): in_south = lax.ppermute(north, ('z', 'core'), down(rows_up))]
  transfers between devices with their start and end apart: 10 -> 12, of which waited for: 8 -> 5; matrix products, arithmetic and copies ran while one was open for 3% -> 0% of each run, Pallas kernels for 0% -> 0%
where the time goes in v1:
time: 200 us; the launch traced here: 199 us
  blocking collectives  115 us (58%)
  Pallas kernels  33.4 us (17%)
  starting transfers between devices  26.4 us (13%)
  waiting for transfers between devices  12.9 us (6%)
  local copies, waits for them, and re-layouts  9.34 us (5%)
    all_to_all x8, blocking collectives, all_to_all(): return lax.all_to_all(value, axes, split_axis=0, concat_axis=0)  115 us
    pallas_call x1, Pallas kernels, local(): call(second_kernel, [whole, whole, whole, ((SY, ROWS, K), BF16)] + edge_o...  12.6 us
    ppermute x4, starting transfers between devices, swap(): return lax.ppermute(value, 'core', [(0, 1), (1, 0)])  10.6 us
    pallas_call x1, Pallas kernels, local(): call(first_kernel, [whole, whole, whole, ((2, B, K), BF16), ((SY, ROWS, K...  10 us
    ppermute x2, waiting for transfers between devices, exchange(): in_south = lax.ppermute(north, ('z', 'core'), down(rows_up))  9.21 us
    unnamed x24, local copies, waits for them, and re-layouts  8.32 us
    pallas_call x1, Pallas kernels, local(): call(third_kernel, [whole] * 4 + [((CS * XS, 8, K), F32)], [SM] + [VM] * 17)  5.58 us
    ppermute x2, starting transfers between devices, exchange(): in_south = lax.ppermute(north, ('z', 'core'), down(rows_up))  4.61 us
  transfers between devices with their start and end apart: 12, of which 5 were waited for; matrix products, arithmetic and copies ran while one was open for 0% of the time, Pallas kernels for 0%

profile of v1, /device:TPU:1, one launch (start us, length us, event | category | flops | bytes accessed | tf_op | source)
XLA Modules:
  0.0 199.2 jit_solution(8494954238848924940)
XLA Ops:
  1.1 1.3 reduce.3
  4.3 1.0 copy-done.8
  6.0 10.0 %shard_map.86 = (f32[2,1024,128]{2,1,0:T(8,128)S(1)}, f32[2,1024,128]{2,1,0:T(8,128)S(1)}, f32[2,1024,128]{2,1,0:T(8,128)S(1)}, bf16[2,1024,128]{2,1,0:T(8,128)(...) custom-call(s32[2]{0:T(128)S(1)} %bitcast.22, ...), custom_call_target="tpu_custom_call" | custom-call | tf_op jit(solution)/shard_map/pallas_call | solution.py:360
  18.9 15.3 %all_to_all.40.rec = bf16[16,80,128]{2,1,0:T(8,128)(2,1)S(1)} all-to-all(bf16[16,80,128]{2,1,0:T(8,128)(2,1)S(1)} %get-tuple-element.34), channel_id=1, replica_groups=mesh['z'=8,'core'=2,'x'=4,'y'=4] {'x','y'}, dimensions={0} | all-to-all | bytes 655360 | tf_op jit(solution)/shard_map/all_to_all | solution.py:319
  34.3 2.7 %shard_map.87 = (f32[136,128]{1,0:T(8,128)S(1)}, f32[136,128]{1,0:T(8,128)S(1)}, bf16[256,1024]{1,0:T(8,128)(2,1)S(1)}) custom-call(bf16[16,80,128]{2,1,0:T(8,128)(2,1)S(1)} %all_to_all.40.rec, bf16[256,4096]{1,0:T(8,128)(2,1)S(1)} %copy-done.1), custom_call_target="tpu_custom_call" | custom-call | tf_op jit(solution)/shard_map/pallas_call | solution.py:368
  36.9 2.4 %collective-permute-start = (f32[136,128]{1,0:T(8,128)S(1)}, f32[136,128]{1,0:T(8,128)S(1)}, u32[]{:S(2)}, u32[]{:S(2)}) collective-permute-start(f32[136,128]{1,0:T(8,128)S(1)} %get-tuple-element.36), channel_id=1, source_target_pairs={{0,16},{16,0},{1,17},{17,1},{2,18},{18,2},{3,19},{19,3},{4,20},{20... | collective-permute-start | bytes 208904 | tf_op jit(solution)/shard_map/ppermute | solution.py:323
  40.3 20.2 %all_to_all.41.rec = bf16[8,144,128]{2,1,0:T(8,128)(2,1)S(1)} all-to-all(bf16[8,144,128]{2,1,0:T(8,128)(2,1)S(1)} %shard_map.88), channel_id=1, replica_groups=mesh['z'=8,'core'=2,'x'=4,'y'=4] {'z'}, dimensions={0} | all-to-all | bytes 589824 | tf_op jit(solution)/shard_map/all_to_all | solution.py:319
  61.1 12.1 %all_to_all.42 = bf16[16,128,128]{2,1,0:T(8,128)(2,1)S(1)} all-to-all(bf16[16,128,128]{2,1,0:T(8,128)(2,1)S(1)} %get-tuple-element.37), channel_id=1, replica_groups=mesh['z'=8,'core'=2,'x'=4,'y'=4] {'x','y'}, dimensions={0} | all-to-all | bytes 1048576 | tf_op jit(solution)/shard_map/all_to_all | solution.py:319
  73.1 3.5 %collective-permute-start.1 = (bf16[2048,128]{1,0:T(8,128)(2,1)S(1)}, bf16[2048,128]{1,0:T(8,128)(2,1)S(1)}, u32[]{:S(2)}, u32[]{:S(2)}) collective-permute-start(bf16[2048,128]{1,0:T(8,128)(2,1)S(1)} %bitcast.18), channel_id=1, source_target_pairs={{0,16},{16,0},{1,17},{17,1},{2,18},{18,2},{3,19},{19,3},{4,20},{20... | collective-permute-start | bytes 1572872 | tf_op jit(solution)/shard_map/ppermute | solution.py:323
  76.7 2.2 %collective-permute-start.4 = (bf16[2,256,384]{2,1,0:T(8,128)(2,1)S(1)}, bf16[2,256,384]{2,1,0:T(8,128)(2,1)S(1)}, u32[]{:S(2)}, u32[]{:S(2)}) collective-permute-start(bf16[2,256,384]{2,1,0:T(8,128)(2,1)S(1)} %get-tuple-element.42), channel_id=1, source_target_pairs={{0,1},{1,2},{2,3},{3,4},{4,5},{5,6},{6,7},{7,8},{8,9},{9,10},{10,1... | collective-permute-start | bytes 1179656 | tf_op jit(solution)/shard_map/ppermute | solution.py:332
  78.9 1.3 collective-permute-start.5
  80.2 1.9 collective-permute-start.2
  82.1 2.6 %collective-permute-start.3 = (bf16[256,384]{1,0:T(8,128)(2,1)S(1)}, bf16[256,384]{1,0:T(8,128)(2,1)S(1)}, u32[]{:S(2)}, u32[]{:S(2)}) collective-permute-start(bf16[256,384]{1,0:T(8,128)(2,1)S(1)} %get-tuple-element.41), channel_id=1, source_target_pairs={{16,0},{32,16},{48,32},{64,48},{80,64},{96,80},{112,96},{128,112},... | collective-permute-start | bytes 589832 | tf_op jit(solution)/shard_map/ppermute | solution.py:331
  84.7 4.7 %collective-permute-done.3.in_south.old_south = bf16[256,384]{1,0:T(8,128)(2,1)S(1)} collective-permute-done((bf16[256,384]{1,0:T(8,128)(2,1)S(1)}, bf16[256,384]{1,0:T(8,128)(2,1)S(1)}, u32[]{:S(2)}, u32[]{:S(2)}) %collective-permute-start.3) | collective-permute-done | bytes 196640 | tf_op jit(solution)/shard_map/ppermute | solution.py:331
  89.4 1.8 collective-permute-done.5.in_east.old_east
  91.2 12.6 %shard_map.90 = (f32[2,1024,128]{2,1,0:T(8,128)S(1)}, f32[2,1024,128]{2,1,0:T(8,128)S(1)}, f32[2,1024,128]{2,1,0:T(8,128)}, bf16[16,80,128]{2,1,0:T(8,128)(2,1)S...) custom-call(s32[2]{0:T(128)S(1)} %bitcast.23, ...), custom_call_target="tpu_custom_call" | custom-call | tf_op jit(solution)/shard_map/pallas_call | solution.py:375
  103.9 15.0 %all_to_all.43.rec = bf16[16,80,128]{2,1,0:T(8,128)(2,1)S(1)} all-to-all(bf16[16,80,128]{2,1,0:T(8,128)(2,1)S(1)} %get-tuple-element.45), channel_id=1, replica_groups=mesh['z'=8,'core'=2,'x'=4,'y'=4] {'x','y'}, dimensions={0} | all-to-all | bytes 655360 | tf_op jit(solution)/shard_map/all_to_all | solution.py:319
  119.1 2.4 %collective-permute-start.6 = (f32[136,128]{1,0:T(8,128)S(1)}, f32[136,128]{1,0:T(8,128)S(1)}, u32[]{:S(2)}, u32[]{:S(2)}) collective-permute-start(f32[136,128]{1,0:T(8,128)S(1)} %get-tuple-element.48), channel_id=1, source_target_pairs={{0,16},{16,0},{1,17},{17,1},{2,18},{18,2},{3,19},{19,3},{4,20},{20... | collective-permute-start | bytes 208904 | tf_op jit(solution)/shard_map/ppermute | solution.py:323
  122.5 15.0 %all_to_all.44.rec = bf16[8,144,128]{2,1,0:T(8,128)(2,1)S(1)} all-to-all(bf16[8,144,128]{2,1,0:T(8,128)(2,1)S(1)} %shard_map.92), channel_id=1, replica_groups=mesh['z'=8,'core'=2,'x'=4,'y'=4] {'z'}, dimensions={0} | all-to-all | bytes 589824 | tf_op jit(solution)/shard_map/all_to_all | solution.py:319
  137.6 13.4 %all_to_all.45 = bf16[16,128,128]{2,1,0:T(8,128)(2,1)S(1)} all-to-all(bf16[16,128,128]{2,1,0:T(8,128)(2,1)S(1)} %get-tuple-element.49), channel_id=1, replica_groups=mesh['z'=8,'core'=2,'x'=4,'y'=4] {'x','y'}, dimensions={0} | all-to-all | bytes 1048576 | tf_op jit(solution)/shard_map/all_to_all | solution.py:319
  151.0 2.2 %collective-permute-start.7 = (bf16[2048,128]{1,0:T(8,128)(2,1)S(1)}, bf16[2048,128]{1,0:T(8,128)(2,1)S(1)}, u32[]{:S(2)}, u32[]{:S(2)}) collective-permute-start(bf16[2048,128]{1,0:T(8,128)(2,1)S(1)} %bitcast.16), channel_id=1, source_target_pairs={{0,16},{16,0},{1,17},{17,1},{2,18},{18,2},{3,19},{19,3},{4,20},{20... | collective-permute-start | bytes 1572872 | tf_op jit(solution)/shard_map/ppermute | solution.py:323
  153.2 2.2 %collective-permute-start.10 = (bf16[2,256,256]{2,1,0:T(8,128)(2,1)S(1)}, bf16[2,256,256]{2,1,0:T(8,128)(2,1)S(1)}, u32[]{:S(2)}, u32[]{:S(2)}) collective-permute-start(bf16[2,256,256]{2,1,0:T(8,128)(2,1)S(1)} %get-tuple-element.53), channel_id=1, source_target_pairs={{0,1},{1,2},{2,3},{3,4},{4,5},{5,6},{6,7},{7,8},{8,9},{9,10},{10,1... | collective-permute-start | bytes 786440 | tf_op jit(solution)/shard_map/ppermute | solution.py:332
  155.4 1.3 collective-permute-start.11
  156.7 2.3 %collective-permute-start.8 = (bf16[256,256]{1,0:T(8,128)(2,1)S(1)}, bf16[256,256]{1,0:T(8,128)(2,1)S(1)}, u32[]{:S(2)}, u32[]{:S(2)}) collective-permute-start(bf16[256,256]{1,0:T(8,128)(2,1)S(1)} %get-tuple-element.51), channel_id=1, source_target_pairs={{0,16},{16,32},{32,48},{48,64},{64,80},{80,96},{96,112},{112,128},... | collective-permute-start | bytes 393224 | tf_op jit(solution)/shard_map/ppermute | solution.py:330
  159.1 2.0 %collective-permute-start.9 = (bf16[256,256]{1,0:T(8,128)(2,1)S(1)}, bf16[256,256]{1,0:T(8,128)(2,1)S(1)}, u32[]{:S(2)}, u32[]{:S(2)}) collective-permute-start(bf16[256,256]{1,0:T(8,128)(2,1)S(1)} %get-tuple-element.52), channel_id=1, source_target_pairs={{16,0},{32,16},{48,32},{64,48},{80,64},{96,80},{112,96},{128,112},... | collective-permute-start | bytes 393224 | tf_op jit(solution)/shard_map/ppermute | solution.py:331
  161.1 4.5 %collective-permute-done.9.in_south = bf16[256,256]{1,0:T(8,128)(2,1)S(1)} collective-permute-done((bf16[256,256]{1,0:T(8,128)(2,1)S(1)}, bf16[256,256]{1,0:T(8,128)(2,1)S(1)}, u32[]{:S(2)}, u32[]{:S(2)}) %collective-permute-start.9) | collective-permute-done | bytes 131104 | tf_op jit(solution)/shard_map/ppermute | solution.py:331
  165.7 5.6 %shard_map.94 = (f32[2,1024,128]{2,1,0:T(8,128)S(1)}, f32[2,1024,128]{2,1,0:T(8,128)S(1)}, f32[2,1024,128]{2,1,0:T(8,128)}, f32[2,1024,128]{2,1,0:T(8,128)}, f32[8,8,128]{2,1,0:T(8,128)S(1)}) custom-call(s32[2]{0:T(128)S(1)} %bitcast.24, bf16[2048,128]{1,0:T(8,128)(2,1)S(1)} %bitcast.17, bf16[2048,128]{1,0:T(8,128)(2,1)S(1)} %collective-permute-done.7.sol_other, ...), custom_call_target="tpu_custom_call" | custom-call | tf_op jit(solution)/shard_map/pallas_call | solution.py:385
  171.3 11.1 %all_to_all.46.rec = f32[8,8,128]{2,1,0:T(8,128)S(1)} all-to-all(f32[8,8,128]{2,1,0:T(8,128)S(1)} %get-tuple-element.59), channel_id=1, replica_groups=mesh['z'=8,'core'=2,'x'=4,'y'=4] {'core','x'}, dimensions={0} | all-to-all | bytes 65536 | tf_op jit(solution)/shard_map/all_to_all | solution.py:319
  182.4 12.8 %all_to_all.47.rec = f32[32,8,128]{2,1,0:T(8,128)S(1)} all-to-all(f32[32,8,128]{2,1,0:T(8,128)S(1)} %shard_map.95), channel_id=1, replica_groups=mesh['z'=8,'core'=2,'x'=4,'y'=4] {'z','y'}, dimensions={0} | all-to-all | bytes 262144 | tf_op jit(solution)/shard_map/all_to_all | solution.py:319
  195.1 1.2 copy-done.3
  196.4 1.2 copy-done.4
  197.6 1.6 shard_map.96
  (44 shorter events, 8.8 us)
Async XLA Ops:
  4.3 1.0 copy-start.8
  5.3 0.7 copy-start.9
  6.0 28.3 %copy-start.1 = (bf16[256,4096]{1,0:T(8,128)(2,1)S(1)}, bf16[256,4096]{1,0:T(8,128)(2,1)}, u32[]{:S(2)}) copy-start(bf16[256,4096]{1,0:T(8,128)(2,1)} %coarse.1) | copy-start | bytes 6291460
  16.0 1.0 copy-start
  17.0 1.0 copy-start.2
  17.9 1.0 copy-start.5
  18.9 72.3 %copy-start.10 = (s32[2,1]{0,1:T(1,128)S(1)}, s32[2,1]{0,1:T(1,128)}, u32[]{:S(2)}) copy-start(s32[2,1]{0,1:T(1,128)} %param.10) | copy-start | bytes 28
  36.9 3.3 %collective-permute-start = (f32[136,128]{1,0:T(8,128)S(1)}, f32[136,128]{1,0:T(8,128)S(1)}, u32[]{:S(2)}, u32[]{:S(2)}) collective-permute-start(f32[136,128]{1,0:T(8,128)S(1)} %get-tuple-element.36), channel_id=1, source_target_pairs={{0,16},{16,0},{1,17},{17,1},{2,18},{18,2},{3,19},{19,3},{4,20},{20... | collective-permute-start | bytes 208904 | tf_op jit(solution)/shard_map/ppermute | solution.py:323
  73.1 18.1 %collective-permute-start.1 = (bf16[2048,128]{1,0:T(8,128)(2,1)S(1)}, bf16[2048,128]{1,0:T(8,128)(2,1)S(1)}, u32[]{:S(2)}, u32[]{:S(2)}) collective-permute-start(bf16[2048,128]{1,0:T(8,128)(2,1)S(1)} %bitcast.18), channel_id=1, source_target_pairs={{0,16},{16,0},{1,17},{17,1},{2,18},{18,2},{3,19},{19,3},{4,20},{20... | collective-permute-start | bytes 1572872 | tf_op jit(solution)/shard_map/ppermute | solution.py:323
  76.7 12.7 %collective-permute-start.4 = (bf16[2,256,384]{2,1,0:T(8,128)(2,1)S(1)}, bf16[2,256,384]{2,1,0:T(8,128)(2,1)S(1)}, u32[]{:S(2)}, u32[]{:S(2)}) collective-permute-start(bf16[2,256,384]{2,1,0:T(8,128)(2,1)S(1)} %get-tuple-element.42), channel_id=1, source_target_pairs={{0,1},{1,2},{2,3},{3,4},{4,5},{5,6},{6,7},{7,8},{8,9},{9,10},{10,1... | collective-permute-start | bytes 1179656 | tf_op jit(solution)/shard_map/ppermute | solution.py:332
  78.9 12.3 %collective-permute-start.5 = (bf16[2,256,384]{2,1,0:T(8,128)(2,1)S(1)}, bf16[2,256,384]{2,1,0:T(8,128)(2,1)S(1)}, u32[]{:S(2)}, u32[]{:S(2)}) collective-permute-start(bf16[2,256,384]{2,1,0:T(8,128)(2,1)S(1)} %get-tuple-element.43), channel_id=1, source_target_pairs={{1,0},{2,1},{3,2},{4,3},{5,4},{6,5},{7,6},{8,7},{9,8},{10,9},{11,1... | collective-permute-start | bytes 1179656 | tf_op jit(solution)/shard_map/ppermute | solution.py:333
  80.2 4.5 %collective-permute-start.2 = (bf16[256,384]{1,0:T(8,128)(2,1)S(1)}, bf16[256,384]{1,0:T(8,128)(2,1)S(1)}, u32[]{:S(2)}, u32[]{:S(2)}) collective-permute-start(bf16[256,384]{1,0:T(8,128)(2,1)S(1)} %get-tuple-element.40), channel_id=1, source_target_pairs={{0,16},{16,32},{32,48},{48,64},{64,80},{80,96},{96,112},{112,128},... | collective-permute-start | bytes 589832 | tf_op jit(solution)/shard_map/ppermute | solution.py:330
  82.1 7.3 %collective-permute-start.3 = (bf16[256,384]{1,0:T(8,128)(2,1)S(1)}, bf16[256,384]{1,0:T(8,128)(2,1)S(1)}, u32[]{:S(2)}, u32[]{:S(2)}) collective-permute-start(bf16[256,384]{1,0:T(8,128)(2,1)S(1)} %get-tuple-element.41), channel_id=1, source_target_pairs={{16,0},{32,16},{48,32},{64,48},{80,64},{96,80},{112,96},{128,112},... | collective-permute-start | bytes 589832 | tf_op jit(solution)/shard_map/ppermute | solution.py:331
  103.8 61.8 %copy-start.6 = (f32[2,1024,128]{2,1,0:T(8,128)}, f32[2,1024,128]{2,1,0:T(8,128)S(1)}, u32[]{:S(2)}) copy-start(f32[2,1024,128]{2,1,0:T(8,128)S(1)} %get-tuple-element.57.jump0) | copy-start | bytes 3145732
  103.9 61.8 %copy-start.7 = (f32[2,1024,128]{2,1,0:T(8,128)}, f32[2,1024,128]{2,1,0:T(8,128)S(1)}, u32[]{:S(2)}) copy-start(f32[2,1024,128]{2,1,0:T(8,128)S(1)} %get-tuple-element.58.prod) | copy-start | bytes 3145732
  119.1 3.3 %collective-permute-start.6 = (f32[136,128]{1,0:T(8,128)S(1)}, f32[136,128]{1,0:T(8,128)S(1)}, u32[]{:S(2)}, u32[]{:S(2)}) collective-permute-start(f32[136,128]{1,0:T(8,128)S(1)} %get-tuple-element.48), channel_id=1, source_target_pairs={{0,16},{16,0},{1,17},{17,1},{2,18},{18,2},{3,19},{19,3},{4,20},{20... | collective-permute-start | bytes 208904 | tf_op jit(solution)/shard_map/ppermute | solution.py:323
  151.0 14.6 %collective-permute-start.7 = (bf16[2048,128]{1,0:T(8,128)(2,1)S(1)}, bf16[2048,128]{1,0:T(8,128)(2,1)S(1)}, u32[]{:S(2)}, u32[]{:S(2)}) collective-permute-start(bf16[2048,128]{1,0:T(8,128)(2,1)S(1)} %bitcast.16), channel_id=1, source_target_pairs={{0,16},{16,0},{1,17},{17,1},{2,18},{18,2},{3,19},{19,3},{4,20},{20... | collective-permute-start | bytes 1572872 | tf_op jit(solution)/shard_map/ppermute | solution.py:323
  153.2 12.4 %collective-permute-start.10 = (bf16[2,256,256]{2,1,0:T(8,128)(2,1)S(1)}, bf16[2,256,256]{2,1,0:T(8,128)(2,1)S(1)}, u32[]{:S(2)}, u32[]{:S(2)}) collective-permute-start(bf16[2,256,256]{2,1,0:T(8,128)(2,1)S(1)} %get-tuple-element.53), channel_id=1, source_target_pairs={{0,1},{1,2},{2,3},{3,4},{4,5},{5,6},{6,7},{7,8},{8,9},{9,10},{10,1... | collective-permute-start | bytes 786440 | tf_op jit(solution)/shard_map/ppermute | solution.py:332
  155.4 10.2 %collective-permute-start.11 = (bf16[2,256,256]{2,1,0:T(8,128)(2,1)S(1)}, bf16[2,256,256]{2,1,0:T(8,128)(2,1)S(1)}, u32[]{:S(2)}, u32[]{:S(2)}) collective-permute-start(bf16[2,256,256]{2,1,0:T(8,128)(2,1)S(1)} %get-tuple-element.54), channel_id=1, source_target_pairs={{1,0},{2,1},{3,2},{4,3},{5,4},{6,5},{7,6},{8,7},{9,8},{10,9},{11,1... | collective-permute-start | bytes 786440 | tf_op jit(solution)/shard_map/ppermute | solution.py:333
  156.7 4.3 %collective-permute-start.8 = (bf16[256,256]{1,0:T(8,128)(2,1)S(1)}, bf16[256,256]{1,0:T(8,128)(2,1)S(1)}, u32[]{:S(2)}, u32[]{:S(2)}) collective-permute-start(bf16[256,256]{1,0:T(8,128)(2,1)S(1)} %get-tuple-element.51), channel_id=1, source_target_pairs={{0,16},{16,32},{32,48},{48,64},{64,80},{80,96},{96,112},{112,128},... | collective-permute-start | bytes 393224 | tf_op jit(solution)/shard_map/ppermute | solution.py:330
  159.1 6.6 %collective-permute-start.9 = (bf16[256,256]{1,0:T(8,128)(2,1)S(1)}, bf16[256,256]{1,0:T(8,128)(2,1)S(1)}, u32[]{:S(2)}, u32[]{:S(2)}) collective-permute-start(bf16[256,256]{1,0:T(8,128)(2,1)S(1)} %get-tuple-element.52), channel_id=1, source_target_pairs={{16,0},{32,16},{48,32},{64,48},{80,64},{96,80},{112,96},{128,112},... | collective-permute-start | bytes 393224 | tf_op jit(solution)/shard_map/ppermute | solution.py:331
  195.1 1.2 copy-start.3
  196.4 1.2 copy-start.4

commit v2 on v1

v2 whole, which is shorter than its diff:
```python
import jax
import jax.numpy as jnp
from jax import lax
from jax.experimental import pallas as pl
from jax.experimental.pallas import tpu as pltpu
from jax.sharding import Mesh
from jax.sharding import PartitionSpec as P

B = 1024
E = 256
K = 128
CORN = 32
NC = 4096
GR = 32
GC = 16
ZS = 8
CS = 2
XS = 4
YS = 4
SY = XS * YS
STRIDE = B // CORN
ROWS = 80
HALF = 128
F32 = jnp.float32
BF16 = jnp.bfloat16
VMEM_LIMIT = 40 * 1024 * 1024

VM = pl.BlockSpec(memory_space=pltpu.VMEM)
SM = pl.BlockSpec(memory_space=pltpu.SMEM)
HB = pl.BlockSpec(memory_space=pltpu.HBM)
AN = pl.BlockSpec(memory_space=pl.ANY)


def dot(a, b):
    return jnp.dot(a, b, preferred_element_type=F32)


def iota(shape, dim):
    return lax.broadcasted_iota(jnp.int32, shape, dim)


def call(kernel, outs, in_specs, out_specs, scratch=(), aliases=None):
    run = pl.pallas_call(
        kernel,
        out_shape=[
            pltpu.HBM(shape, dtype) if spec is HB else jax.ShapeDtypeStruct(shape, dtype)
            for (shape, dtype), spec in zip(outs, out_specs)
        ],
        in_specs=in_specs,
        out_specs=out_specs,
        scratch_shapes=[pltpu.VMEM(*item) if isinstance(item, tuple) else item for item in scratch],
        input_output_aliases=aliases or {},
        compiler_params=pltpu.CompilerParams(vmem_limit_bytes=VMEM_LIMIT),
    )

    def placed(*args):
        return run(
            *[pltpu.with_memory_space_constraint(a, pltpu.HBM) if spec is HB else a for a, spec in zip(args, in_specs)]
        )

    return placed


class Copies:
    def __init__(self, sems):
        self.sems = sems
        self.count = 0
        self.out = []

    def fetch(self, source, target):
        copy = pltpu.make_async_copy(source, target, self.sems.at[self.count])
        self.count += 1
        copy.start()
        return copy

    def send(self, source, target):
        self.out.append(self.fetch(source, target))

    def finish(self):
        for copy in self.out:
            copy.wait()


def sems(count):
    return pltpu.SemaphoreType.DMA((count,))


def fetch_lower(copies, source, target):
    loads = []
    for block in range(B // E):
        rows, cols = pl.ds(block * E, E), pl.ds(0, (block + 1) * E)
        loads.append(copies.fetch(source.at[rows, cols], target.at[rows, cols]))
    return loads


def lower_times(matrix, loads, right):
    parts = []
    for block in range(B // E):
        loads[block].wait()
        width = (block + 1) * E
        parts.append(dot(matrix[block * E : width, :width], right[:width]))
    return jnp.concatenate(parts, axis=0)


def times_lower(left, matrix):
    parts = []
    for block in range(B // E):
        start = block * E
        parts.append(dot(left[:, start:], matrix[start:, start : start + E]))
    return jnp.concatenate(parts, axis=1)


def split2(value):
    high = value.astype(BF16)
    low = (value - high.astype(F32)).astype(BF16)
    return high, low


def split3(value):
    high, _ = split2(value)
    rest = value - high.astype(F32)
    mid, low = split2(rest)
    return high, mid, low


def active_mask(size):
    return ((iota((B, K), 0) & (E - 1)) < size).astype(F32)


def rows_of(shape, rows):
    index = iota(shape, 0)
    result = jnp.zeros(shape, F32)
    for number, row in enumerate(rows):
        result = jnp.where(index == number, jnp.broadcast_to(row.astype(F32), shape), result)
    return result


def send_payload(copies, pay, block, corners, tail):
    block[...] = jnp.concatenate([c.astype(BF16) for c in corners] + [tail.astype(BF16)], axis=0)
    for dest in range(SY):
        copies.send(block, pay.at[dest])


def send_edges(copies, bufs, targets, interface, extra):
    chip, far, near, other = bufs
    core = lax.axis_index("core")
    odd = lax.axis_index("y") & 1

    def packed(s, edge):
        rows = pl.ds(pl.multiple_of(edge * E, E), E)
        parts = list(split2(interface[s, rows, :]))
        if extra is not None:
            parts.append(extra[s, rows, :])
        return jnp.concatenate(parts, axis=1)

    chip[...] = packed(1 - core, 1 - core)
    far[...] = packed(core, core)
    for s in range(2):
        near[s] = packed(s, 3 - odd)
        other[s] = packed(s, 2 + odd)
    for source, target in zip(bufs, targets):
        copies.send(source, target)


def first_kernel(sizes_hbm, snow_hbm, cmap_hbm, press_hbm, dir_hbm, fac_hbm,
                 res, search, half, pay, dbuf, lbuf, press, resv, searchv, halfv, block, snow, cmap, sizes, sem):
    copies = Copies(sem)
    small = [copies.fetch(a, b) for a, b in ((sizes_hbm, sizes), (snow_hbm, snow), (cmap_hbm, cmap))]
    load = copies.fetch(press_hbm, press)
    dirs, facs = [], []
    for s in range(2):
        dirs.append(copies.fetch(dir_hbm.at[s, 0], dbuf.at[s]))
    for s in range(2):
        facs.append(fetch_lower(copies, fac_hbm.at[s, 0], lbuf.at[s]))
    grid_row = lax.axis_index("z") * (2 * CS) + lax.axis_index("core") * 2
    grid_col = lax.axis_index("x") * YS + lax.axis_index("y")
    lane = iota((B, K), 1)
    for copy in small:
        copy.wait()
    masks = [active_mask(sizes[s]) for s in range(2)]
    pick_col = jnp.where((iota((B, K), 0) == lane * STRIDE) & (lane < CORN), 1.0, 0.0).astype(BF16)
    columns = []
    for s in range(2):
        place = jnp.full((1, B), grid_row + s + grid_col, jnp.int32).astype(F32)
        drift = 1.0 + 2.0 * place / (GR + GC - 2)
        depth = 0.5 + 0.25 * snow[s].astype(F32)
        columns.append([jnp.transpose(jnp.broadcast_to(row, (K, B))) for row in (depth, drift)])
    load.wait()
    for s in range(2):
        resv[s] = press[s, 0].astype(F32) * columns[s][0] * columns[s][1] * masks[s]
        copies.send(resv.at[s], res.at[s])
    for s in range(2):
        dirs[s].wait()
        searchv[s] = masks[s] * dot(dbuf[s], resv[s].astype(BF16))
        copies.send(searchv.at[s], search.at[s])
    corners = []
    for s in range(2):
        right = jnp.concatenate([searchv[s].astype(BF16), pick_col], axis=1)
        wide = lower_times(lbuf.at[s], facs[s], right)
        turned = jnp.transpose(wide).astype(BF16)
        halfv[s] = turned
        copies.send(halfv.at[s], half.at[s])
        rows = dot(turned[K : K + CORN], wide[:, :K].astype(BF16))
        corners.append(corner_mask(sizes[s]) * rows)
    cm = two_rows(cmap)
    tail = rows_of((16, K), [(cm >> 8).astype(F32), (cm & 255).astype(F32)])
    send_payload(copies, pay, block, corners, tail)
    copies.finish()


def corner_mask(size):
    return (((iota((CORN, K), 0) * STRIDE) & (E - 1)) < size).astype(F32)


def tiled_row(row):
    return jnp.concatenate([row] * (K // CORN), axis=1)


def two_rows(cmap):
    lane = iota((1, K), 1)
    return jnp.where((lane & CORN) == 0, tiled_row(cmap[0]), tiled_row(cmap[1]))


def back_first_kernel(sizes, cmap, half_hbm, fac_hbm, inter, gram, chip, far, near, other,
                      half, lbuf, interv, gramv, e0, e1, e2, e3, sem):
    copies = Copies(sem)
    facs, halves_in = [], []
    for s in range(2):
        halves_in.append(copies.fetch(half_hbm.at[s], half.at[s]))
        facs.append(fetch_lower(copies, fac_hbm.at[s, 0], lbuf.at[s]))
    lane = iota((B, K), 1)
    for s in range(2):
        mask = active_mask(sizes[s])
        square = jnp.transpose(jnp.broadcast_to(tiled_row(cmap[s]), (K, K)))
        column = jnp.concatenate([square] * (B // K), axis=0)
        digits = jnp.where(lane < 96, column >> 8, column & 255).astype(F32)
        halves_in[s].wait()
        for load in facs[s]:
            load.wait()
        back = jnp.transpose(times_lower(half.at[s], lbuf.at[s]))
        interv[s] = mask * back[:, :K]
        copies.send(interv.at[s], inter.at[s])
        ghigh, glow = split2(mask * back[:, K:])
        low_moved = pltpu.roll(glow.astype(F32), CORN, axis=1)
        gramv[s] = jnp.where(
            lane < CORN, ghigh.astype(F32), jnp.where(lane < 2 * CORN, low_moved, digits)
        ).astype(BF16)
        copies.send(gramv.at[s], gram.at[s])
    send_edges(copies, (e0, e1, e2, e3), (chip, far, near, other), interv, gramv)
    copies.finish()


def coarse_rows(rec):
    return jnp.concatenate([rec[b, 0:64, :] for b in range(SY)], axis=0)


def halves(value, stats, own, snd):
    mine = lax.axis_index("core") == 0
    tail = rows_of((8, K), stats)
    own[0:HALF] = jnp.where(mine, value[:HALF], value[HALF:])
    snd[0:HALF] = jnp.where(mine, value[HALF:], value[:HALF])
    own[HALF : HALF + 8] = tail
    snd[HALF : HALF + 8] = tail


def coarse_first_kernel(rec, coarse_hbm, _, own, snd, picked_inv, coarse, matrix, hot, sem):
    copies = Copies(sem)
    load = copies.fetch(coarse_hbm, coarse)
    lane = iota((1, K), 1)
    tails = [rec[b, 64:80, :].astype(F32) for b in range(SY)]

    def row(number):
        parts = [
            jnp.where(lane < 64, tails[2 * m][number : number + 1], tails[2 * m + 1][number : number + 1])
            for m in range(SY // 2)
        ]
        return jnp.concatenate(parts, axis=1)

    high, low = row(0), row(1)
    low_hot = jnp.where(iota((E, B), 0) == low.astype(jnp.int32), 1.0, 0.0).astype(BF16)
    high_hot = jnp.where(iota((NC // E, B), 0) == high.astype(jnp.int32), 1.0, 0.0).astype(BF16)
    for digit in range(NC // E):
        hot[digit * E : (digit + 1) * E] = low_hot * high_hot[digit : digit + 1]
    load.wait()
    matrix[...] = dot(coarse[...], hot[...]).astype(BF16)
    copies.send(matrix, picked_inv)
    halves(dot(matrix[...], coarse_rows(rec)), [], own, snd)
    copies.finish()


def coarse_next_kernel(rec, picked_inv, _, own, snd):
    value = dot(picked_inv[...], coarse_rows(rec))
    tails = sum(rec[b, 64:80, :].astype(F32) for b in range(SY))
    stats = [tails[q : q + 1] + tails[q + 1 : q + 2] + tails[q + 2 : q + 3] for q in (2, 5)]
    halves(value, stats, own, snd)


def pair_sum_kernel(own, rcv, pay, block, sem):
    copies = Copies(sem)
    total = own[...] + rcv[...]
    rows = []
    for q in range(2):
        rows += list(split3(total[HALF + q : HALF + q + 1]))
    tail = rows_of((16, K), rows).astype(BF16)
    block[...] = jnp.concatenate([total[:HALF].astype(BF16), tail], axis=0)
    for dest in range(ZS):
        copies.send(block, pay.at[dest])
    copies.finish()


def z_sum_kernel(rec, _, __, pay, stats, block, sem):
    copies = Copies(sem)
    total = sum(rec[z].astype(F32) for z in range(ZS))
    block[...] = total[:HALF].astype(BF16)
    for dest in range(SY):
        copies.send(block, pay.at[dest])
    rows = total[HALF:]
    stats[...] = rows_of(
        (8, K), [rows[q : q + 1] + rows[q + 1 : q + 2] + rows[q + 2 : q + 3] for q in (0, 3)]
    )
    copies.finish()


def tie_kernel(source, _, __, target):
    pass


def jumps(sizes, sol_own, sol_other, inter, gram, edges, grams):
    core = lax.axis_index("core")
    odd = lax.axis_index("y") & 1
    chip, far, near, other = edges
    gchip, gfar, gnear, gother = grams

    def ordered(flag, a, b):
        return jnp.where(flag == 0, b, a), jnp.where(flag == 0, a, b)

    north, south = ordered(core, chip[...], far[...])
    gnorth, gsouth = ordered(core, gchip, gfar)
    west, east = ordered(odd, near[...], other[...])
    gwest, geast = ordered(odd, gnear, gother)
    gram_edges = [gram[0, 0:CORN, :], gram[1, 0:CORN, :], gnorth[0:CORN], gsouth[0:CORN]]
    gram_edges += [g[s, 0:CORN, :] for g in (gwest, geast) for s in range(2)]
    digits = jnp.concatenate(gram_edges, axis=0).astype(F32)
    cm = digits[:, 64:65].astype(jnp.int32) * 256 + digits[:, 96:97].astype(jnp.int32)
    half = ((cm >> 7) & 1) ^ core
    place = half * 2048 + (cm >> 8) * HALF + (cm & (HALF - 1))
    hot = jnp.where(iota((8 * CORN, NC), 1) == place, 1.0, 0.0).astype(BF16)
    picks = (dot(hot[:, :2048], sol_own[...]) + dot(hot[:, 2048:], sol_other[...])).astype(BF16)
    zero = jnp.zeros((2 * CORN, K), BF16)

    def stacked(number):
        rows = picks[number * CORN : (number + 1) * CORN]
        return jnp.concatenate([rows, rows, zero], axis=0)

    full = [inter[s] + dot(gram[s], stacked(s)) for s in range(2)]

    def arrived(edge, gedge, number):
        return edge[:, :K].astype(F32) + edge[:, K : 2 * K].astype(F32) + dot(gedge, stacked(number))

    above = [arrived(north, gnorth, 2), full[0][E : 2 * E]]
    below = [full[1][0:E], arrived(south, gsouth, 3)]
    left = [arrived(west[s], gwest[s], 4 + s) for s in range(2)]
    right = [arrived(east[s], geast[s], 6 + s) for s in range(2)]
    return [
        active_mask(sizes[s]) * (full[s] - jnp.concatenate([above[s], below[s], left[s], right[s]], axis=0))
        for s in range(2)
    ]


def edge_grams(chip, far, near, other):
    return chip[:, 2 * K :], far[:, 2 * K :], near[:, :, 2 * K :], other[:, :, 2 * K :]


def second_kernel(sizes, sol_own, sol_other, inter_hbm, gram_hbm, chip_hbm, far_hbm, near_hbm, other_hbm,
                  res_hbm, dir_hbm, fac_hbm, half_hbm,
                  jump0, prod, half, pay,
                  inter, gram, chip, far, near, other, res, dbuf, lbuf, corner, jumpv, prodv, halfv, block, sem):
    copies = Copies(sem)
    edges = (chip, far, near, other)
    loads = [copies.fetch(gram_hbm, gram)]
    loads += [copies.fetch(a, b) for a, b in zip((chip_hbm, far_hbm, near_hbm, other_hbm), edges)]
    loads.append(copies.fetch(inter_hbm, inter))
    res_in = copies.fetch(res_hbm, res)
    dirs = [copies.fetch(dir_hbm.at[s, 0], dbuf.at[s]) for s in range(2)]
    facs = [fetch_lower(copies, fac_hbm.at[s, 0], lbuf.at[s]) for s in range(2)]
    corner_in = copies.fetch(half_hbm.at[:, pl.ds(K, CORN), :], corner)
    for load in loads:
        load.wait()
    jumped = jumps(sizes, sol_own, sol_other, inter, gram, edges, edge_grams(*edges))
    res_in.wait()
    cross = jnp.zeros((1, K), F32)
    energy = jnp.zeros((1, K), F32)
    for s in range(2):
        jumpv[s] = jumped[s]
        copies.send(jumpv.at[s], jump0.at[s])
        cross += jnp.sum(res[s] * jumped[s], axis=0, keepdims=True)
        energy += jnp.sum(jumped[s] * jumped[s], axis=0, keepdims=True)
    for s in range(2):
        dirs[s].wait()
        wide = dot(dbuf[s], jnp.concatenate(split2(jumpv[s]), axis=1))
        prodv[s] = active_mask(sizes[s]) * (wide[:, :K] + wide[:, K:])
        copies.send(prodv.at[s], prod.at[s])
    corner_in.wait()
    corners = []
    for s in range(2):
        wide = lower_times(lbuf.at[s], facs[s], jnp.concatenate(split2(prodv[s]), axis=1))
        inner = wide[:, :K] + wide[:, K:]
        halfv[s] = jnp.concatenate(split2(jnp.transpose(inner)), axis=0)
        copies.send(halfv.at[s], half.at[s])
        rows = dot(corner[s], jnp.concatenate(split2(inner), axis=1))
        corners.append(corner_mask(sizes[s]) * (rows[:, :K] + rows[:, K:]))
    rows = [jnp.zeros((1, K), F32)] * 2 + list(split3(cross)) + list(split3(energy))
    send_payload(copies, pay, block, corners, rows_of((16, K), rows))
    copies.finish()


def back_next_kernel(sizes, half_hbm, fac_hbm, inter, chip, far, near, other,
                     half, lbuf, interv, e0, e1, e2, e3, sem):
    copies = Copies(sem)
    facs, halves_in = [], []
    for s in range(2):
        halves_in.append(copies.fetch(half_hbm.at[s], half.at[s]))
        facs.append(fetch_lower(copies, fac_hbm.at[s, 0], lbuf.at[s]))
    for s in range(2):
        halves_in[s].wait()
        for load in facs[s]:
            load.wait()
        wide = times_lower(half.at[s], lbuf.at[s])
        interv[s] = active_mask(sizes[s]) * jnp.transpose(wide[:K] + wide[K:])
        copies.send(interv.at[s], inter.at[s])
    send_edges(copies, (e0, e1, e2, e3), (chip, far, near, other), interv, None)
    copies.finish()


def third_kernel(sizes, sol_own, sol_other, stats, inter_hbm, gram_hbm, chip_hbm, far_hbm, near_hbm, other_hbm,
                 old_chip, old_far, old_near, old_other, res_hbm, jump_hbm,
                 res1, jump1, pay,
                 inter, gram, chip, far, near, other, gchip, gfar, gnear, gother, res, jump0, sem):
    copies = Copies(sem)
    edges = (chip, far, near, other)
    grams = (gchip, gfar, gnear, gother)
    width = pl.ds(2 * K, K)
    loads = [copies.fetch(gram_hbm, gram)]
    loads += [copies.fetch(a.at[:, width], b) for a, b in zip((old_chip, old_far), grams[:2])]
    loads += [copies.fetch(a.at[:, :, width], b) for a, b in zip((old_near, old_other), grams[2:])]
    loads += [copies.fetch(a, b) for a, b in zip((chip_hbm, far_hbm, near_hbm, other_hbm), edges)]
    loads.append(copies.fetch(inter_hbm, inter))
    late = [copies.fetch(res_hbm, res), copies.fetch(jump_hbm, jump0)]
    for load in loads:
        load.wait()
    again = jumps(sizes, sol_own, sol_other, inter, gram, edges, tuple(g[...] for g in grams))
    for load in late:
        load.wait()
    step = stats[0:1] / (stats[1:2] + 1e-06)
    cross = jnp.zeros((1, K), F32)
    energy = jnp.zeros((1, K), F32)
    for s in range(2):
        before = res[s] - step * jump0[s]
        jumped = jump0[s] - step * again[s]
        res1[s] = before
        jump1[s] = jumped
        cross += jnp.sum(before * jumped, axis=0, keepdims=True)
        energy += jnp.sum(jumped * jumped, axis=0, keepdims=True)
    block = rows_of((8, K), [cross, energy])
    for dest in range(CS * XS):
        pay[dest] = block


def partial_kernel(rec, pay):
    total = sum(rec[b] for b in range(CS * XS))
    for dest in range(ZS * YS):
        pay[dest] = total


def last_kernel(rec, stats, res1, jump1, search, prod, mult, res, multv, resv, sem):
    copies = Copies(sem)
    total = sum(rec[b] for b in range(ZS * YS))
    first = stats[0:1] / (stats[1:2] + 1e-06)
    step = total[0:1] / (total[1:2] + 1e-06)
    for s in range(2):
        multv[s] = first * search[s] + step * (search[s] - first * prod[s])
        copies.send(multv.at[s], mult.at[s])
        resv[s] = res1[s] - step * jump1[s]
        copies.send(resv.at[s], res.at[s])
    copies.finish()


def all_to_all(value, axes):
    return lax.all_to_all(value, axes, split_axis=0, concat_axis=0)


def swap(value):
    return lax.ppermute(value, "core", [(0, 1), (1, 0)])


def exchange(chip, far, near, other):
    even = [(i, i ^ 1) for i in range(16)]
    odd = [(i, i + 1) for i in range(1, 15, 2)] + [(i + 1, i) for i in range(1, 15, 2)]
    rows, cols = ("z", "core"), ("x", "y")
    return (
        lax.ppermute(chip, rows, even),
        lax.ppermute(far, rows, odd),
        lax.ppermute(near, cols, even),
        lax.ppermute(other, cols, odd),
    )


def coarse_solution(own, snd, arrived):
    pay3 = ((ZS, HALF + 16, K), BF16)
    rcv = swap(snd)
    (pay,) = call(pair_sum_kernel, [pay3], [VM] * 2, [HB], [(pay3[0][1:], BF16), sems(ZS)])(own, rcv)
    rec = all_to_all(pay, "z")
    pay, stats = call(
        z_sum_kernel,
        [((SY, HALF, K), BF16), ((8, K), F32)],
        [VM, HB, HB],
        [HB, VM],
        [((HALF, K), BF16), sems(SY)],
    )(rec, *arrived[2:])
    sol = all_to_all(pay, ("x", "y"))
    (sol,) = call(tie_kernel, [((SY, HALF, K), BF16)], [AN] + [HB] * 2, [AN], aliases={0: 0})(sol, *arrived[:2])
    sol = sol.reshape(SY * HALF, K)
    return sol, swap(sol), stats


def local(factor, pre, coarse_inv, sizes, cmap, snow_level, pressure):
    sizes = sizes.reshape(2)
    whole = ((2, B, K), F32)
    gramed = ((2, B, K), BF16)
    halved = ((2, 2 * K, B), BF16)
    square = ((2, B, B), BF16)
    payload = ((SY, ROWS, K), BF16)
    block = (payload[0][1:], BF16)
    sent = [((HALF + 8, K), F32)] * 2

    def edges_of(width):
        return [((E, width), BF16)] * 2 + [((2, E, width), BF16)] * 2

    res, search, half, pay = call(
        first_kernel,
        [whole, whole, halved, payload],
        [HB] * 6,
        [HB] * 4,
        [square, square, ((2, 1, B, K), BF16), whole, whole, halved, block]
        + [((2, 1, B), jnp.int32), ((2, 1, CORN), jnp.int32), pltpu.SMEM((2,), jnp.int32), sems(20 + SY)],
    )(sizes, snow_level, cmap, pressure, pre, factor)
    rec = all_to_all(pay, ("x", "y"))
    wide = edges_of(3 * K)
    inter, gram, *edges = call(
        back_first_kernel,
        [whole, gramed] + wide,
        [SM, VM, HB, HB],
        [HB] * 6,
        [halved, square, whole, gramed] + wide + [sems(18)],
    )(sizes, cmap, half, factor)
    arrived = exchange(*edges)
    own, snd, picked_inv = call(
        coarse_first_kernel,
        sent + [((E, B), BF16)],
        [VM, HB, HB],
        [VM, VM, HB],
        [((E, NC), BF16), ((E, B), BF16), ((NC, B), BF16), sems(2)],
    )(rec, coarse_inv, gram)
    sol_own, sol_other, _ = coarse_solution(own, snd, arrived)
    jump0, prod, half1, pay = call(
        second_kernel,
        [whole, whole, halved, payload],
        [SM, VM, VM] + [HB] * 10,
        [HB] * 4,
        [whole, gramed] + wide + [whole, square, square, ((2, CORN, B), BF16), whole, whole, halved, block, sems(24 + SY)],
    )(sizes, sol_own, sol_other, inter, gram, *arrived, res, pre, factor, half)
    rec = all_to_all(pay, ("x", "y"))
    slim = edges_of(2 * K)
    inter1, *edges = call(
        back_next_kernel,
        [whole] + slim,
        [SM] + [HB] * 2,
        [HB] * 5,
        [halved, square, whole] + slim + [sems(16)],
    )(sizes, half1, factor)
    arrived1 = exchange(*edges)
    own, snd = call(coarse_next_kernel, sent, [VM] * 2 + [HB], [VM] * 2)(rec, picked_inv, inter1)
    sol_own, sol_other, stats = coarse_solution(own, snd, arrived1)
    res1, jump1, pay = call(
        third_kernel,
        [whole] * 2 + [((CS * XS, 8, K), F32)],
        [SM] + [VM] * 3 + [HB] * 12,
        [VM] * 3,
        [whole, gramed] + slim + edges_of(K) + [whole, whole, sems(12)],
    )(sizes, sol_own, sol_other, stats, inter1, gram, *arrived1, *arrived, res, jump0)
    rec = all_to_all(pay, ("core", "x"))
    (pay,) = call(partial_kernel, [((ZS * YS, 8, K), F32)], [VM], [VM])(rec)
    rec = all_to_all(pay, ("z", "y"))
    mult, res = call(last_kernel, [whole] * 2, [VM] * 6, [HB] * 2, [whole, whole, sems(4)])(
        rec, stats, res1, jump1, search, prod
    )
    return mult.reshape(2, 1, B, K), res.reshape(2, 1, B, K)


def solution(mesh):
    fine = Mesh(mesh.devices.reshape(ZS, CS, XS, YS), ("z", "core", "x", "y"))
    rows, cols = ("z", "core"), ("x", "y")
    return jax.shard_map(
        local,
        mesh=fine,
        in_specs=(
            P(rows, cols, None, None),
            P(rows, cols, None, None),
            P(cols, None),
            P(rows, cols),
            P(rows, cols, None),
            P(rows, cols, None),
            P(rows, cols, None, None),
        ),
        out_specs=(P(rows, cols, None, None), P(rows, cols, None, None)),
        check_vma=False,
    )
```

time: 200 us -> 174 us (0.87)
  blocking collectives: 115 us -> 26 us
  starting transfers between devices: 26.4 us -> 59.8 us
  waiting for transfers between devices: 12.9 us -> 42.3 us
  Pallas kernels: 33.4 us -> 43.5 us
  local copies, waits for them, and re-layouts: 9.34 us -> 0.73 us
    all_to_all x8 -> x2, blocking collectives: 115 us -> 26 us  [all_to_all(): return lax.all_to_all(value, axes, split_axis=0, concat_axis=0)]
    all_to_all x0 -> x6, starting transfers between devices: none -> 37.7 us  [all_to_all(): return lax.all_to_all(value, axes, split_axis=0, concat_axis=0)]
    all_to_all x0 -> x6, waiting for transfers between devices: none -> 14.1 us  [all_to_all(): return lax.all_to_all(value, axes, split_axis=0, concat_axis=0)]
    ppermute x8, waiting for transfers between devices: 11 us -> 23.3 us  [the longest x2 16.1 us: exchange(): lax.ppermute(near, cols, even)]
    pallas_call x11 -> x15, Pallas kernels: 33.4 us -> 43.5 us  [placed(): run(*[pltpu.with_memory_space_constraint(a, pltpu.HBM) if spec is HB else...]
    unnamed x24 -> x34, local copies, waits for them, and re-layouts: 8.32 us -> 0.73 us
    ppermute x8, starting transfers between devices: 15.8 us -> 12.1 us  [the longest x2 6.7 us: exchange(): lax.ppermute(far, rows, odd)]
    ppermute x4, waiting for transfers between devices: 1.82 us -> 4.89 us  [swap(): return lax.ppermute(value, 'core', [(0, 1), (1, 0)])]
  transfers between devices with their start and end apart: 12 -> 18, of which waited for: 5 -> 13; matrix products, arithmetic and copies ran while one was open for 0% -> 0% of each run, Pallas kernels for 0% -> 6%
where the time goes in v2:
time: 174 us; the launch traced here: 173 us
  starting transfers between devices  59.8 us (34%)
  Pallas kernels  43.5 us (25%)
  waiting for transfers between devices  42.3 us (24%)
  blocking collectives  26 us (15%)
    pallas_call x15, Pallas kernels, placed(): run(*[pltpu.with_memory_space_constraint(a, pltpu.HBM) if spec is HB else...  43.5 us
    all_to_all x6, starting transfers between devices, all_to_all(): return lax.all_to_all(value, axes, split_axis=0, concat_axis=0)  37.7 us
    all_to_all x2, blocking collectives, all_to_all(): return lax.all_to_all(value, axes, split_axis=0, concat_axis=0)  26 us
    ppermute x2, waiting for transfers between devices, exchange(): lax.ppermute(near, cols, even)  16.1 us
    all_to_all x6, waiting for transfers between devices, all_to_all(): return lax.all_to_all(value, axes, split_axis=0, concat_axis=0)  14.1 us
    ppermute x4, starting transfers between devices, swap(): return lax.ppermute(value, 'core', [(0, 1), (1, 0)])  10 us
    ppermute x2, waiting for transfers between devices, exchange(): lax.ppermute(far, rows, odd)  7.22 us
    ppermute x2, starting transfers between devices, exchange(): lax.ppermute(far, rows, odd)  6.7 us
  transfers between devices with their start and end apart: 18, of which 13 were waited for; matrix products, arithmetic and copies ran while one was open for 0% of the time, Pallas kernels for 6%

profile of v2, /device:TPU:1, one launch (start us, length us, event | category | flops | bytes accessed | tf_op | source)
XLA Modules:
  0.0 173.4 jit_solution(9278615445543926046)
XLA Ops:
  0.7 8.3 %shard_map.86 = (f32[2,1024,128]{2,1,0:T(8,128)}, f32[2,1024,128]{2,1,0:T(8,128)}, bf16[2,256,1024]{2,1,0:T(8,128)(2,1)}, bf16[16,80,128]{2,1,0:T(8,128)(2,1)}) custom-call(s32[2]{0:T(128)} %bitcast.13, s32[2,1,1024]{2,1,0:T(1,128)} %snow_hbm.1, s32[2,1,32]{2,1,0:T(1,128)} %cmap.1, bf16[2,1,1024,128]{3,2,1,0:T(8,128)(2,1)} %press_hbm.1, ...), custom_call_target="tpu_custom_call" | custom-call | tf_op jit(solution)/shard_map/pallas_call | solution.py:57
  9.0 7.6 %all-to-all-start = ((bf16[16,80,128]{2,1,0:T(8,128)(2,1)}), bf16[16,80,128]{2,1,0:T(8,128)(2,1)S(1)}, u32[]{:S(2)}, u32[]{:S(2)}) async-start(bf16[16,80,128]{2,1,0:T(8,128)(2,1)} %get-tuple-element.34), calls=%async_computation | async-start | bytes 655360 | tf_op jit(solution)/shard_map/all_to_all | solution.py:489
  16.6 5.2 %shard_map.87 = (f32[2,1024,128]{2,1,0:T(8,128)}, bf16[2,1024,128]{2,1,0:T(8,128)(2,1)}, bf16[256,384]{1,0:T(8,128)(2,1)}, bf16[256,384]{1,0:T(8,128)(2,1)}, bf1...) custom-call(s32[2]{0:T(128)S(1)} %bitcast.14, s32[2,1,32]{2,1,0:T(1,128)S(1)} %copy-done.4, ...), custom_call_target="tpu_custom_call" | custom-call | tf_op jit(solution)/shard_map/pallas_call | solution.py:57
  21.9 2.5 %all-to-all-done.rec = bf16[16,80,128]{2,1,0:T(8,128)(2,1)S(1)} async-done(((bf16[16,80,128]{2,1,0:T(8,128)(2,1)}), bf16[16,80,128]{2,1,0:T(8,128)(2,1)S(1)}, u32[]{:S(2)}, u32[]{:S(2)}) %all-to-all-start) | async-done | bytes 327712 | tf_op jit(solution)/shard_map/all_to_all | solution.py:489
  24.4 4.7 %shard_map.88 = (f32[136,128]{1,0:T(8,128)S(1)}, f32[136,128]{1,0:T(8,128)S(1)}, bf16[256,1024]{1,0:T(8,128)(2,1)}) custom-call(bf16[16,80,128]{2,1,0:T(8,128)(2,1)S(1)} %all-to-all-done.rec, bf16[256,4096]{1,0:T(8,128)(2,1)} %coarse_hbm.1, bf16[2,1024,128]{2,1,0:T(8,128)(2,1)} %get-tuple-element.36._.gram_hbm), custom_call_target="tpu_custom_call" | custom-call | tf_op jit(solution)/shard_map/pallas_call | solution.py:57
  29.1 2.4 %collective-permute-start = (f32[136,128]{1,0:T(8,128)S(1)}, f32[136,128]{1,0:T(8,128)S(1)}, u32[]{:S(2)}, u32[]{:S(2)}) collective-permute-start(f32[136,128]{1,0:T(8,128)S(1)} %get-tuple-element.38), channel_id=1, source_target_pairs={{0,16},{16,0},{1,17},{17,1},{2,18},{18,2},{3,19},{19,3},{4,20},{20... | collective-permute-start | bytes 208904 | tf_op jit(solution)/shard_map/ppermute | solution.py:493
  33.2 8.2 %all-to-all-start.1 = ((bf16[8,144,128]{2,1,0:T(8,128)(2,1)}), bf16[8,144,128]{2,1,0:T(8,128)(2,1)S(1)}, u32[]{:S(2)}, u32[]{:S(2)}) async-start(bf16[8,144,128]{2,1,0:T(8,128)(2,1)} %shard_map.89), calls=%async_computation.1 | async-start | bytes 589824 | tf_op jit(solution)/shard_map/all_to_all | solution.py:489
  42.3 9.4 %collective-permute-done.1._.near_hbm.old_near = bf16[2,256,384]{2,1,0:T(8,128)(2,1)S(1)} collective-permute-done((bf16[2,256,384]{2,1,0:T(8,128)(2,1)}, bf16[2,256,384]{2,1,0:T(8,128)(2,1)S(1)}, u32[]{:S(2)}, u32[]{:S(2)}) %collective-permute-start.1) | collective-permute-done | bytes 393248 | tf_op jit(solution)/shard_map/ppermute | solution.py:503
  51.7 2.2 %all-to-all-done.1.rec = bf16[8,144,128]{2,1,0:T(8,128)(2,1)S(1)} async-done(((bf16[8,144,128]{2,1,0:T(8,128)(2,1)}), bf16[8,144,128]{2,1,0:T(8,128)(2,1)S(1)}, u32[]{:S(2)}, u32[]{:S(2)}) %all-to-all-start.1) | async-done | bytes 294944 | tf_op jit(solution)/shard_map/all_to_all | solution.py:489
  53.9 1.6 shard_map.90
  55.5 5.9 %all-to-all-start.2 = ((bf16[16,128,128]{2,1,0:T(8,128)(2,1)}), bf16[16,128,128]{2,1,0:T(8,128)(2,1)S(1)}, u32[]{:S(2)}, u32[]{:S(2)}) async-start(bf16[16,128,128]{2,1,0:T(8,128)(2,1)} %get-tuple-element.41), calls=%async_computation.2 | async-start | bytes 1048576 | tf_op jit(solution)/shard_map/all_to_all | solution.py:489
  61.4 2.2 %collective-permute-start.3 = (bf16[256,384]{1,0:T(8,128)(2,1)S(1)}, bf16[256,384]{1,0:T(8,128)(2,1)S(1)}, u32[]{:S(2)}, u32[]{:S(2)}) collective-permute-start(bf16[256,384]{1,0:T(8,128)(2,1)S(1)} %copy-done.14), channel_id=1, source_target_pairs={{0,16},{16,0},{32,48},{48,32},{64,80},{80,64},{96,112},{112,96},{1... | collective-permute-start | bytes 589832 | tf_op jit(solution)/shard_map/ppermute | solution.py:501
  63.6 3.3 %collective-permute-start.4 = (bf16[256,384]{1,0:T(8,128)(2,1)S(1)}, bf16[256,384]{1,0:T(8,128)(2,1)S(1)}, u32[]{:S(2)}, u32[]{:S(2)}) collective-permute-start(bf16[256,384]{1,0:T(8,128)(2,1)S(1)} %copy-done.13), channel_id=1, source_target_pairs={{16,32},{48,64},{80,96},{112,128},{144,160},{176,192},{208,224},{3... | collective-permute-start | bytes 589832 | tf_op jit(solution)/shard_map/ppermute | solution.py:502
  66.9 4.0 %collective-permute-done.4.__.far_hbm.old_far = bf16[256,384]{1,0:T(8,128)(2,1)S(1)} collective-permute-done((bf16[256,384]{1,0:T(8,128)(2,1)S(1)}, bf16[256,384]{1,0:T(8,128)(2,1)S(1)}, u32[]{:S(2)}, u32[]{:S(2)}) %collective-permute-start.4) | collective-permute-done | bytes 196640 | tf_op jit(solution)/shard_map/ppermute | solution.py:502
  71.5 2.3 %collective-permute-start.5 = (bf16[2048,128]{1,0:T(8,128)(2,1)S(1)}, bf16[2048,128]{1,0:T(8,128)(2,1)S(1)}, u32[]{:S(2)}, u32[]{:S(2)}) collective-permute-start(bf16[2048,128]{1,0:T(8,128)(2,1)S(1)} %bitcast.11), channel_id=1, source_target_pairs={{0,16},{16,0},{1,17},{17,1},{2,18},{18,2},{3,19},{19,3},{4,20},{20... | collective-permute-start | bytes 1572872 | tf_op jit(solution)/shard_map/ppermute | solution.py:493
  73.8 1.5 collective-permute-done.5.sol_other
  75.4 10.6 %shard_map.92 = (f32[2,1024,128]{2,1,0:T(8,128)}, f32[2,1024,128]{2,1,0:T(8,128)}, bf16[2,256,1024]{2,1,0:T(8,128)(2,1)}, bf16[16,80,128]{2,1,0:T(8,128)(2,1)}) custom-call(s32[2]{0:T(128)S(1)} %bitcast.15, bf16[2048,128]{1,0:T(8,128)(2,1)S(1)} %bitcast.12, bf16[2048,128]{1,0:T(8,128)(2,1)S(1)} %collective-permute-done.5.sol_other, ...), custom_call_target="tpu_custom_call" | custom-call | tf_op jit(solution)/shard_map/pallas_call | solution.py:57
  86.0 4.9 %all-to-all-start.3 = ((bf16[16,80,128]{2,1,0:T(8,128)(2,1)}), bf16[16,80,128]{2,1,0:T(8,128)(2,1)S(1)}, u32[]{:S(2)}, u32[]{:S(2)}) async-start(bf16[16,80,128]{2,1,0:T(8,128)(2,1)} %get-tuple-element.46), calls=%async_computation.3 | async-start | bytes 655360 | tf_op jit(solution)/shard_map/all_to_all | solution.py:489
  90.9 4.5 %shard_map.93 = (f32[2,1024,128]{2,1,0:T(8,128)}, bf16[256,256]{1,0:T(8,128)(2,1)}, bf16[256,256]{1,0:T(8,128)(2,1)}, bf16[2,256,256]{2,1,0:T(8,128)(2,1)}, bf16[2,256,256]{2,1,0:T(8,128)(2,1)}) custom-call(s32[2]{0:T(128)S(1)} %bitcast.16, bf16[2,256,1024]{2,1,0:T(8,128)(2,1)} %get-tuple-element.48.half_hbm, bf16[2,1,1024,1024]{3,2,1,0:T(8,128)(2,1)} %fac_hbm.7), custom_call_target="tpu_custom_call" | custom-call | tf_op jit(solution)/shard_map/pallas_call | solution.py:57
  95.4 3.7 %all-to-all-done.3.rec = bf16[16,80,128]{2,1,0:T(8,128)(2,1)S(1)} async-done(((bf16[16,80,128]{2,1,0:T(8,128)(2,1)}), bf16[16,80,128]{2,1,0:T(8,128)(2,1)S(1)}, u32[]{:S(2)}, u32[]{:S(2)}) %all-to-all-start.3) | async-done | bytes 327712 | tf_op jit(solution)/shard_map/all_to_all | solution.py:489
  99.4 2.0 %collective-permute-start.6 = (f32[136,128]{1,0:T(8,128)S(1)}, f32[136,128]{1,0:T(8,128)S(1)}, u32[]{:S(2)}, u32[]{:S(2)}) collective-permute-start(f32[136,128]{1,0:T(8,128)S(1)} %get-tuple-element.51), channel_id=1, source_target_pairs={{0,16},{16,0},{1,17},{17,1},{2,18},{18,2},{3,19},{19,3},{4,20},{20... | collective-permute-start | bytes 208904 | tf_op jit(solution)/shard_map/ppermute | solution.py:493
  103.1 7.5 %all-to-all-start.4 = ((bf16[8,144,128]{2,1,0:T(8,128)(2,1)}), bf16[8,144,128]{2,1,0:T(8,128)(2,1)S(1)}, u32[]{:S(2)}, u32[]{:S(2)}) async-start(bf16[8,144,128]{2,1,0:T(8,128)(2,1)} %shard_map.95), calls=%async_computation.4 | async-start | bytes 589824 | tf_op jit(solution)/shard_map/all_to_all | solution.py:489
  111.4 6.7 %collective-permute-done.7._.near_hbm = bf16[2,256,256]{2,1,0:T(8,128)(2,1)S(1)} collective-permute-done((bf16[2,256,256]{2,1,0:T(8,128)(2,1)}, bf16[2,256,256]{2,1,0:T(8,128)(2,1)S(1)}, u32[]{:S(2)}, u32[]{:S(2)}) %collective-permute-start.7) | collective-permute-done | bytes 262176 | tf_op jit(solution)/shard_map/ppermute | solution.py:503
  118.1 5.0 %all-to-all-done.4.rec = bf16[8,144,128]{2,1,0:T(8,128)(2,1)S(1)} async-done(((bf16[8,144,128]{2,1,0:T(8,128)(2,1)}), bf16[8,144,128]{2,1,0:T(8,128)(2,1)S(1)}, u32[]{:S(2)}, u32[]{:S(2)}) %all-to-all-start.4) | async-done | bytes 294944 | tf_op jit(solution)/shard_map/all_to_all | solution.py:489
  124.1 3.6 %all-to-all-start.5 = ((bf16[16,128,128]{2,1,0:T(8,128)(2,1)}), bf16[16,128,128]{2,1,0:T(8,128)(2,1)S(1)}, u32[]{:S(2)}, u32[]{:S(2)}) async-start(bf16[16,128,128]{2,1,0:T(8,128)(2,1)} %get-tuple-element.54), calls=%async_computation.5 | async-start | bytes 1048576 | tf_op jit(solution)/shard_map/all_to_all | solution.py:489
  127.7 1.7 collective-permute-start.9
  129.4 3.4 %collective-permute-start.10 = (bf16[256,256]{1,0:T(8,128)(2,1)S(1)}, bf16[256,256]{1,0:T(8,128)(2,1)S(1)}, u32[]{:S(2)}, u32[]{:S(2)}) collective-permute-start(bf16[256,256]{1,0:T(8,128)(2,1)S(1)} %copy-done.15), channel_id=1, source_target_pairs={{16,32},{48,64},{80,96},{112,128},{144,160},{176,192},{208,224},{3... | collective-permute-start | bytes 393224 | tf_op jit(solution)/shard_map/ppermute | solution.py:502
  132.8 3.2 %collective-permute-done.10.__.far_hbm = bf16[256,256]{1,0:T(8,128)(2,1)S(1)} collective-permute-done((bf16[256,256]{1,0:T(8,128)(2,1)S(1)}, bf16[256,256]{1,0:T(8,128)(2,1)S(1)}, u32[]{:S(2)}, u32[]{:S(2)}) %collective-permute-start.10) | collective-permute-done | bytes 131104 | tf_op jit(solution)/shard_map/ppermute | solution.py:502
  136.7 3.4 %collective-permute-start.11 = (bf16[2048,128]{1,0:T(8,128)(2,1)S(1)}, bf16[2048,128]{1,0:T(8,128)(2,1)S(1)}, u32[]{:S(2)}, u32[]{:S(2)}) collective-permute-start(bf16[2048,128]{1,0:T(8,128)(2,1)S(1)} %bitcast.9), channel_id=1, source_target_pairs={{0,16},{16,0},{1,17},{17,1},{2,18},{18,2},{3,19},{19,3},{4,20},{20... | collective-permute-start | bytes 1572872 | tf_op jit(solution)/shard_map/ppermute | solution.py:493
  141.6 4.1 %shard_map.98 = (f32[2,1024,128]{2,1,0:T(8,128)S(1)}, f32[2,1024,128]{2,1,0:T(8,128)S(1)}, f32[8,8,128]{2,1,0:T(8,128)S(1)}) custom-call(s32[2]{0:T(128)S(1)} %bitcast.17, bf16[2048,128]{1,0:T(8,128)(2,1)S(1)} %bitcast.10, bf16[2048,128]{1,0:T(8,128)(2,1)S(1)} %collective-permute-done.11.sol_other, f32[8,128]{1,0:T(8,128)S(1)} %get-tuple-element.57.stats, ...), custom_call_target="tpu_custom_call" | custom-call | tf_op jit(solution)/shard_map/pallas_call | solution.py:57
  145.7 7.7 %all_to_all.40.rec = f32[8,8,128]{2,1,0:T(8,128)S(1)} all-to-all(f32[8,8,128]{2,1,0:T(8,128)S(1)} %get-tuple-element.59), channel_id=1, replica_groups=mesh['z'=8,'core'=2,'x'=4,'y'=4] {'core','x'}, dimensions={0} | all-to-all | bytes 65536 | tf_op jit(solution)/shard_map/all_to_all | solution.py:489
  153.4 18.3 %all_to_all.41.rec = f32[32,8,128]{2,1,0:T(8,128)S(1)} all-to-all(f32[32,8,128]{2,1,0:T(8,128)S(1)} %shard_map.99), channel_id=1, replica_groups=mesh['z'=8,'core'=2,'x'=4,'y'=4] {'z','y'}, dimensions={0} | all-to-all | bytes 262144 | tf_op jit(solution)/shard_map/all_to_all | solution.py:489
  (55 shorter events, 10.7 us)
Async XLA Ops:
  0.6 15.9 %copy-start.3 = (s32[2,1]{0,1:T(1,128)S(1)}, s32[2,1]{0,1:T(1,128)}, u32[]{:S(2)}) copy-start(s32[2,1]{0,1:T(1,128)} %param.10) | copy-start | bytes 28
  0.6 15.9 %copy-start.4 = (s32[2,1,32]{2,1,0:T(1,128)S(1)}, s32[2,1,32]{2,1,0:T(1,128)}, u32[]{:S(2)}) copy-start(s32[2,1,32]{2,1,0:T(1,128)} %cmap.1) | copy-start | bytes 772
  9.0 15.4 %all-to-all-start = ((bf16[16,80,128]{2,1,0:T(8,128)(2,1)}), bf16[16,80,128]{2,1,0:T(8,128)(2,1)S(1)}, u32[]{:S(2)}, u32[]{:S(2)}) async-start(bf16[16,80,128]{2,1,0:T(8,128)(2,1)} %get-tuple-element.34), calls=%async_computation | async-start | bytes 655360 | tf_op jit(solution)/shard_map/all_to_all | solution.py:489
  21.8 39.5 %copy-start.14 = (bf16[256,384]{1,0:T(8,128)(2,1)S(1)}, bf16[256,384]{1,0:T(8,128)(2,1)}, u32[]{:S(2)}) copy-start(bf16[256,384]{1,0:T(8,128)(2,1)} %get-tuple-element.42) | copy-start | bytes 589828
  21.9 41.7 %copy-start.13 = (bf16[256,384]{1,0:T(8,128)(2,1)S(1)}, bf16[256,384]{1,0:T(8,128)(2,1)}, u32[]{:S(2)}) copy-start(bf16[256,384]{1,0:T(8,128)(2,1)} %get-tuple-element.43) | copy-start | bytes 589828
  29.1 3.3 %collective-permute-start = (f32[136,128]{1,0:T(8,128)S(1)}, f32[136,128]{1,0:T(8,128)S(1)}, u32[]{:S(2)}, u32[]{:S(2)}) collective-permute-start(f32[136,128]{1,0:T(8,128)S(1)} %get-tuple-element.38), channel_id=1, source_target_pairs={{0,16},{16,0},{1,17},{17,1},{2,18},{18,2},{3,19},{19,3},{4,20},{20... | collective-permute-start | bytes 208904 | tf_op jit(solution)/shard_map/ppermute | solution.py:493
  33.2 20.6 %all-to-all-start.1 = ((bf16[8,144,128]{2,1,0:T(8,128)(2,1)}), bf16[8,144,128]{2,1,0:T(8,128)(2,1)S(1)}, u32[]{:S(2)}, u32[]{:S(2)}) async-start(bf16[8,144,128]{2,1,0:T(8,128)(2,1)} %shard_map.89), calls=%async_computation.1 | async-start | bytes 589824 | tf_op jit(solution)/shard_map/all_to_all | solution.py:489
  41.4 10.2 %collective-permute-start.1 = (bf16[2,256,384]{2,1,0:T(8,128)(2,1)}, bf16[2,256,384]{2,1,0:T(8,128)(2,1)S(1)}, u32[]{:S(2)}, u32[]{:S(2)}) collective-permute-start(bf16[2,256,384]{2,1,0:T(8,128)(2,1)} %get-tuple-element.39), channel_id=1, source_target_pairs={{0,1},{1,0},{2,3},{3,2},{4,5},{5,4},{6,7},{7,6},{8,9},{9,8},{10,11... | collective-permute-start | bytes 1179656 | tf_op jit(solution)/shard_map/ppermute | solution.py:503
  41.6 10.1 %collective-permute-start.2 = (bf16[2,256,384]{2,1,0:T(8,128)(2,1)}, bf16[2,256,384]{2,1,0:T(8,128)(2,1)S(1)}, u32[]{:S(2)}, u32[]{:S(2)}) collective-permute-start(bf16[2,256,384]{2,1,0:T(8,128)(2,1)} %get-tuple-element.40), channel_id=1, source_target_pairs={{1,2},{3,4},{5,6},{7,8},{9,10},{11,12},{13,14},{2,1},{4,3},{6,5},{... | collective-permute-start | bytes 1179656 | tf_op jit(solution)/shard_map/ppermute | solution.py:504
  51.7 2.2 %copy-start.5 = (bf16[2,256,384]{2,1,0:T(8,128)(2,1)}, bf16[2,256,384]{2,1,0:T(8,128)(2,1)S(1)}, u32[]{:S(2)}) copy-start(bf16[2,256,384]{2,1,0:T(8,128)(2,1)S(1)} %collective-permute-done.1._.near_hbm.old_near) | copy-start | bytes 1179652
  55.5 15.4 %all-to-all-start.2 = ((bf16[16,128,128]{2,1,0:T(8,128)(2,1)}), bf16[16,128,128]{2,1,0:T(8,128)(2,1)S(1)}, u32[]{:S(2)}, u32[]{:S(2)}) async-start(bf16[16,128,128]{2,1,0:T(8,128)(2,1)} %get-tuple-element.41), calls=%async_computation.2 | async-start | bytes 1048576 | tf_op jit(solution)/shard_map/all_to_all | solution.py:489
  61.4 5.5 %collective-permute-start.3 = (bf16[256,384]{1,0:T(8,128)(2,1)S(1)}, bf16[256,384]{1,0:T(8,128)(2,1)S(1)}, u32[]{:S(2)}, u32[]{:S(2)}) collective-permute-start(bf16[256,384]{1,0:T(8,128)(2,1)S(1)} %copy-done.14), channel_id=1, source_target_pairs={{0,16},{16,0},{32,48},{48,32},{64,80},{80,64},{96,112},{112,96},{1... | collective-permute-start | bytes 589832 | tf_op jit(solution)/shard_map/ppermute | solution.py:501
  63.6 7.3 %collective-permute-start.4 = (bf16[256,384]{1,0:T(8,128)(2,1)S(1)}, bf16[256,384]{1,0:T(8,128)(2,1)S(1)}, u32[]{:S(2)}, u32[]{:S(2)}) collective-permute-start(bf16[256,384]{1,0:T(8,128)(2,1)S(1)} %copy-done.13), channel_id=1, source_target_pairs={{16,32},{48,64},{80,96},{112,128},{144,160},{176,192},{208,224},{3... | collective-permute-start | bytes 589832 | tf_op jit(solution)/shard_map/ppermute | solution.py:502
  66.9 4.0 %copy-start.7 = (bf16[256,384]{1,0:T(8,128)(2,1)}, bf16[256,384]{1,0:T(8,128)(2,1)S(1)}, u32[]{:S(2)}) copy-start(bf16[256,384]{1,0:T(8,128)(2,1)S(1)} %collective-permute-done.3._.chip_hbm.old_chip) | copy-start | bytes 589828
  71.5 3.8 %collective-permute-start.5 = (bf16[2048,128]{1,0:T(8,128)(2,1)S(1)}, bf16[2048,128]{1,0:T(8,128)(2,1)S(1)}, u32[]{:S(2)}, u32[]{:S(2)}) collective-permute-start(bf16[2048,128]{1,0:T(8,128)(2,1)S(1)} %bitcast.11), channel_id=1, source_target_pairs={{0,16},{16,0},{1,17},{17,1},{2,18},{18,2},{3,19},{19,3},{4,20},{20... | collective-permute-start | bytes 1572872 | tf_op jit(solution)/shard_map/ppermute | solution.py:493
  86.0 13.1 %copy-start.2 = (bf16[256,1024]{1,0:T(8,128)(2,1)S(1)}, bf16[256,1024]{1,0:T(8,128)(2,1)}, u32[]{:S(2)}) copy-start(bf16[256,1024]{1,0:T(8,128)(2,1)} %get-tuple-element.47.picked_inv) | copy-start | bytes 1572868
  86.0 13.1 %all-to-all-start.3 = ((bf16[16,80,128]{2,1,0:T(8,128)(2,1)}), bf16[16,80,128]{2,1,0:T(8,128)(2,1)S(1)}, u32[]{:S(2)}, u32[]{:S(2)}) async-start(bf16[16,80,128]{2,1,0:T(8,128)(2,1)} %get-tuple-element.46), calls=%async_computation.3 | async-start | bytes 655360 | tf_op jit(solution)/shard_map/all_to_all | solution.py:489
  95.4 32.3 %copy-start.16 = (bf16[256,256]{1,0:T(8,128)(2,1)S(1)}, bf16[256,256]{1,0:T(8,128)(2,1)}, u32[]{:S(2)}) copy-start(bf16[256,256]{1,0:T(8,128)(2,1)} %get-tuple-element.55) | copy-start | bytes 393220
  95.4 34.0 %copy-start.15 = (bf16[256,256]{1,0:T(8,128)(2,1)S(1)}, bf16[256,256]{1,0:T(8,128)(2,1)}, u32[]{:S(2)}) copy-start(bf16[256,256]{1,0:T(8,128)(2,1)} %get-tuple-element.56) | copy-start | bytes 393220
  99.4 2.9 %collective-permute-start.6 = (f32[136,128]{1,0:T(8,128)S(1)}, f32[136,128]{1,0:T(8,128)S(1)}, u32[]{:S(2)}, u32[]{:S(2)}) collective-permute-start(f32[136,128]{1,0:T(8,128)S(1)} %get-tuple-element.51), channel_id=1, source_target_pairs={{0,16},{16,0},{1,17},{17,1},{2,18},{18,2},{3,19},{19,3},{4,20},{20... | collective-permute-start | bytes 208904 | tf_op jit(solution)/shard_map/ppermute | solution.py:493
  103.1 20.0 %all-to-all-start.4 = ((bf16[8,144,128]{2,1,0:T(8,128)(2,1)}), bf16[8,144,128]{2,1,0:T(8,128)(2,1)S(1)}, u32[]{:S(2)}, u32[]{:S(2)}) async-start(bf16[8,144,128]{2,1,0:T(8,128)(2,1)} %shard_map.95), calls=%async_computation.4 | async-start | bytes 589824 | tf_op jit(solution)/shard_map/all_to_all | solution.py:489
  110.6 7.4 %collective-permute-start.7 = (bf16[2,256,256]{2,1,0:T(8,128)(2,1)}, bf16[2,256,256]{2,1,0:T(8,128)(2,1)S(1)}, u32[]{:S(2)}, u32[]{:S(2)}) collective-permute-start(bf16[2,256,256]{2,1,0:T(8,128)(2,1)} %get-tuple-element.52), channel_id=1, source_target_pairs={{0,1},{1,0},{2,3},{3,2},{4,5},{5,4},{6,7},{7,6},{8,9},{9,8},{10,11... | collective-permute-start | bytes 786440 | tf_op jit(solution)/shard_map/ppermute | solution.py:503
  110.7 7.4 %collective-permute-start.8 = (bf16[2,256,256]{2,1,0:T(8,128)(2,1)}, bf16[2,256,256]{2,1,0:T(8,128)(2,1)S(1)}, u32[]{:S(2)}, u32[]{:S(2)}) collective-permute-start(bf16[2,256,256]{2,1,0:T(8,128)(2,1)} %get-tuple-element.53), channel_id=1, source_target_pairs={{1,2},{3,4},{5,6},{7,8},{9,10},{11,12},{13,14},{2,1},{4,3},{6,5},{... | collective-permute-start | bytes 786440 | tf_op jit(solution)/shard_map/ppermute | solution.py:504
  118.1 5.0 %copy-start.9 = (bf16[2,256,256]{2,1,0:T(8,128)(2,1)}, bf16[2,256,256]{2,1,0:T(8,128)(2,1)S(1)}, u32[]{:S(2)}) copy-start(bf16[2,256,256]{2,1,0:T(8,128)(2,1)S(1)} %collective-permute-done.7._.near_hbm) | copy-start | bytes 786436
  118.1 5.0 %copy-start.10 = (bf16[2,256,256]{2,1,0:T(8,128)(2,1)}, bf16[2,256,256]{2,1,0:T(8,128)(2,1)S(1)}, u32[]{:S(2)}) copy-start(bf16[2,256,256]{2,1,0:T(8,128)(2,1)S(1)} %collective-permute-done.8.__.other_hbm) | copy-start | bytes 786436
  124.1 12.6 %all-to-all-start.5 = ((bf16[16,128,128]{2,1,0:T(8,128)(2,1)}), bf16[16,128,128]{2,1,0:T(8,128)(2,1)S(1)}, u32[]{:S(2)}, u32[]{:S(2)}) async-start(bf16[16,128,128]{2,1,0:T(8,128)(2,1)} %get-tuple-element.54), calls=%async_computation.5 | async-start | bytes 1048576 | tf_op jit(solution)/shard_map/all_to_all | solution.py:489
  127.7 5.1 %collective-permute-start.9 = (bf16[256,256]{1,0:T(8,128)(2,1)S(1)}, bf16[256,256]{1,0:T(8,128)(2,1)S(1)}, u32[]{:S(2)}, u32[]{:S(2)}) collective-permute-start(bf16[256,256]{1,0:T(8,128)(2,1)S(1)} %copy-done.16), channel_id=1, source_target_pairs={{0,16},{16,0},{32,48},{48,32},{64,80},{80,64},{96,112},{112,96},{1... | collective-permute-start | bytes 393224 | tf_op jit(solution)/shard_map/ppermute | solution.py:501
  129.4 42.4 %copy-start = (f32[2,1024,128]{2,1,0:T(8,128)S(1)}, f32[2,1024,128]{2,1,0:T(8,128)}, u32[]{:S(2)}) copy-start(f32[2,1024,128]{2,1,0:T(8,128)} %get-tuple-element.62.search) | copy-start | bytes 3145732
  129.4 42.4 %copy-start.1 = (f32[2,1024,128]{2,1,0:T(8,128)S(1)}, f32[2,1024,128]{2,1,0:T(8,128)}, u32[]{:S(2)}) copy-start(f32[2,1024,128]{2,1,0:T(8,128)} %get-tuple-element.63.prod) | copy-start | bytes 3145732
  129.4 6.7 %collective-permute-start.10 = (bf16[256,256]{1,0:T(8,128)(2,1)S(1)}, bf16[256,256]{1,0:T(8,128)(2,1)S(1)}, u32[]{:S(2)}, u32[]{:S(2)}) collective-permute-start(bf16[256,256]{1,0:T(8,128)(2,1)S(1)} %copy-done.15), channel_id=1, source_target_pairs={{16,32},{48,64},{80,96},{112,128},{144,160},{176,192},{208,224},{3... | collective-permute-start | bytes 393224 | tf_op jit(solution)/shard_map/ppermute | solution.py:502
  132.8 3.9 %copy-start.11 = (bf16[256,256]{1,0:T(8,128)(2,1)}, bf16[256,256]{1,0:T(8,128)(2,1)S(1)}, u32[]{:S(2)}) copy-start(bf16[256,256]{1,0:T(8,128)(2,1)S(1)} %collective-permute-done.9._.chip_hbm) | copy-start | bytes 393220
  136.7 4.9 %collective-permute-start.11 = (bf16[2048,128]{1,0:T(8,128)(2,1)S(1)}, bf16[2048,128]{1,0:T(8,128)(2,1)S(1)}, u32[]{:S(2)}, u32[]{:S(2)}) collective-permute-start(bf16[2048,128]{1,0:T(8,128)(2,1)S(1)} %bitcast.9), channel_id=1, source_target_pairs={{0,16},{16,0},{1,17},{17,1},{2,18},{18,2},{3,19},{19,3},{4,20},{20... | collective-permute-start | bytes 1572872 | tf_op jit(solution)/shard_map/ppermute | solution.py:493
  (3 other events, 3.6 us)

commit v3 on v2

--- a/solution.py
+++ b/solution.py
@@ -93,13 +93,18 @@
     return loads
 
 
-def lower_times(matrix, loads, right):
+def dot_turned(a, b):
+    return lax.dot_general(a, b, (((1,), (1,)), ((), ())), preferred_element_type=F32)
+
+
+def times_lower_turned(left, matrix, loads):
+    for load in loads:
+        load.wait()
     parts = []
     for block in range(B // E):
-        loads[block].wait()
         width = (block + 1) * E
-        parts.append(dot(matrix[block * E : width, :width], right[:width]))
-    return jnp.concatenate(parts, axis=0)
+        parts.append(dot_turned(left[:, :width], matrix[block * E : width, :width]))
+    return jnp.concatenate(parts, axis=1)
 
 
 def times_lower(left, matrix):
@@ -148,7 +153,7 @@
 
     def packed(s, edge):
         rows = pl.ds(pl.multiple_of(edge * E, E), E)
-        parts = list(split2(interface[s, rows, :]))
+        parts = [interface[s, rows, :].astype(BF16)]
         if extra is not None:
             parts.append(extra[s, rows, :])
         return jnp.concatenate(parts, axis=1)
@@ -174,11 +179,10 @@
         facs.append(fetch_lower(copies, fac_hbm.at[s, 0], lbuf.at[s]))
     grid_row = lax.axis_index("z") * (2 * CS) + lax.axis_index("core") * 2
     grid_col = lax.axis_index("x") * YS + lax.axis_index("y")
-    lane = iota((B, K), 1)
     for copy in small:
         copy.wait()
     masks = [active_mask(sizes[s]) for s in range(2)]
-    pick_col = jnp.where((iota((B, K), 0) == lane * STRIDE) & (lane < CORN), 1.0, 0.0).astype(BF16)
+    pick = jnp.where(iota((CORN, B), 1) == iota((CORN, B), 0) * STRIDE, 1.0, 0.0).astype(BF16)
     columns = []
     for s in range(2):
         place = jnp.full((1, B), grid_row + s + grid_col, jnp.int32).astype(F32)
@@ -195,12 +199,11 @@
         copies.send(searchv.at[s], search.at[s])
     corners = []
     for s in range(2):
-        right = jnp.concatenate([searchv[s].astype(BF16), pick_col], axis=1)
-        wide = lower_times(lbuf.at[s], facs[s], right)
-        turned = jnp.transpose(wide).astype(BF16)
+        left = jnp.concatenate([jnp.transpose(searchv[s]).astype(BF16), pick], axis=0)
+        turned = times_lower_turned(left, lbuf.at[s], facs[s]).astype(BF16)
         halfv[s] = turned
         copies.send(halfv.at[s], half.at[s])
-        rows = dot(turned[K : K + CORN], wide[:, :K].astype(BF16))
+        rows = dot_turned(turned[K:], turned[:K])
         corners.append(corner_mask(sizes[s]) * rows)
     cm = two_rows(cmap)
     tail = rows_of((16, K), [(cm >> 8).astype(F32), (cm & 255).astype(F32)])
@@ -240,7 +243,7 @@
         back = jnp.transpose(times_lower(half.at[s], lbuf.at[s]))
         interv[s] = mask * back[:, :K]
         copies.send(interv.at[s], inter.at[s])
-        ghigh, glow = split2(mask * back[:, K:])
+        ghigh, glow = split2(mask * jnp.concatenate([back[:, K:], jnp.zeros((B, K - CORN), F32)], axis=1))
         low_moved = pltpu.roll(glow.astype(F32), CORN, axis=1)
         gramv[s] = jnp.where(
             lane < CORN, ghigh.astype(F32), jnp.where(lane < 2 * CORN, low_moved, digits)
@@ -355,7 +358,7 @@
     full = [inter[s] + dot(gram[s], stacked(s)) for s in range(2)]
 
     def arrived(edge, gedge, number):
-        return edge[:, :K].astype(F32) + edge[:, K : 2 * K].astype(F32) + dot(gedge, stacked(number))
+        return edge[:, :K].astype(F32) + dot(gedge, stacked(number))
 
     above = [arrived(north, gnorth, 2), full[0][E : 2 * E]]
     below = [full[1][0:E], arrived(south, gsouth, 3)]
@@ -368,7 +371,7 @@
 
 
 def edge_grams(chip, far, near, other):
-    return chip[:, 2 * K :], far[:, 2 * K :], near[:, :, 2 * K :], other[:, :, 2 * K :]
+    return chip[:, K:], far[:, K:], near[:, :, K:], other[:, :, K:]
 
 
 def second_kernel(sizes, sol_own, sol_other, inter_hbm, gram_hbm, chip_hbm, far_hbm, near_hbm, other_hbm,
@@ -403,11 +406,12 @@
     corner_in.wait()
     corners = []
     for s in range(2):
-        wide = lower_times(lbuf.at[s], facs[s], jnp.concatenate(split2(prodv[s]), axis=1))
-        inner = wide[:, :K] + wide[:, K:]
-        halfv[s] = jnp.concatenate(split2(jnp.transpose(inner)), axis=0)
+        left = jnp.concatenate(split2(jnp.transpose(prodv[s])), axis=0)
+        wide = times_lower_turned(left, lbuf.at[s], facs[s])
+        turned = jnp.concatenate(split2(wide[:K] + wide[K:]), axis=0)
+        halfv[s] = turned
         copies.send(halfv.at[s], half.at[s])
-        rows = dot(corner[s], jnp.concatenate(split2(inner), axis=1))
+        rows = dot_turned(corner[s], turned)
         corners.append(corner_mask(sizes[s]) * (rows[:, :K] + rows[:, K:]))
     rows = [jnp.zeros((1, K), F32)] * 2 + list(split3(cross)) + list(split3(energy))
     send_payload(copies, pay, block, corners, rows_of((16, K), rows))
@@ -439,7 +443,7 @@
     copies = Copies(sem)
     edges = (chip, far, near, other)
     grams = (gchip, gfar, gnear, gother)
-    width = pl.ds(2 * K, K)
+    width = pl.ds(K, K)
     loads = [copies.fetch(gram_hbm, gram)]
     loads += [copies.fetch(a.at[:, width], b) for a, b in zip((old_chip, old_far), grams[:2])]
     loads += [copies.fetch(a.at[:, :, width], b) for a, b in zip((old_near, old_other), grams[2:])]
@@ -462,19 +466,19 @@
         cross += jnp.sum(before * jumped, axis=0, keepdims=True)
         energy += jnp.sum(jumped * jumped, axis=0, keepdims=True)
     block = rows_of((8, K), [cross, energy])
-    for dest in range(CS * XS):
+    for dest in range(CS * YS):
         pay[dest] = block
 
 
 def partial_kernel(rec, pay):
-    total = sum(rec[b] for b in range(CS * XS))
-    for dest in range(ZS * YS):
+    total = sum(rec[b] for b in range(CS * YS))
+    for dest in range(ZS * XS):
         pay[dest] = total
 
 
 def last_kernel(rec, stats, res1, jump1, search, prod, mult, res, multv, resv, sem):
     copies = Copies(sem)
-    total = sum(rec[b] for b in range(ZS * YS))
+    total = sum(rec[b] for b in range(ZS * XS))
     first = stats[0:1] / (stats[1:2] + 1e-06)
     step = total[0:1] / (total[1:2] + 1e-06)
     for s in range(2):
@@ -528,6 +532,7 @@
     whole = ((2, B, K), F32)
     gramed = ((2, B, K), BF16)
     halved = ((2, 2 * K, B), BF16)
+    cornered = ((2, K + CORN, B), BF16)
     square = ((2, B, B), BF16)
     payload = ((SY, ROWS, K), BF16)
     block = (payload[0][1:], BF16)
@@ -538,20 +543,20 @@
 
     res, search, half, pay = call(
         first_kernel,
-        [whole, whole, halved, payload],
+        [whole, whole, cornered, payload],
         [HB] * 6,
         [HB] * 4,
-        [square, square, ((2, 1, B, K), BF16), whole, whole, halved, block]
+        [square, square, ((2, 1, B, K), BF16), whole, whole, cornered, block]
         + [((2, 1, B), jnp.int32), ((2, 1, CORN), jnp.int32), pltpu.SMEM((2,), jnp.int32), sems(20 + SY)],
     )(sizes, snow_level, cmap, pressure, pre, factor)
     rec = all_to_all(pay, ("x", "y"))
-    wide = edges_of(3 * K)
+    wide = edges_of(2 * K)
     inter, gram, *edges = call(
         back_first_kernel,
         [whole, gramed] + wide,
         [SM, VM, HB, HB],
         [HB] * 6,
-        [halved, square, whole, gramed] + wide + [sems(18)],
+        [cornered, square, whole, gramed] + wide + [sems(18)],
     )(sizes, cmap, half, factor)
     arrived = exchange(*edges)
     own, snd, picked_inv = call(
@@ -570,7 +575,7 @@
         [whole, gramed] + wide + [whole, square, square, ((2, CORN, B), BF16), whole, whole, halved, block, sems(24 + SY)],
     )(sizes, sol_own, sol_other, inter, gram, *arrived, res, pre, factor, half)
     rec = all_to_all(pay, ("x", "y"))
-    slim = edges_of(2 * K)
+    slim = edges_of(K)
     inter1, *edges = call(
         back_next_kernel,
         [whole] + slim,
@@ -583,14 +588,14 @@
     sol_own, sol_other, stats = coarse_solution(own, snd, arrived1)
     res1, jump1, pay = call(
         third_kernel,
-        [whole] * 2 + [((CS * XS, 8, K), F32)],
+        [whole] * 2 + [((CS * YS, 8, K), F32)],
         [SM] + [VM] * 3 + [HB] * 12,
         [VM] * 3,
         [whole, gramed] + slim + edges_of(K) + [whole, whole, sems(12)],
     )(sizes, sol_own, sol_other, stats, inter1, gram, *arrived1, *arrived, res, jump0)
-    rec = all_to_all(pay, ("core", "x"))
-    (pay,) = call(partial_kernel, [((ZS * YS, 8, K), F32)], [VM], [VM])(rec)
-    rec = all_to_all(pay, ("z", "y"))
+    rec = all_to_all(pay, ("core", "y"))
+    (pay,) = call(partial_kernel, [((ZS * XS, 8, K), F32)], [VM], [VM])(rec)
+    rec = all_to_all(pay, ("z", "x"))
     mult, res = call(last_kernel, [whole] * 2, [VM] * 6, [HB] * 2, [whole, whole, sems(4)])(
         rec, stats, res1, jump1, search, prod
     )

time: 174 us -> 164 us (0.943)
  starting transfers between devices: 59.8 us -> 54.3 us
  Pallas kernels: 43.5 us -> 39.7 us
  blocking collectives: 26 us -> 22.5 us
  waiting for transfers between devices: 42.3 us -> 45.7 us
    all_to_all x6, waiting for transfers between devices: 14.1 us -> 23.3 us  [all_to_all(): return lax.all_to_all(value, axes, split_axis=0, concat_axis=0)]
    ppermute x2, waiting for transfers between devices: 16.1 us -> 10.5 us  [exchange(): lax.ppermute(near, cols, even)]
    pallas_call x15, Pallas kernels: 43.5 us -> 39.7 us  [placed(): run(*[pltpu.with_memory_space_constraint(a, pltpu.HBM) if spec is HB else...]
    all_to_all x2, blocking collectives: 26 us -> 22.5 us  [all_to_all(): return lax.all_to_all(value, axes, split_axis=0, concat_axis=0)]
    all_to_all x6, starting transfers between devices: 37.7 us -> 34.3 us  [all_to_all(): return lax.all_to_all(value, axes, split_axis=0, concat_axis=0)]
  transfers between devices with their start and end apart: 18 -> 18, of which waited for: 13 -> 14; matrix products, arithmetic and copies ran while one was open for 0% -> 0% of each run, Pallas kernels for 6% -> 6%
where the time goes in v3:
time: 164 us; the launch traced here: 163 us
  starting transfers between devices  54.3 us (33%)
  waiting for transfers between devices  45.7 us (28%)
  Pallas kernels  39.7 us (24%)
  blocking collectives  22.5 us (14%)
    pallas_call x15, Pallas kernels, placed(): run(*[pltpu.with_memory_space_constraint(a, pltpu.HBM) if spec is HB else...  39.7 us
    all_to_all x6, starting transfers between devices, all_to_all(): return lax.all_to_all(value, axes, split_axis=0, concat_axis=0)  34.3 us
    all_to_all x6, waiting for transfers between devices, all_to_all(): return lax.all_to_all(value, axes, split_axis=0, concat_axis=0)  23.3 us
    all_to_all x2, blocking collectives, all_to_all(): return lax.all_to_all(value, axes, split_axis=0, concat_axis=0)  22.5 us
    ppermute x2, waiting for transfers between devices, exchange(): lax.ppermute(near, cols, even)  10.5 us
    ppermute x4, starting transfers between devices, swap(): return lax.ppermute(value, 'core', [(0, 1), (1, 0)])  10.3 us
    ppermute x2, waiting for transfers between devices, exchange(): lax.ppermute(far, rows, odd)  7.01 us
    ppermute x2, starting transfers between devices, exchange(): lax.ppermute(far, rows, odd)  5.37 us
  transfers between devices with their start and end apart: 18, of which 14 were waited for; matrix products, arithmetic and copies ran while one was open for 0% of the time, Pallas kernels for 6%

profile of v3, /device:TPU:1, one launch (start us, length us, event | category | flops | bytes accessed | tf_op | source)
XLA Modules:
  0.0 163.4 jit_solution(7704827953744017676)
XLA Ops:
  0.7 6.9 %shard_map.86 = (f32[2,1024,128]{2,1,0:T(8,128)}, f32[2,1024,128]{2,1,0:T(8,128)}, bf16[2,160,1024]{2,1,0:T(8,128)(2,1)}, bf16[16,80,128]{2,1,0:T(8,128)(2,1)}) custom-call(s32[2]{0:T(128)} %bitcast.13, s32[2,1,1024]{2,1,0:T(1,128)} %snow_hbm.1, s32[2,1,32]{2,1,0:T(1,128)} %cmap.1, bf16[2,1,1024,128]{3,2,1,0:T(8,128)(2,1)} %press_hbm.1, ...), custom_call_target="tpu_custom_call" | custom-call | tf_op jit(solution)/shard_map/pallas_call | solution.py:57
  7.5 7.6 %all-to-all-start = ((bf16[16,80,128]{2,1,0:T(8,128)(2,1)}), bf16[16,80,128]{2,1,0:T(8,128)(2,1)S(1)}, u32[]{:S(2)}, u32[]{:S(2)}) async-start(bf16[16,80,128]{2,1,0:T(8,128)(2,1)} %get-tuple-element.34), calls=%async_computation | async-start | bytes 655360 | tf_op jit(solution)/shard_map/all_to_all | solution.py:493
  15.2 4.7 %shard_map.87 = (f32[2,1024,128]{2,1,0:T(8,128)}, bf16[2,1024,128]{2,1,0:T(8,128)(2,1)}, bf16[256,256]{1,0:T(8,128)(2,1)}, bf16[256,256]{1,0:T(8,128)(2,1)}, bf1...) custom-call(s32[2]{0:T(128)S(1)} %bitcast.14, s32[2,1,32]{2,1,0:T(1,128)S(1)} %copy-done.4, ...), custom_call_target="tpu_custom_call" | custom-call | tf_op jit(solution)/shard_map/pallas_call | solution.py:57
  19.9 3.1 %all-to-all-done.rec = bf16[16,80,128]{2,1,0:T(8,128)(2,1)S(1)} async-done(((bf16[16,80,128]{2,1,0:T(8,128)(2,1)}), bf16[16,80,128]{2,1,0:T(8,128)(2,1)S(1)}, u32[]{:S(2)}, u32[]{:S(2)}) %all-to-all-start) | async-done | bytes 327712 | tf_op jit(solution)/shard_map/all_to_all | solution.py:493
  23.0 4.7 %shard_map.88 = (f32[136,128]{1,0:T(8,128)S(1)}, f32[136,128]{1,0:T(8,128)S(1)}, bf16[256,1024]{1,0:T(8,128)(2,1)}) custom-call(bf16[16,80,128]{2,1,0:T(8,128)(2,1)S(1)} %all-to-all-done.rec, bf16[256,4096]{1,0:T(8,128)(2,1)} %coarse_hbm.1, bf16[2,1024,128]{2,1,0:T(8,128)(2,1)} %get-tuple-element.36._.gram_hbm), custom_call_target="tpu_custom_call" | custom-call | tf_op jit(solution)/shard_map/pallas_call | solution.py:57
  27.7 2.4 %collective-permute-start = (f32[136,128]{1,0:T(8,128)S(1)}, f32[136,128]{1,0:T(8,128)S(1)}, u32[]{:S(2)}, u32[]{:S(2)}) collective-permute-start(f32[136,128]{1,0:T(8,128)S(1)} %get-tuple-element.38), channel_id=1, source_target_pairs={{0,16},{16,0},{1,17},{17,1},{2,18},{18,2},{3,19},{19,3},{4,20},{20... | collective-permute-start | bytes 208904 | tf_op jit(solution)/shard_map/ppermute | solution.py:497
  31.8 8.2 %all-to-all-start.1 = ((bf16[8,144,128]{2,1,0:T(8,128)(2,1)}), bf16[8,144,128]{2,1,0:T(8,128)(2,1)S(1)}, u32[]{:S(2)}, u32[]{:S(2)}) async-start(bf16[8,144,128]{2,1,0:T(8,128)(2,1)} %shard_map.89), calls=%async_computation.1 | async-start | bytes 589824 | tf_op jit(solution)/shard_map/all_to_all | solution.py:493
  40.8 6.6 %collective-permute-done.1._.near_hbm.old_near = bf16[2,256,256]{2,1,0:T(8,128)(2,1)S(1)} collective-permute-done((bf16[2,256,256]{2,1,0:T(8,128)(2,1)}, bf16[2,256,256]{2,1,0:T(8,128)(2,1)S(1)}, u32[]{:S(2)}, u32[]{:S(2)}) %collective-permute-start.1) | collective-permute-done | bytes 262176 | tf_op jit(solution)/shard_map/ppermute | solution.py:507
  47.5 5.0 %all-to-all-done.1.rec = bf16[8,144,128]{2,1,0:T(8,128)(2,1)S(1)} async-done(((bf16[8,144,128]{2,1,0:T(8,128)(2,1)}), bf16[8,144,128]{2,1,0:T(8,128)(2,1)S(1)}, u32[]{:S(2)}, u32[]{:S(2)}) %all-to-all-start.1) | async-done | bytes 294944 | tf_op jit(solution)/shard_map/all_to_all | solution.py:493
  52.5 1.6 shard_map.90
  54.1 3.6 %all-to-all-start.2 = ((bf16[16,128,128]{2,1,0:T(8,128)(2,1)}), bf16[16,128,128]{2,1,0:T(8,128)(2,1)S(1)}, u32[]{:S(2)}, u32[]{:S(2)}) async-start(bf16[16,128,128]{2,1,0:T(8,128)(2,1)} %get-tuple-element.41), calls=%async_computation.2 | async-start | bytes 1048576 | tf_op jit(solution)/shard_map/all_to_all | solution.py:493
  57.7 1.7 %collective-permute-start.3 = (bf16[256,256]{1,0:T(8,128)(2,1)S(1)}, bf16[256,256]{1,0:T(8,128)(2,1)S(1)}, u32[]{:S(2)}, u32[]{:S(2)}) collective-permute-start(bf16[256,256]{1,0:T(8,128)(2,1)S(1)} %copy-done.14), channel_id=1, source_target_pairs={{0,16},{16,0},{32,48},{48,32},{64,80},{80,64},{96,112},{112,96},{1... | collective-permute-start | bytes 393224 | tf_op jit(solution)/shard_map/ppermute | solution.py:505
  59.3 3.3 %collective-permute-start.4 = (bf16[256,256]{1,0:T(8,128)(2,1)S(1)}, bf16[256,256]{1,0:T(8,128)(2,1)S(1)}, u32[]{:S(2)}, u32[]{:S(2)}) collective-permute-start(bf16[256,256]{1,0:T(8,128)(2,1)S(1)} %copy-done.13), channel_id=1, source_target_pairs={{16,32},{48,64},{80,96},{112,128},{144,160},{176,192},{208,224},{3... | collective-permute-start | bytes 393224 | tf_op jit(solution)/shard_map/ppermute | solution.py:506
  62.6 3.3 %collective-permute-done.4.__.far_hbm.old_far = bf16[256,256]{1,0:T(8,128)(2,1)S(1)} collective-permute-done((bf16[256,256]{1,0:T(8,128)(2,1)S(1)}, bf16[256,256]{1,0:T(8,128)(2,1)S(1)}, u32[]{:S(2)}, u32[]{:S(2)}) %collective-permute-start.4) | collective-permute-done | bytes 131104 | tf_op jit(solution)/shard_map/ppermute | solution.py:506
  66.7 3.3 %collective-permute-start.5 = (bf16[2048,128]{1,0:T(8,128)(2,1)S(1)}, bf16[2048,128]{1,0:T(8,128)(2,1)S(1)}, u32[]{:S(2)}, u32[]{:S(2)}) collective-permute-start(bf16[2048,128]{1,0:T(8,128)(2,1)S(1)} %bitcast.11), channel_id=1, source_target_pairs={{0,16},{16,0},{1,17},{17,1},{2,18},{18,2},{3,19},{19,3},{4,20},{20... | collective-permute-start | bytes 1572872 | tf_op jit(solution)/shard_map/ppermute | solution.py:497
  70.1 1.5 collective-permute-done.5.sol_other
  71.6 9.2 %shard_map.92 = (f32[2,1024,128]{2,1,0:T(8,128)}, f32[2,1024,128]{2,1,0:T(8,128)}, bf16[2,256,1024]{2,1,0:T(8,128)(2,1)}, bf16[16,80,128]{2,1,0:T(8,128)(2,1)}) custom-call(s32[2]{0:T(128)S(1)} %bitcast.15, bf16[2048,128]{1,0:T(8,128)(2,1)S(1)} %bitcast.12, bf16[2048,128]{1,0:T(8,128)(2,1)S(1)} %collective-permute-done.5.sol_other, ...), custom_call_target="tpu_custom_call" | custom-call | tf_op jit(solution)/shard_map/pallas_call | solution.py:57
  80.8 3.9 %all-to-all-start.3 = ((bf16[16,80,128]{2,1,0:T(8,128)(2,1)}), bf16[16,80,128]{2,1,0:T(8,128)(2,1)S(1)}, u32[]{:S(2)}, u32[]{:S(2)}) async-start(bf16[16,80,128]{2,1,0:T(8,128)(2,1)} %get-tuple-element.46), calls=%async_computation.3 | async-start | bytes 655360 | tf_op jit(solution)/shard_map/all_to_all | solution.py:493
  84.7 4.3 %shard_map.93 = (f32[2,1024,128]{2,1,0:T(8,128)}, bf16[256,128]{1,0:T(8,128)(2,1)}, bf16[256,128]{1,0:T(8,128)(2,1)}, bf16[2,256,128]{2,1,0:T(8,128)(2,1)}, bf16[2,256,128]{2,1,0:T(8,128)(2,1)}) custom-call(s32[2]{0:T(128)S(1)} %bitcast.16, bf16[2,256,1024]{2,1,0:T(8,128)(2,1)} %get-tuple-element.48.half_hbm, bf16[2,1,1024,1024]{3,2,1,0:T(8,128)(2,1)} %fac_hbm.7), custom_call_target="tpu_custom_call" | custom-call | tf_op jit(solution)/shard_map/pallas_call | solution.py:57
  89.1 3.8 %all-to-all-done.3.rec = bf16[16,80,128]{2,1,0:T(8,128)(2,1)S(1)} async-done(((bf16[16,80,128]{2,1,0:T(8,128)(2,1)}), bf16[16,80,128]{2,1,0:T(8,128)(2,1)S(1)}, u32[]{:S(2)}, u32[]{:S(2)}) %all-to-all-start.3) | async-done | bytes 327712 | tf_op jit(solution)/shard_map/all_to_all | solution.py:493
  93.2 2.0 %collective-permute-start.6 = (f32[136,128]{1,0:T(8,128)S(1)}, f32[136,128]{1,0:T(8,128)S(1)}, u32[]{:S(2)}, u32[]{:S(2)}) collective-permute-start(f32[136,128]{1,0:T(8,128)S(1)} %get-tuple-element.51), channel_id=1, source_target_pairs={{0,16},{16,0},{1,17},{17,1},{2,18},{18,2},{3,19},{19,3},{4,20},{20... | collective-permute-start | bytes 208904 | tf_op jit(solution)/shard_map/ppermute | solution.py:497
  97.0 7.2 %all-to-all-start.4 = ((bf16[8,144,128]{2,1,0:T(8,128)(2,1)}), bf16[8,144,128]{2,1,0:T(8,128)(2,1)S(1)}, u32[]{:S(2)}, u32[]{:S(2)}) async-start(bf16[8,144,128]{2,1,0:T(8,128)(2,1)} %shard_map.95), calls=%async_computation.4 | async-start | bytes 589824 | tf_op jit(solution)/shard_map/all_to_all | solution.py:493
  104.9 3.9 %collective-permute-done.7._.near_hbm = bf16[2,256,128]{2,1,0:T(8,128)(2,1)S(1)} collective-permute-done((bf16[2,256,128]{2,1,0:T(8,128)(2,1)}, bf16[2,256,128]{2,1,0:T(8,128)(2,1)S(1)}, u32[]{:S(2)}, u32[]{:S(2)}) %collective-permute-start.7) | collective-permute-done | bytes 131104 | tf_op jit(solution)/shard_map/ppermute | solution.py:507
  108.8 7.8 %all-to-all-done.4.rec = bf16[8,144,128]{2,1,0:T(8,128)(2,1)S(1)} async-done(((bf16[8,144,128]{2,1,0:T(8,128)(2,1)}), bf16[8,144,128]{2,1,0:T(8,128)(2,1)S(1)}, u32[]{:S(2)}, u32[]{:S(2)}) %all-to-all-start.4) | async-done | bytes 294944 | tf_op jit(solution)/shard_map/all_to_all | solution.py:493
  117.7 3.7 %all-to-all-start.5 = ((bf16[16,128,128]{2,1,0:T(8,128)(2,1)}), bf16[16,128,128]{2,1,0:T(8,128)(2,1)S(1)}, u32[]{:S(2)}, u32[]{:S(2)}) async-start(bf16[16,128,128]{2,1,0:T(8,128)(2,1)} %get-tuple-element.54), calls=%async_computation.5 | async-start | bytes 1048576 | tf_op jit(solution)/shard_map/all_to_all | solution.py:493
  122.7 2.1 %collective-permute-start.10 = (bf16[256,128]{1,0:T(8,128)(2,1)S(1)}, bf16[256,128]{1,0:T(8,128)(2,1)S(1)}, u32[]{:S(2)}, u32[]{:S(2)}) collective-permute-start(bf16[256,128]{1,0:T(8,128)(2,1)S(1)} %copy-done.15), channel_id=1, source_target_pairs={{16,32},{48,64},{80,96},{112,128},{144,160},{176,192},{208,224},{3... | collective-permute-start | bytes 196616 | tf_op jit(solution)/shard_map/ppermute | solution.py:506
  124.8 3.7 %collective-permute-done.10.__.far_hbm = bf16[256,128]{1,0:T(8,128)(2,1)S(1)} collective-permute-done((bf16[256,128]{1,0:T(8,128)(2,1)S(1)}, bf16[256,128]{1,0:T(8,128)(2,1)S(1)}, u32[]{:S(2)}, u32[]{:S(2)}) %collective-permute-start.10) | collective-permute-done | bytes 65568 | tf_op jit(solution)/shard_map/ppermute | solution.py:506
  128.5 2.8 %all-to-all-done.5.source = bf16[16,128,128]{2,1,0:T(8,128)(2,1)S(1)} async-done(((bf16[16,128,128]{2,1,0:T(8,128)(2,1)}), bf16[16,128,128]{2,1,0:T(8,128)(2,1)S(1)}, u32[]{:S(2)}, u32[]{:S(2)}) %all-to-all-start.5) | async-done | bytes 524320 | tf_op jit(solution)/shard_map/all_to_all | solution.py:493
  131.3 2.5 %collective-permute-start.11 = (bf16[2048,128]{1,0:T(8,128)(2,1)S(1)}, bf16[2048,128]{1,0:T(8,128)(2,1)S(1)}, u32[]{:S(2)}, u32[]{:S(2)}) collective-permute-start(bf16[2048,128]{1,0:T(8,128)(2,1)S(1)} %bitcast.9), channel_id=1, source_target_pairs={{0,16},{16,0},{1,17},{17,1},{2,18},{18,2},{3,19},{19,3},{4,20},{20... | collective-permute-start | bytes 1572872 | tf_op jit(solution)/shard_map/ppermute | solution.py:497
  135.3 3.9 %shard_map.98 = (f32[2,1024,128]{2,1,0:T(8,128)S(1)}, f32[2,1024,128]{2,1,0:T(8,128)S(1)}, f32[8,8,128]{2,1,0:T(8,128)S(1)}) custom-call(s32[2]{0:T(128)S(1)} %bitcast.17, bf16[2048,128]{1,0:T(8,128)(2,1)S(1)} %bitcast.10, bf16[2048,128]{1,0:T(8,128)(2,1)S(1)} %collective-permute-done.11.sol_other, f32[8,128]{1,0:T(8,128)S(1)} %get-tuple-element.57.stats, ...), custom_call_target="tpu_custom_call" | custom-call | tf_op jit(solution)/shard_map/pallas_call | solution.py:57
  139.3 7.7 %all_to_all.40.rec = f32[8,8,128]{2,1,0:T(8,128)S(1)} all-to-all(f32[8,8,128]{2,1,0:T(8,128)S(1)} %get-tuple-element.59), channel_id=1, replica_groups=mesh['z'=8,'core'=2,'x'=4,'y'=4] {'core','y'}, dimensions={0} | all-to-all | bytes 65536 | tf_op jit(solution)/shard_map/all_to_all | solution.py:493
  146.9 14.8 %all_to_all.41.rec = f32[32,8,128]{2,1,0:T(8,128)S(1)} all-to-all(f32[32,8,128]{2,1,0:T(8,128)S(1)} %shard_map.99), channel_id=1, replica_groups=mesh['z'=8,'core'=2,'x'=4,'y'=4] {'z','x'}, dimensions={0} | all-to-all | bytes 262144 | tf_op jit(solution)/shard_map/all_to_all | solution.py:493
  (55 shorter events, 11.4 us)
Async XLA Ops:
  0.6 14.5 %copy-start.3 = (s32[2,1]{0,1:T(1,128)S(1)}, s32[2,1]{0,1:T(1,128)}, u32[]{:S(2)}) copy-start(s32[2,1]{0,1:T(1,128)} %param.10) | copy-start | bytes 28
  0.6 14.5 %copy-start.4 = (s32[2,1,32]{2,1,0:T(1,128)S(1)}, s32[2,1,32]{2,1,0:T(1,128)}, u32[]{:S(2)}) copy-start(s32[2,1,32]{2,1,0:T(1,128)} %cmap.1) | copy-start | bytes 772
  7.5 15.4 %all-to-all-start = ((bf16[16,80,128]{2,1,0:T(8,128)(2,1)}), bf16[16,80,128]{2,1,0:T(8,128)(2,1)S(1)}, u32[]{:S(2)}, u32[]{:S(2)}) async-start(bf16[16,80,128]{2,1,0:T(8,128)(2,1)} %get-tuple-element.34), calls=%async_computation | async-start | bytes 655360 | tf_op jit(solution)/shard_map/all_to_all | solution.py:493
  19.9 37.8 %copy-start.14 = (bf16[256,256]{1,0:T(8,128)(2,1)S(1)}, bf16[256,256]{1,0:T(8,128)(2,1)}, u32[]{:S(2)}) copy-start(bf16[256,256]{1,0:T(8,128)(2,1)} %get-tuple-element.42) | copy-start | bytes 393220
  19.9 39.5 %copy-start.13 = (bf16[256,256]{1,0:T(8,128)(2,1)S(1)}, bf16[256,256]{1,0:T(8,128)(2,1)}, u32[]{:S(2)}) copy-start(bf16[256,256]{1,0:T(8,128)(2,1)} %get-tuple-element.43) | copy-start | bytes 393220
  27.7 3.3 %collective-permute-start = (f32[136,128]{1,0:T(8,128)S(1)}, f32[136,128]{1,0:T(8,128)S(1)}, u32[]{:S(2)}, u32[]{:S(2)}) collective-permute-start(f32[136,128]{1,0:T(8,128)S(1)} %get-tuple-element.38), channel_id=1, source_target_pairs={{0,16},{16,0},{1,17},{17,1},{2,18},{18,2},{3,19},{19,3},{4,20},{20... | collective-permute-start | bytes 208904 | tf_op jit(solution)/shard_map/ppermute | solution.py:497
  31.8 20.6 %all-to-all-start.1 = ((bf16[8,144,128]{2,1,0:T(8,128)(2,1)}), bf16[8,144,128]{2,1,0:T(8,128)(2,1)S(1)}, u32[]{:S(2)}, u32[]{:S(2)}) async-start(bf16[8,144,128]{2,1,0:T(8,128)(2,1)} %shard_map.89), calls=%async_computation.1 | async-start | bytes 589824 | tf_op jit(solution)/shard_map/all_to_all | solution.py:493
  40.0 7.4 %collective-permute-start.1 = (bf16[2,256,256]{2,1,0:T(8,128)(2,1)}, bf16[2,256,256]{2,1,0:T(8,128)(2,1)S(1)}, u32[]{:S(2)}, u32[]{:S(2)}) collective-permute-start(bf16[2,256,256]{2,1,0:T(8,128)(2,1)} %get-tuple-element.39), channel_id=1, source_target_pairs={{0,1},{1,0},{2,3},{3,2},{4,5},{5,4},{6,7},{7,6},{8,9},{9,8},{10,11... | collective-permute-start | bytes 786440 | tf_op jit(solution)/shard_map/ppermute | solution.py:507
  40.2 7.3 %collective-permute-start.2 = (bf16[2,256,256]{2,1,0:T(8,128)(2,1)}, bf16[2,256,256]{2,1,0:T(8,128)(2,1)S(1)}, u32[]{:S(2)}, u32[]{:S(2)}) collective-permute-start(bf16[2,256,256]{2,1,0:T(8,128)(2,1)} %get-tuple-element.40), channel_id=1, source_target_pairs={{1,2},{3,4},{5,6},{7,8},{9,10},{11,12},{13,14},{2,1},{4,3},{6,5},{... | collective-permute-start | bytes 786440 | tf_op jit(solution)/shard_map/ppermute | solution.py:508
  47.5 5.0 %copy-start.5 = (bf16[2,256,256]{2,1,0:T(8,128)(2,1)}, bf16[2,256,256]{2,1,0:T(8,128)(2,1)S(1)}, u32[]{:S(2)}) copy-start(bf16[2,256,256]{2,1,0:T(8,128)(2,1)S(1)} %collective-permute-done.1._.near_hbm.old_near) | copy-start | bytes 786436
  47.5 5.0 %copy-start.6 = (bf16[2,256,256]{2,1,0:T(8,128)(2,1)}, bf16[2,256,256]{2,1,0:T(8,128)(2,1)S(1)}, u32[]{:S(2)}) copy-start(bf16[2,256,256]{2,1,0:T(8,128)(2,1)S(1)} %collective-permute-done.2.__.other_hbm.old_other) | copy-start | bytes 786436
  54.1 12.7 %all-to-all-start.2 = ((bf16[16,128,128]{2,1,0:T(8,128)(2,1)}), bf16[16,128,128]{2,1,0:T(8,128)(2,1)S(1)}, u32[]{:S(2)}, u32[]{:S(2)}) async-start(bf16[16,128,128]{2,1,0:T(8,128)(2,1)} %get-tuple-element.41), calls=%async_computation.2 | async-start | bytes 1048576 | tf_op jit(solution)/shard_map/all_to_all | solution.py:493
  57.7 5.0 %collective-permute-start.3 = (bf16[256,256]{1,0:T(8,128)(2,1)S(1)}, bf16[256,256]{1,0:T(8,128)(2,1)S(1)}, u32[]{:S(2)}, u32[]{:S(2)}) collective-permute-start(bf16[256,256]{1,0:T(8,128)(2,1)S(1)} %copy-done.14), channel_id=1, source_target_pairs={{0,16},{16,0},{32,48},{48,32},{64,80},{80,64},{96,112},{112,96},{1... | collective-permute-start | bytes 393224 | tf_op jit(solution)/shard_map/ppermute | solution.py:505
  59.3 6.6 %collective-permute-start.4 = (bf16[256,256]{1,0:T(8,128)(2,1)S(1)}, bf16[256,256]{1,0:T(8,128)(2,1)S(1)}, u32[]{:S(2)}, u32[]{:S(2)}) collective-permute-start(bf16[256,256]{1,0:T(8,128)(2,1)S(1)} %copy-done.13), channel_id=1, source_target_pairs={{16,32},{48,64},{80,96},{112,128},{144,160},{176,192},{208,224},{3... | collective-permute-start | bytes 393224 | tf_op jit(solution)/shard_map/ppermute | solution.py:506
  66.7 4.9 %collective-permute-start.5 = (bf16[2048,128]{1,0:T(8,128)(2,1)S(1)}, bf16[2048,128]{1,0:T(8,128)(2,1)S(1)}, u32[]{:S(2)}, u32[]{:S(2)}) collective-permute-start(bf16[2048,128]{1,0:T(8,128)(2,1)S(1)} %bitcast.11), channel_id=1, source_target_pairs={{0,16},{16,0},{1,17},{17,1},{2,18},{18,2},{3,19},{19,3},{4,20},{20... | collective-permute-start | bytes 1572872 | tf_op jit(solution)/shard_map/ppermute | solution.py:497
  80.8 12.1 %copy-start.2 = (bf16[256,1024]{1,0:T(8,128)(2,1)S(1)}, bf16[256,1024]{1,0:T(8,128)(2,1)}, u32[]{:S(2)}) copy-start(bf16[256,1024]{1,0:T(8,128)(2,1)} %get-tuple-element.47.picked_inv) | copy-start | bytes 1572868
  80.8 12.1 %all-to-all-start.3 = ((bf16[16,80,128]{2,1,0:T(8,128)(2,1)}), bf16[16,80,128]{2,1,0:T(8,128)(2,1)S(1)}, u32[]{:S(2)}, u32[]{:S(2)}) async-start(bf16[16,80,128]{2,1,0:T(8,128)(2,1)} %get-tuple-element.46), calls=%async_computation.3 | async-start | bytes 655360 | tf_op jit(solution)/shard_map/all_to_all | solution.py:493
  89.1 32.3 %copy-start.16 = (bf16[256,128]{1,0:T(8,128)(2,1)S(1)}, bf16[256,128]{1,0:T(8,128)(2,1)}, u32[]{:S(2)}) copy-start(bf16[256,128]{1,0:T(8,128)(2,1)} %get-tuple-element.55) | copy-start | bytes 196612
  89.1 33.6 %copy-start.15 = (bf16[256,128]{1,0:T(8,128)(2,1)S(1)}, bf16[256,128]{1,0:T(8,128)(2,1)}, u32[]{:S(2)}) copy-start(bf16[256,128]{1,0:T(8,128)(2,1)} %get-tuple-element.56) | copy-start | bytes 196612
  93.2 2.9 %collective-permute-start.6 = (f32[136,128]{1,0:T(8,128)S(1)}, f32[136,128]{1,0:T(8,128)S(1)}, u32[]{:S(2)}, u32[]{:S(2)}) collective-permute-start(f32[136,128]{1,0:T(8,128)S(1)} %get-tuple-element.51), channel_id=1, source_target_pairs={{0,16},{16,0},{1,17},{17,1},{2,18},{18,2},{3,19},{19,3},{4,20},{20... | collective-permute-start | bytes 208904 | tf_op jit(solution)/shard_map/ppermute | solution.py:497
  97.0 19.7 %all-to-all-start.4 = ((bf16[8,144,128]{2,1,0:T(8,128)(2,1)}), bf16[8,144,128]{2,1,0:T(8,128)(2,1)S(1)}, u32[]{:S(2)}, u32[]{:S(2)}) async-start(bf16[8,144,128]{2,1,0:T(8,128)(2,1)} %shard_map.95), calls=%async_computation.4 | async-start | bytes 589824 | tf_op jit(solution)/shard_map/all_to_all | solution.py:493
  104.2 4.6 %collective-permute-start.7 = (bf16[2,256,128]{2,1,0:T(8,128)(2,1)}, bf16[2,256,128]{2,1,0:T(8,128)(2,1)S(1)}, u32[]{:S(2)}, u32[]{:S(2)}) collective-permute-start(bf16[2,256,128]{2,1,0:T(8,128)(2,1)} %get-tuple-element.52), channel_id=1, source_target_pairs={{0,1},{1,0},{2,3},{3,2},{4,5},{5,4},{6,7},{7,6},{8,9},{9,8},{10,11... | collective-permute-start | bytes 393224 | tf_op jit(solution)/shard_map/ppermute | solution.py:507
  104.3 4.6 %collective-permute-start.8 = (bf16[2,256,128]{2,1,0:T(8,128)(2,1)}, bf16[2,256,128]{2,1,0:T(8,128)(2,1)S(1)}, u32[]{:S(2)}, u32[]{:S(2)}) collective-permute-start(bf16[2,256,128]{2,1,0:T(8,128)(2,1)} %get-tuple-element.53), channel_id=1, source_target_pairs={{1,2},{3,4},{5,6},{7,8},{9,10},{11,12},{13,14},{2,1},{4,3},{6,5},{... | collective-permute-start | bytes 393224 | tf_op jit(solution)/shard_map/ppermute | solution.py:508
  108.8 7.8 %copy-start.9 = (bf16[2,256,128]{2,1,0:T(8,128)(2,1)}, bf16[2,256,128]{2,1,0:T(8,128)(2,1)S(1)}, u32[]{:S(2)}) copy-start(bf16[2,256,128]{2,1,0:T(8,128)(2,1)S(1)} %collective-permute-done.7._.near_hbm) | copy-start | bytes 393220
  108.8 7.8 %copy-start.10 = (bf16[2,256,128]{2,1,0:T(8,128)(2,1)}, bf16[2,256,128]{2,1,0:T(8,128)(2,1)S(1)}, u32[]{:S(2)}) copy-start(bf16[2,256,128]{2,1,0:T(8,128)(2,1)S(1)} %collective-permute-done.8.__.other_hbm) | copy-start | bytes 393220
  117.6 44.1 %copy-start = (f32[2,1024,128]{2,1,0:T(8,128)S(1)}, f32[2,1024,128]{2,1,0:T(8,128)}, u32[]{:S(2)}) copy-start(f32[2,1024,128]{2,1,0:T(8,128)} %get-tuple-element.62.search) | copy-start | bytes 3145732
  117.6 44.1 %copy-start.1 = (f32[2,1024,128]{2,1,0:T(8,128)S(1)}, f32[2,1024,128]{2,1,0:T(8,128)}, u32[]{:S(2)}) copy-start(f32[2,1024,128]{2,1,0:T(8,128)} %get-tuple-element.63.prod) | copy-start | bytes 3145732
  117.7 13.6 %all-to-all-start.5 = ((bf16[16,128,128]{2,1,0:T(8,128)(2,1)}), bf16[16,128,128]{2,1,0:T(8,128)(2,1)S(1)}, u32[]{:S(2)}, u32[]{:S(2)}) async-start(bf16[16,128,128]{2,1,0:T(8,128)(2,1)} %get-tuple-element.54), calls=%async_computation.5 | async-start | bytes 1048576 | tf_op jit(solution)/shard_map/all_to_all | solution.py:493
  121.4 3.4 %collective-permute-start.9 = (bf16[256,128]{1,0:T(8,128)(2,1)S(1)}, bf16[256,128]{1,0:T(8,128)(2,1)S(1)}, u32[]{:S(2)}, u32[]{:S(2)}) collective-permute-start(bf16[256,128]{1,0:T(8,128)(2,1)S(1)} %copy-done.16), channel_id=1, source_target_pairs={{0,16},{16,0},{32,48},{48,32},{64,80},{80,64},{96,112},{112,96},{1... | collective-permute-start | bytes 196616 | tf_op jit(solution)/shard_map/ppermute | solution.py:505
  122.7 5.9 %collective-permute-start.10 = (bf16[256,128]{1,0:T(8,128)(2,1)S(1)}, bf16[256,128]{1,0:T(8,128)(2,1)S(1)}, u32[]{:S(2)}, u32[]{:S(2)}) collective-permute-start(bf16[256,128]{1,0:T(8,128)(2,1)S(1)} %copy-done.15), channel_id=1, source_target_pairs={{16,32},{48,64},{80,96},{112,128},{144,160},{176,192},{208,224},{3... | collective-permute-start | bytes 196616 | tf_op jit(solution)/shard_map/ppermute | solution.py:506
  124.8 6.5 %copy-start.11 = (bf16[256,128]{1,0:T(8,128)(2,1)}, bf16[256,128]{1,0:T(8,128)(2,1)S(1)}, u32[]{:S(2)}) copy-start(bf16[256,128]{1,0:T(8,128)(2,1)S(1)} %collective-permute-done.9._.chip_hbm) | copy-start | bytes 196612
  131.3 4.0 %collective-permute-start.11 = (bf16[2048,128]{1,0:T(8,128)(2,1)S(1)}, bf16[2048,128]{1,0:T(8,128)(2,1)S(1)}, u32[]{:S(2)}, u32[]{:S(2)}) collective-permute-start(bf16[2048,128]{1,0:T(8,128)(2,1)S(1)} %bitcast.9), channel_id=1, source_target_pairs={{0,16},{16,0},{1,17},{17,1},{2,18},{18,2},{3,19},{19,3},{4,20},{20... | collective-permute-start | bytes 1572872 | tf_op jit(solution)/shard_map/ppermute | solution.py:497
  (3 other events, 7.7 us)

commit v4 on v3

--- a/solution.py
+++ b/solution.py
@@ -188,10 +188,12 @@
         place = jnp.full((1, B), grid_row + s + grid_col, jnp.int32).astype(F32)
         drift = 1.0 + 2.0 * place / (GR + GC - 2)
         depth = 0.5 + 0.25 * snow[s].astype(F32)
-        columns.append([jnp.transpose(jnp.broadcast_to(row, (K, B))) for row in (depth, drift)])
+        present = (iota((1, B), 1) & (E - 1)) < sizes[s]
+        scale = jnp.where(present, depth * drift, 0.0)
+        columns.append(jnp.transpose(jnp.broadcast_to(scale, (K, B))))
     load.wait()
     for s in range(2):
-        resv[s] = press[s, 0].astype(F32) * columns[s][0] * columns[s][1] * masks[s]
+        resv[s] = press[s, 0].astype(F32) * columns[s]
         copies.send(resv.at[s], res.at[s])
     for s in range(2):
         dirs[s].wait()
@@ -324,6 +326,14 @@
     copies.finish()
 
 
+def preload_kernel(_, *refs):
+    count = len(refs) // 2
+    copies = Copies(refs[-1])
+    for source, target in zip(refs[:count], refs[count:-1]):
+        copies.send(source, target)
+    copies.finish()
+
+
 def tie_kernel(source, _, __, target):
     pass
 
@@ -374,45 +384,34 @@
     return chip[:, K:], far[:, K:], near[:, :, K:], other[:, :, K:]
 
 
-def second_kernel(sizes, sol_own, sol_other, inter_hbm, gram_hbm, chip_hbm, far_hbm, near_hbm, other_hbm,
+def second_kernel(sizes, sol_own, sol_other, inter, gram, chip, far, near, other,
                   res_hbm, dir_hbm, fac_hbm, half_hbm,
                   jump0, prod, half, pay,
-                  inter, gram, chip, far, near, other, res, dbuf, lbuf, corner, jumpv, prodv, halfv, block, sem):
+                  res, dbuf, lbuf, corner, jumpv, prodv, halfv, block, sem):
     copies = Copies(sem)
     edges = (chip, far, near, other)
-    loads = [copies.fetch(gram_hbm, gram)]
-    loads += [copies.fetch(a, b) for a, b in zip((chip_hbm, far_hbm, near_hbm, other_hbm), edges)]
-    loads.append(copies.fetch(inter_hbm, inter))
-    res_in = copies.fetch(res_hbm, res)
     dirs = [copies.fetch(dir_hbm.at[s, 0], dbuf.at[s]) for s in range(2)]
     facs = [fetch_lower(copies, fac_hbm.at[s, 0], lbuf.at[s]) for s in range(2)]
     corner_in = copies.fetch(half_hbm.at[:, pl.ds(K, CORN), :], corner)
-    for load in loads:
-        load.wait()
+    res_in = copies.fetch(res_hbm, res)
     jumped = jumps(sizes, sol_own, sol_other, inter, gram, edges, edge_grams(*edges))
-    res_in.wait()
-    cross = jnp.zeros((1, K), F32)
-    energy = jnp.zeros((1, K), F32)
     for s in range(2):
         jumpv[s] = jumped[s]
         copies.send(jumpv.at[s], jump0.at[s])
-        cross += jnp.sum(res[s] * jumped[s], axis=0, keepdims=True)
-        energy += jnp.sum(jumped[s] * jumped[s], axis=0, keepdims=True)
     for s in range(2):
         dirs[s].wait()
-        wide = dot(dbuf[s], jnp.concatenate(split2(jumpv[s]), axis=1))
-        prodv[s] = active_mask(sizes[s]) * (wide[:, :K] + wide[:, K:])
+        prodv[s] = active_mask(sizes[s]) * dot(dbuf[s], jumpv[s].astype(BF16))
         copies.send(prodv.at[s], prod.at[s])
     corner_in.wait()
     corners = []
     for s in range(2):
-        left = jnp.concatenate(split2(jnp.transpose(prodv[s])), axis=0)
-        wide = times_lower_turned(left, lbuf.at[s], facs[s])
-        turned = jnp.concatenate(split2(wide[:K] + wide[K:]), axis=0)
+        turned = times_lower_turned(jnp.transpose(prodv[s]).astype(BF16), lbuf.at[s], facs[s]).astype(BF16)
         halfv[s] = turned
         copies.send(halfv.at[s], half.at[s])
-        rows = dot_turned(corner[s], turned)
-        corners.append(corner_mask(sizes[s]) * (rows[:, :K] + rows[:, K:]))
+        corners.append(corner_mask(sizes[s]) * dot_turned(corner[s], turned))
+    res_in.wait()
+    cross = sum(jnp.sum(res[s] * jumpv[s], axis=0, keepdims=True) for s in range(2))
+    energy = sum(jnp.sum(jumpv[s] * jumpv[s], axis=0, keepdims=True) for s in range(2))
     rows = [jnp.zeros((1, K), F32)] * 2 + list(split3(cross)) + list(split3(energy))
     send_payload(copies, pay, block, corners, rows_of((16, K), rows))
     copies.finish()
@@ -429,30 +428,20 @@
         halves_in[s].wait()
         for load in facs[s]:
             load.wait()
-        wide = times_lower(half.at[s], lbuf.at[s])
-        interv[s] = active_mask(sizes[s]) * jnp.transpose(wide[:K] + wide[K:])
+        interv[s] = active_mask(sizes[s]) * jnp.transpose(times_lower(half.at[s], lbuf.at[s]))
         copies.send(interv.at[s], inter.at[s])
     send_edges(copies, (e0, e1, e2, e3), (chip, far, near, other), interv, None)
     copies.finish()
 
 
-def third_kernel(sizes, sol_own, sol_other, stats, inter_hbm, gram_hbm, chip_hbm, far_hbm, near_hbm, other_hbm,
+def third_kernel(sizes, sol_own, sol_other, stats, inter, gram, chip, far, near, other,
                  old_chip, old_far, old_near, old_other, res_hbm, jump_hbm,
-                 res1, jump1, pay,
-                 inter, gram, chip, far, near, other, gchip, gfar, gnear, gother, res, jump0, sem):
+                 res1, jump1, pay, res, jump0, sem):
     copies = Copies(sem)
     edges = (chip, far, near, other)
-    grams = (gchip, gfar, gnear, gother)
-    width = pl.ds(K, K)
-    loads = [copies.fetch(gram_hbm, gram)]
-    loads += [copies.fetch(a.at[:, width], b) for a, b in zip((old_chip, old_far), grams[:2])]
-    loads += [copies.fetch(a.at[:, :, width], b) for a, b in zip((old_near, old_other), grams[2:])]
-    loads += [copies.fetch(a, b) for a, b in zip((chip_hbm, far_hbm, near_hbm, other_hbm), edges)]
-    loads.append(copies.fetch(inter_hbm, inter))
     late = [copies.fetch(res_hbm, res), copies.fetch(jump_hbm, jump0)]
-    for load in loads:
-        load.wait()
-    again = jumps(sizes, sol_own, sol_other, inter, gram, edges, tuple(g[...] for g in grams))
+    grams = edge_grams(old_chip, old_far, old_near, old_other)
+    again = jumps(sizes, sol_own, sol_other, inter, gram, edges, grams)
     for load in late:
         load.wait()
     step = stats[0:1] / (stats[1:2] + 1e-06)
@@ -509,7 +498,7 @@
     )
 
 
-def coarse_solution(own, snd, arrived):
+def coarse_solution(own, snd, arrived, needed):
     pay3 = ((ZS, HALF + 16, K), BF16)
     rcv = swap(snd)
     (pay,) = call(pair_sum_kernel, [pay3], [VM] * 2, [HB], [(pay3[0][1:], BF16), sems(ZS)])(own, rcv)
@@ -523,15 +512,17 @@
     )(rec, *arrived[2:])
     sol = all_to_all(pay, ("x", "y"))
     (sol,) = call(tie_kernel, [((SY, HALF, K), BF16)], [AN] + [HB] * 2, [AN], aliases={0: 0})(sol, *arrived[:2])
+    kinds = [(a.shape, a.dtype) for a in needed]
+    needed = call(preload_kernel, kinds, [AN] + [HB] * len(kinds), [VM] * len(kinds), [sems(len(kinds))])(sol, *needed)
     sol = sol.reshape(SY * HALF, K)
-    return sol, swap(sol), stats
+    return sol, swap(sol), stats, needed
 
 
 def local(factor, pre, coarse_inv, sizes, cmap, snow_level, pressure):
     sizes = sizes.reshape(2)
     whole = ((2, B, K), F32)
     gramed = ((2, B, K), BF16)
-    halved = ((2, 2 * K, B), BF16)
+    halved = ((2, K, B), BF16)
     cornered = ((2, K + CORN, B), BF16)
     square = ((2, B, B), BF16)
     payload = ((SY, ROWS, K), BF16)
@@ -566,14 +557,14 @@
         [VM, VM, HB],
         [((E, NC), BF16), ((E, B), BF16), ((NC, B), BF16), sems(2)],
     )(rec, coarse_inv, gram)
-    sol_own, sol_other, _ = coarse_solution(own, snd, arrived)
+    sol_own, sol_other, _, needed = coarse_solution(own, snd, arrived, [inter, gram, *arrived])
     jump0, prod, half1, pay = call(
         second_kernel,
         [whole, whole, halved, payload],
-        [SM, VM, VM] + [HB] * 10,
+        [SM] + [VM] * 8 + [HB] * 4,
         [HB] * 4,
-        [whole, gramed] + wide + [whole, square, square, ((2, CORN, B), BF16), whole, whole, halved, block, sems(24 + SY)],
-    )(sizes, sol_own, sol_other, inter, gram, *arrived, res, pre, factor, half)
+        [whole, square, square, ((2, CORN, B), BF16), whole, whole, halved, block, sems(24 + SY)],
+    )(sizes, sol_own, sol_other, *needed, res, pre, factor, half)
     rec = all_to_all(pay, ("x", "y"))
     slim = edges_of(K)
     inter1, *edges = call(
@@ -585,14 +576,14 @@
     )(sizes, half1, factor)
     arrived1 = exchange(*edges)
     own, snd = call(coarse_next_kernel, sent, [VM] * 2 + [HB], [VM] * 2)(rec, picked_inv, inter1)
-    sol_own, sol_other, stats = coarse_solution(own, snd, arrived1)
+    sol_own, sol_other, stats, needed = coarse_solution(own, snd, arrived1, [inter1, gram, *arrived1, *arrived])
     res1, jump1, pay = call(
         third_kernel,
         [whole] * 2 + [((CS * YS, 8, K), F32)],
-        [SM] + [VM] * 3 + [HB] * 12,
+        [SM] + [VM] * 13 + [HB] * 2,
         [VM] * 3,
-        [whole, gramed] + slim + edges_of(K) + [whole, whole, sems(12)],
-    )(sizes, sol_own, sol_other, stats, inter1, gram, *arrived1, *arrived, res, jump0)
+        [whole, whole, sems(2)],
+    )(sizes, sol_own, sol_other, stats, *needed, res, jump0)
     rec = all_to_all(pay, ("core", "y"))
     (pay,) = call(partial_kernel, [((ZS * XS, 8, K), F32)], [VM], [VM])(rec)
     rec = all_to_all(pay, ("z", "x"))

time: 164 us -> 162 us (0.988)
  waiting for transfers between devices: 45.7 us -> 42.7 us
    ppermute x4, waiting for transfers between devices: 4.89 us -> 1.82 us  [swap(): return lax.ppermute(value, 'core', [(0, 1), (1, 0)])]
    pallas_call x15 -> x17, Pallas kernels: 39.7 us -> 40.7 us  [placed(): run(*[pltpu.with_memory_space_constraint(a, pltpu.HBM) if spec is HB else...]
  transfers between devices with their start and end apart: 18 -> 18, of which waited for: 14 -> 12; matrix products, arithmetic and copies ran while one was open for 0% -> 0% of each run, Pallas kernels for 6% -> 8%
where the time goes in v4:
time: 162 us; the launch traced here: 161 us
  starting transfers between devices  54.5 us (34%)
  waiting for transfers between devices  42.7 us (26%)
  Pallas kernels  40.7 us (25%)
  blocking collectives  22.2 us (14%)
    pallas_call x17, Pallas kernels, placed(): run(*[pltpu.with_memory_space_constraint(a, pltpu.HBM) if spec is HB else...  40.7 us
    all_to_all x6, starting transfers between devices, all_to_all(): return lax.all_to_all(value, axes, split_axis=0, concat_axis=0)  34.1 us
    all_to_all x6, waiting for transfers between devices, all_to_all(): return lax.all_to_all(value, axes, split_axis=0, concat_axis=0)  23.3 us
    all_to_all x2, blocking collectives, all_to_all(): return lax.all_to_all(value, axes, split_axis=0, concat_axis=0)  22.2 us
    ppermute x4, starting transfers between devices, swap(): return lax.ppermute(value, 'core', [(0, 1), (1, 0)])  10.6 us
    ppermute x2, waiting for transfers between devices, exchange(): lax.ppermute(near, cols, even)  10.5 us
    ppermute x2, waiting for transfers between devices, exchange(): lax.ppermute(far, rows, odd)  7.01 us
    ppermute x2, starting transfers between devices, exchange(): lax.ppermute(far, rows, odd)  5.37 us
  transfers between devices with their start and end apart: 18, of which 12 were waited for; matrix products, arithmetic and copies ran while one was open for 0% of the time, Pallas kernels for 8%

profile of v4, /device:TPU:1, one launch (start us, length us, event | category | flops | bytes accessed | tf_op | source)
XLA Modules:
  0.0 161.3 jit_solution(15681834083033343317)
XLA Ops:
  0.7 6.8 %shard_map.86 = (f32[2,1024,128]{2,1,0:T(8,128)}, f32[2,1024,128]{2,1,0:T(8,128)}, bf16[2,160,1024]{2,1,0:T(8,128)(2,1)}, bf16[16,80,128]{2,1,0:T(8,128)(2,1)}) custom-call(s32[2]{0:T(128)} %bitcast.13, s32[2,1,1024]{2,1,0:T(1,128)} %snow_hbm.1, s32[2,1,32]{2,1,0:T(1,128)} %cmap.1, bf16[2,1,1024,128]{3,2,1,0:T(8,128)(2,1)} %press_hbm.1, ...), custom_call_target="tpu_custom_call" | custom-call | tf_op jit(solution)/shard_map/pallas_call | solution.py:57
  7.5 7.6 %all-to-all-start = ((bf16[16,80,128]{2,1,0:T(8,128)(2,1)}), bf16[16,80,128]{2,1,0:T(8,128)(2,1)S(1)}, u32[]{:S(2)}, u32[]{:S(2)}) async-start(bf16[16,80,128]{2,1,0:T(8,128)(2,1)} %get-tuple-element.50), calls=%async_computation | async-start | bytes 655360 | tf_op jit(solution)/shard_map/all_to_all | solution.py:482
  15.1 4.7 %shard_map.87 = (f32[2,1024,128]{2,1,0:T(8,128)}, bf16[2,1024,128]{2,1,0:T(8,128)(2,1)}, bf16[256,256]{1,0:T(8,128)(2,1)}, bf16[256,256]{1,0:T(8,128)(2,1)}, bf1...) custom-call(s32[2]{0:T(128)S(1)} %bitcast.14, s32[2,1,32]{2,1,0:T(1,128)S(1)} %copy-done.4, ...), custom_call_target="tpu_custom_call" | custom-call | tf_op jit(solution)/shard_map/pallas_call | solution.py:57
  19.9 3.0 %all-to-all-done.rec = bf16[16,80,128]{2,1,0:T(8,128)(2,1)S(1)} async-done(((bf16[16,80,128]{2,1,0:T(8,128)(2,1)}), bf16[16,80,128]{2,1,0:T(8,128)(2,1)S(1)}, u32[]{:S(2)}, u32[]{:S(2)}) %all-to-all-start) | async-done | bytes 327712 | tf_op jit(solution)/shard_map/all_to_all | solution.py:482
  22.9 4.7 %shard_map.88 = (f32[136,128]{1,0:T(8,128)S(1)}, f32[136,128]{1,0:T(8,128)S(1)}, bf16[256,1024]{1,0:T(8,128)(2,1)}) custom-call(bf16[16,80,128]{2,1,0:T(8,128)(2,1)S(1)} %all-to-all-done.rec, bf16[256,4096]{1,0:T(8,128)(2,1)} %coarse_hbm.1, bf16[2,1024,128]{2,1,0:T(8,128)(2,1)} %get-tuple-element.52._.refs_1_), custom_call_target="tpu_custom_call" | custom-call | tf_op jit(solution)/shard_map/pallas_call | solution.py:57
  27.7 2.4 %collective-permute-start = (f32[136,128]{1,0:T(8,128)S(1)}, f32[136,128]{1,0:T(8,128)S(1)}, u32[]{:S(2)}, u32[]{:S(2)}) collective-permute-start(f32[136,128]{1,0:T(8,128)S(1)} %get-tuple-element.54), channel_id=1, source_target_pairs={{0,16},{16,0},{1,17},{17,1},{2,18},{18,2},{3,19},{19,3},{4,20},{20... | collective-permute-start | bytes 208904 | tf_op jit(solution)/shard_map/ppermute | solution.py:486
  31.8 8.2 %all-to-all-start.1 = ((bf16[8,144,128]{2,1,0:T(8,128)(2,1)}), bf16[8,144,128]{2,1,0:T(8,128)(2,1)S(1)}, u32[]{:S(2)}, u32[]{:S(2)}) async-start(bf16[8,144,128]{2,1,0:T(8,128)(2,1)} %shard_map.89), calls=%async_computation.1 | async-start | bytes 589824 | tf_op jit(solution)/shard_map/all_to_all | solution.py:482
  40.8 6.6 %collective-permute-done.1._.refs_4_.refs_8_ = bf16[2,256,256]{2,1,0:T(8,128)(2,1)S(1)} collective-permute-done((bf16[2,256,256]{2,1,0:T(8,128)(2,1)}, bf16[2,256,256]{2,1,0:T(8,128)(2,1)S(1)}, u32[]{:S(2)}, u32[]{:S(2)}) %collective-permute-start.1) | collective-permute-done | bytes 262176 | tf_op jit(solution)/shard_map/ppermute | solution.py:496
  47.4 5.0 %all-to-all-done.1.rec = bf16[8,144,128]{2,1,0:T(8,128)(2,1)S(1)} async-done(((bf16[8,144,128]{2,1,0:T(8,128)(2,1)}), bf16[8,144,128]{2,1,0:T(8,128)(2,1)S(1)}, u32[]{:S(2)}, u32[]{:S(2)}) %all-to-all-start.1) | async-done | bytes 294944 | tf_op jit(solution)/shard_map/all_to_all | solution.py:482
  54.0 3.6 %all-to-all-start.2 = ((bf16[16,128,128]{2,1,0:T(8,128)(2,1)}), bf16[16,128,128]{2,1,0:T(8,128)(2,1)S(1)}, u32[]{:S(2)}, u32[]{:S(2)}) async-start(bf16[16,128,128]{2,1,0:T(8,128)(2,1)} %get-tuple-element.57), calls=%async_computation.2 | async-start | bytes 1048576 | tf_op jit(solution)/shard_map/all_to_all | solution.py:482
  57.6 1.6 %collective-permute-start.3 = (bf16[256,256]{1,0:T(8,128)(2,1)S(1)}, bf16[256,256]{1,0:T(8,128)(2,1)S(1)}, u32[]{:S(2)}, u32[]{:S(2)}) collective-permute-start(bf16[256,256]{1,0:T(8,128)(2,1)S(1)} %copy-done.14), channel_id=1, source_target_pairs={{0,16},{16,0},{32,48},{48,32},{64,80},{80,64},{96,112},{112,96},{1... | collective-permute-start | bytes 393224 | tf_op jit(solution)/shard_map/ppermute | solution.py:494
  59.3 3.3 %collective-permute-start.4 = (bf16[256,256]{1,0:T(8,128)(2,1)S(1)}, bf16[256,256]{1,0:T(8,128)(2,1)S(1)}, u32[]{:S(2)}, u32[]{:S(2)}) collective-permute-start(bf16[256,256]{1,0:T(8,128)(2,1)S(1)} %copy-done.13), channel_id=1, source_target_pairs={{16,32},{48,64},{80,96},{112,128},{144,160},{176,192},{208,224},{3... | collective-permute-start | bytes 393224 | tf_op jit(solution)/shard_map/ppermute | solution.py:495
  62.6 3.3 %collective-permute-done.4.__.refs_3_.refs_7_ = bf16[256,256]{1,0:T(8,128)(2,1)S(1)} collective-permute-done((bf16[256,256]{1,0:T(8,128)(2,1)S(1)}, bf16[256,256]{1,0:T(8,128)(2,1)S(1)}, u32[]{:S(2)}, u32[]{:S(2)}) %collective-permute-start.4) | collective-permute-done | bytes 131104 | tf_op jit(solution)/shard_map/ppermute | solution.py:495
  66.7 3.4 %collective-permute-start.5 = (bf16[2048,128]{1,0:T(8,128)(2,1)S(1)}, bf16[2048,128]{1,0:T(8,128)(2,1)S(1)}, u32[]{:S(2)}, u32[]{:S(2)}) collective-permute-start(bf16[2048,128]{1,0:T(8,128)(2,1)S(1)} %bitcast.11), channel_id=1, source_target_pairs={{0,16},{16,0},{1,17},{17,1},{2,18},{18,2},{3,19},{19,3},{4,20},{20... | collective-permute-start | bytes 1572872 | tf_op jit(solution)/shard_map/ppermute | solution.py:486
  70.0 1.6 %shard_map.92 = (f32[2,1024,128]{2,1,0:T(8,128)S(1)}, bf16[2,1024,128]{2,1,0:T(8,128)(2,1)S(1)}, bf16[256,256]{1,0:T(8,128)(2,1)S(1)}, bf16[256,256]{1,0:T(8,128...) custom-call(bf16[16,128,128]{2,1,0:T(8,128)(2,1)S(1)} %shard_map.91._, ...), custom_call_target="tpu_custom_call" | custom-call | tf_op jit(solution)/shard_map/pallas_call | solution.py:57
  71.7 7.6 %shard_map.93 = (f32[2,1024,128]{2,1,0:T(8,128)}, f32[2,1024,128]{2,1,0:T(8,128)}, bf16[2,128,1024]{2,1,0:T(8,128)(2,1)}, bf16[16,80,128]{2,1,0:T(8,128)(2,1)}) custom-call(s32[2]{0:T(128)S(1)} %bitcast.15, bf16[2048,128]{1,0:T(8,128)(2,1)S(1)} %bitcast.12, bf16[2048,128]{1,0:T(8,128)(2,1)S(1)} %collective-permute-done.5.sol_other, ...), custom_call_target="tpu_custom_call" | custom-call | tf_op jit(solution)/shard_map/pallas_call | solution.py:57
  79.3 3.8 %all-to-all-start.3 = ((bf16[16,80,128]{2,1,0:T(8,128)(2,1)}), bf16[16,80,128]{2,1,0:T(8,128)(2,1)S(1)}, u32[]{:S(2)}, u32[]{:S(2)}) async-start(bf16[16,80,128]{2,1,0:T(8,128)(2,1)} %get-tuple-element.68), calls=%async_computation.3 | async-start | bytes 655360 | tf_op jit(solution)/shard_map/all_to_all | solution.py:482
  83.1 4.0 %shard_map.94 = (f32[2,1024,128]{2,1,0:T(8,128)}, bf16[256,128]{1,0:T(8,128)(2,1)}, bf16[256,128]{1,0:T(8,128)(2,1)}, bf16[2,256,128]{2,1,0:T(8,128)(2,1)}, bf16[2,256,128]{2,1,0:T(8,128)(2,1)}) custom-call(s32[2]{0:T(128)S(1)} %bitcast.16, bf16[2,128,1024]{2,1,0:T(8,128)(2,1)} %get-tuple-element.70.half_hbm, bf16[2,1,1024,1024]{3,2,1,0:T(8,128)(2,1)} %fac_hbm.7), custom_call_target="tpu_custom_call" | custom-call | tf_op jit(solution)/shard_map/pallas_call | solution.py:57
  87.1 3.9 %all-to-all-done.3.rec = bf16[16,80,128]{2,1,0:T(8,128)(2,1)S(1)} async-done(((bf16[16,80,128]{2,1,0:T(8,128)(2,1)}), bf16[16,80,128]{2,1,0:T(8,128)(2,1)S(1)}, u32[]{:S(2)}, u32[]{:S(2)}) %all-to-all-start.3) | async-done | bytes 327712 | tf_op jit(solution)/shard_map/all_to_all | solution.py:482
  91.4 2.2 %collective-permute-start.6 = (f32[136,128]{1,0:T(8,128)S(1)}, f32[136,128]{1,0:T(8,128)S(1)}, u32[]{:S(2)}, u32[]{:S(2)}) collective-permute-start(f32[136,128]{1,0:T(8,128)S(1)} %get-tuple-element.73), channel_id=1, source_target_pairs={{0,16},{16,0},{1,17},{17,1},{2,18},{18,2},{3,19},{19,3},{4,20},{20... | collective-permute-start | bytes 208904 | tf_op jit(solution)/shard_map/ppermute | solution.py:486
  95.3 7.4 %all-to-all-start.4 = ((bf16[8,144,128]{2,1,0:T(8,128)(2,1)}), bf16[8,144,128]{2,1,0:T(8,128)(2,1)S(1)}, u32[]{:S(2)}, u32[]{:S(2)}) async-start(bf16[8,144,128]{2,1,0:T(8,128)(2,1)} %shard_map.96), calls=%async_computation.4 | async-start | bytes 589824 | tf_op jit(solution)/shard_map/all_to_all | solution.py:482
  103.4 3.9 %collective-permute-done.7._.refs_4_ = bf16[2,256,128]{2,1,0:T(8,128)(2,1)S(1)} collective-permute-done((bf16[2,256,128]{2,1,0:T(8,128)(2,1)}, bf16[2,256,128]{2,1,0:T(8,128)(2,1)S(1)}, u32[]{:S(2)}, u32[]{:S(2)}) %collective-permute-start.7) | collective-permute-done | bytes 131104 | tf_op jit(solution)/shard_map/ppermute | solution.py:496
  107.3 7.8 %all-to-all-done.4.rec = bf16[8,144,128]{2,1,0:T(8,128)(2,1)S(1)} async-done(((bf16[8,144,128]{2,1,0:T(8,128)(2,1)}), bf16[8,144,128]{2,1,0:T(8,128)(2,1)S(1)}, u32[]{:S(2)}, u32[]{:S(2)}) %all-to-all-start.4) | async-done | bytes 294944 | tf_op jit(solution)/shard_map/all_to_all | solution.py:482
  116.1 3.6 %all-to-all-start.5 = ((bf16[16,128,128]{2,1,0:T(8,128)(2,1)}), bf16[16,128,128]{2,1,0:T(8,128)(2,1)S(1)}, u32[]{:S(2)}, u32[]{:S(2)}) async-start(bf16[16,128,128]{2,1,0:T(8,128)(2,1)} %get-tuple-element.76), calls=%async_computation.5 | async-start | bytes 1048576 | tf_op jit(solution)/shard_map/all_to_all | solution.py:482
  121.0 2.1 %collective-permute-start.10 = (bf16[256,128]{1,0:T(8,128)(2,1)S(1)}, bf16[256,128]{1,0:T(8,128)(2,1)S(1)}, u32[]{:S(2)}, u32[]{:S(2)}) collective-permute-start(bf16[256,128]{1,0:T(8,128)(2,1)S(1)} %copy-done.15), channel_id=1, source_target_pairs={{16,32},{48,64},{80,96},{112,128},{144,160},{176,192},{208,224},{3... | collective-permute-start | bytes 196616 | tf_op jit(solution)/shard_map/ppermute | solution.py:495
  123.2 3.7 %collective-permute-done.10.__.refs_3_ = bf16[256,128]{1,0:T(8,128)(2,1)S(1)} collective-permute-done((bf16[256,128]{1,0:T(8,128)(2,1)S(1)}, bf16[256,128]{1,0:T(8,128)(2,1)S(1)}, u32[]{:S(2)}, u32[]{:S(2)}) %collective-permute-start.10) | collective-permute-done | bytes 65568 | tf_op jit(solution)/shard_map/ppermute | solution.py:495
  126.9 2.7 %all-to-all-done.5.source = bf16[16,128,128]{2,1,0:T(8,128)(2,1)S(1)} async-done(((bf16[16,128,128]{2,1,0:T(8,128)(2,1)}), bf16[16,128,128]{2,1,0:T(8,128)(2,1)S(1)}, u32[]{:S(2)}, u32[]{:S(2)}) %all-to-all-start.5) | async-done | bytes 524320 | tf_op jit(solution)/shard_map/all_to_all | solution.py:482
  129.7 2.6 %collective-permute-start.11 = (bf16[2048,128]{1,0:T(8,128)(2,1)S(1)}, bf16[2048,128]{1,0:T(8,128)(2,1)S(1)}, u32[]{:S(2)}, u32[]{:S(2)}) collective-permute-start(bf16[2048,128]{1,0:T(8,128)(2,1)S(1)} %bitcast.9), channel_id=1, source_target_pairs={{0,16},{16,0},{1,17},{17,1},{2,18},{18,2},{3,19},{19,3},{4,20},{20... | collective-permute-start | bytes 1572872 | tf_op jit(solution)/shard_map/ppermute | solution.py:486
  132.3 1.8 %shard_map.99 = (f32[2,1024,128]{2,1,0:T(8,128)S(1)}, bf16[2,1024,128]{2,1,0:T(8,128)(2,1)S(1)}, bf16[256,128]{1,0:T(8,128)(2,1)S(1)}, bf16[256,128]{1,0:T(8,128...) custom-call(bf16[16,128,128]{2,1,0:T(8,128)(2,1)S(1)} %shard_map.98., ...), custom_call_target="tpu_custom_call" | custom-call | tf_op jit(solution)/shard_map/pallas_call | solution.py:57
  134.1 3.4 %shard_map.100 = (f32[2,1024,128]{2,1,0:T(8,128)S(1)}, f32[2,1024,128]{2,1,0:T(8,128)S(1)}, f32[8,8,128]{2,1,0:T(8,128)S(1)}) custom-call(s32[2]{0:T(128)S(1)} %bitcast.17, bf16[2048,128]{1,0:T(8,128)(2,1)S(1)} %bitcast.10, bf16[2048,128]{1,0:T(8,128)(2,1)S(1)} %collective-permute-done.11.sol_other, f32[8,128]{1,0:T(8,128)S(1)} %get-tuple-element.79.stats, ...), custom_call_target="tpu_custom_call" | custom-call | tf_op jit(solution)/shard_map/pallas_call | solution.py:57
  137.5 7.4 %all_to_all.40.rec = f32[8,8,128]{2,1,0:T(8,128)S(1)} all-to-all(f32[8,8,128]{2,1,0:T(8,128)S(1)} %get-tuple-element.91), channel_id=1, replica_groups=mesh['z'=8,'core'=2,'x'=4,'y'=4] {'core','y'}, dimensions={0} | all-to-all | bytes 65536 | tf_op jit(solution)/shard_map/all_to_all | solution.py:482
  144.9 14.8 %all_to_all.41.rec = f32[32,8,128]{2,1,0:T(8,128)S(1)} all-to-all(f32[32,8,128]{2,1,0:T(8,128)S(1)} %shard_map.101), channel_id=1, replica_groups=mesh['z'=8,'core'=2,'x'=4,'y'=4] {'z','x'}, dimensions={0} | all-to-all | bytes 262144 | tf_op jit(solution)/shard_map/all_to_all | solution.py:482
  (57 shorter events, 11.5 us)
Async XLA Ops:
  0.6 14.5 %copy-start.3 = (s32[2,1]{0,1:T(1,128)S(1)}, s32[2,1]{0,1:T(1,128)}, u32[]{:S(2)}) copy-start(s32[2,1]{0,1:T(1,128)} %param.10) | copy-start | bytes 28
  0.6 14.5 %copy-start.4 = (s32[2,1,32]{2,1,0:T(1,128)S(1)}, s32[2,1,32]{2,1,0:T(1,128)}, u32[]{:S(2)}) copy-start(s32[2,1,32]{2,1,0:T(1,128)} %cmap.1) | copy-start | bytes 772
  7.5 15.4 %all-to-all-start = ((bf16[16,80,128]{2,1,0:T(8,128)(2,1)}), bf16[16,80,128]{2,1,0:T(8,128)(2,1)S(1)}, u32[]{:S(2)}, u32[]{:S(2)}) async-start(bf16[16,80,128]{2,1,0:T(8,128)(2,1)} %get-tuple-element.50), calls=%async_computation | async-start | bytes 655360 | tf_op jit(solution)/shard_map/all_to_all | solution.py:482
  19.9 37.8 %copy-start.14 = (bf16[256,256]{1,0:T(8,128)(2,1)S(1)}, bf16[256,256]{1,0:T(8,128)(2,1)}, u32[]{:S(2)}) copy-start(bf16[256,256]{1,0:T(8,128)(2,1)} %get-tuple-element.58) | copy-start | bytes 393220
  19.9 39.4 %copy-start.13 = (bf16[256,256]{1,0:T(8,128)(2,1)S(1)}, bf16[256,256]{1,0:T(8,128)(2,1)}, u32[]{:S(2)}) copy-start(bf16[256,256]{1,0:T(8,128)(2,1)} %get-tuple-element.59) | copy-start | bytes 393220
  27.7 3.3 %collective-permute-start = (f32[136,128]{1,0:T(8,128)S(1)}, f32[136,128]{1,0:T(8,128)S(1)}, u32[]{:S(2)}, u32[]{:S(2)}) collective-permute-start(f32[136,128]{1,0:T(8,128)S(1)} %get-tuple-element.54), channel_id=1, source_target_pairs={{0,16},{16,0},{1,17},{17,1},{2,18},{18,2},{3,19},{19,3},{4,20},{20... | collective-permute-start | bytes 208904 | tf_op jit(solution)/shard_map/ppermute | solution.py:486
  31.8 20.6 %all-to-all-start.1 = ((bf16[8,144,128]{2,1,0:T(8,128)(2,1)}), bf16[8,144,128]{2,1,0:T(8,128)(2,1)S(1)}, u32[]{:S(2)}, u32[]{:S(2)}) async-start(bf16[8,144,128]{2,1,0:T(8,128)(2,1)} %shard_map.89), calls=%async_computation.1 | async-start | bytes 589824 | tf_op jit(solution)/shard_map/all_to_all | solution.py:482
  40.0 7.4 %collective-permute-start.1 = (bf16[2,256,256]{2,1,0:T(8,128)(2,1)}, bf16[2,256,256]{2,1,0:T(8,128)(2,1)S(1)}, u32[]{:S(2)}, u32[]{:S(2)}) collective-permute-start(bf16[2,256,256]{2,1,0:T(8,128)(2,1)} %get-tuple-element.55), channel_id=1, source_target_pairs={{0,1},{1,0},{2,3},{3,2},{4,5},{5,4},{6,7},{7,6},{8,9},{9,8},{10,11... | collective-permute-start | bytes 786440 | tf_op jit(solution)/shard_map/ppermute | solution.py:496
  40.1 7.3 %collective-permute-start.2 = (bf16[2,256,256]{2,1,0:T(8,128)(2,1)}, bf16[2,256,256]{2,1,0:T(8,128)(2,1)S(1)}, u32[]{:S(2)}, u32[]{:S(2)}) collective-permute-start(bf16[2,256,256]{2,1,0:T(8,128)(2,1)} %get-tuple-element.56), channel_id=1, source_target_pairs={{1,2},{3,4},{5,6},{7,8},{9,10},{11,12},{13,14},{2,1},{4,3},{6,5},{... | collective-permute-start | bytes 786440 | tf_op jit(solution)/shard_map/ppermute | solution.py:497
  47.4 5.0 %copy-start.5 = (bf16[2,256,256]{2,1,0:T(8,128)(2,1)}, bf16[2,256,256]{2,1,0:T(8,128)(2,1)S(1)}, u32[]{:S(2)}) copy-start(bf16[2,256,256]{2,1,0:T(8,128)(2,1)S(1)} %collective-permute-done.1._.refs_4_.refs_8_) | copy-start | bytes 786436
  47.4 5.0 %copy-start.6 = (bf16[2,256,256]{2,1,0:T(8,128)(2,1)}, bf16[2,256,256]{2,1,0:T(8,128)(2,1)S(1)}, u32[]{:S(2)}) copy-start(bf16[2,256,256]{2,1,0:T(8,128)(2,1)S(1)} %collective-permute-done.2.__.refs_5_.refs_9_) | copy-start | bytes 786436
  54.0 12.6 %all-to-all-start.2 = ((bf16[16,128,128]{2,1,0:T(8,128)(2,1)}), bf16[16,128,128]{2,1,0:T(8,128)(2,1)S(1)}, u32[]{:S(2)}, u32[]{:S(2)}) async-start(bf16[16,128,128]{2,1,0:T(8,128)(2,1)} %get-tuple-element.57), calls=%async_computation.2 | async-start | bytes 1048576 | tf_op jit(solution)/shard_map/all_to_all | solution.py:482
  57.6 4.9 %collective-permute-start.3 = (bf16[256,256]{1,0:T(8,128)(2,1)S(1)}, bf16[256,256]{1,0:T(8,128)(2,1)S(1)}, u32[]{:S(2)}, u32[]{:S(2)}) collective-permute-start(bf16[256,256]{1,0:T(8,128)(2,1)S(1)} %copy-done.14), channel_id=1, source_target_pairs={{0,16},{16,0},{32,48},{48,32},{64,80},{80,64},{96,112},{112,96},{1... | collective-permute-start | bytes 393224 | tf_op jit(solution)/shard_map/ppermute | solution.py:494
  59.3 6.6 %collective-permute-start.4 = (bf16[256,256]{1,0:T(8,128)(2,1)S(1)}, bf16[256,256]{1,0:T(8,128)(2,1)S(1)}, u32[]{:S(2)}, u32[]{:S(2)}) collective-permute-start(bf16[256,256]{1,0:T(8,128)(2,1)S(1)} %copy-done.13), channel_id=1, source_target_pairs={{16,32},{48,64},{80,96},{112,128},{144,160},{176,192},{208,224},{3... | collective-permute-start | bytes 393224 | tf_op jit(solution)/shard_map/ppermute | solution.py:495
  66.7 5.0 %collective-permute-start.5 = (bf16[2048,128]{1,0:T(8,128)(2,1)S(1)}, bf16[2048,128]{1,0:T(8,128)(2,1)S(1)}, u32[]{:S(2)}, u32[]{:S(2)}) collective-permute-start(bf16[2048,128]{1,0:T(8,128)(2,1)S(1)} %bitcast.11), channel_id=1, source_target_pairs={{0,16},{16,0},{1,17},{17,1},{2,18},{18,2},{3,19},{19,3},{4,20},{20... | collective-permute-start | bytes 1572872 | tf_op jit(solution)/shard_map/ppermute | solution.py:486
  79.3 11.8 %copy-start.2 = (bf16[256,1024]{1,0:T(8,128)(2,1)S(1)}, bf16[256,1024]{1,0:T(8,128)(2,1)}, u32[]{:S(2)}) copy-start(bf16[256,1024]{1,0:T(8,128)(2,1)} %get-tuple-element.69.picked_inv) | copy-start | bytes 1572868
  79.3 11.8 %all-to-all-start.3 = ((bf16[16,80,128]{2,1,0:T(8,128)(2,1)}), bf16[16,80,128]{2,1,0:T(8,128)(2,1)S(1)}, u32[]{:S(2)}, u32[]{:S(2)}) async-start(bf16[16,80,128]{2,1,0:T(8,128)(2,1)} %get-tuple-element.68), calls=%async_computation.3 | async-start | bytes 655360 | tf_op jit(solution)/shard_map/all_to_all | solution.py:482
  87.1 32.6 %copy-start.16 = (bf16[256,128]{1,0:T(8,128)(2,1)S(1)}, bf16[256,128]{1,0:T(8,128)(2,1)}, u32[]{:S(2)}) copy-start(bf16[256,128]{1,0:T(8,128)(2,1)} %get-tuple-element.77) | copy-start | bytes 196612
  87.1 33.9 %copy-start.15 = (bf16[256,128]{1,0:T(8,128)(2,1)S(1)}, bf16[256,128]{1,0:T(8,128)(2,1)}, u32[]{:S(2)}) copy-start(bf16[256,128]{1,0:T(8,128)(2,1)} %get-tuple-element.78) | copy-start | bytes 196612
  91.4 3.1 %collective-permute-start.6 = (f32[136,128]{1,0:T(8,128)S(1)}, f32[136,128]{1,0:T(8,128)S(1)}, u32[]{:S(2)}, u32[]{:S(2)}) collective-permute-start(f32[136,128]{1,0:T(8,128)S(1)} %get-tuple-element.73), channel_id=1, source_target_pairs={{0,16},{16,0},{1,17},{17,1},{2,18},{18,2},{3,19},{19,3},{4,20},{20... | collective-permute-start | bytes 208904 | tf_op jit(solution)/shard_map/ppermute | solution.py:486
  95.3 19.8 %all-to-all-start.4 = ((bf16[8,144,128]{2,1,0:T(8,128)(2,1)}), bf16[8,144,128]{2,1,0:T(8,128)(2,1)S(1)}, u32[]{:S(2)}, u32[]{:S(2)}) async-start(bf16[8,144,128]{2,1,0:T(8,128)(2,1)} %shard_map.96), calls=%async_computation.4 | async-start | bytes 589824 | tf_op jit(solution)/shard_map/all_to_all | solution.py:482
  102.7 4.6 %collective-permute-start.7 = (bf16[2,256,128]{2,1,0:T(8,128)(2,1)}, bf16[2,256,128]{2,1,0:T(8,128)(2,1)S(1)}, u32[]{:S(2)}, u32[]{:S(2)}) collective-permute-start(bf16[2,256,128]{2,1,0:T(8,128)(2,1)} %get-tuple-element.74), channel_id=1, source_target_pairs={{0,1},{1,0},{2,3},{3,2},{4,5},{5,4},{6,7},{7,6},{8,9},{9,8},{10,11... | collective-permute-start | bytes 393224 | tf_op jit(solution)/shard_map/ppermute | solution.py:496
  102.8 4.6 %collective-permute-start.8 = (bf16[2,256,128]{2,1,0:T(8,128)(2,1)}, bf16[2,256,128]{2,1,0:T(8,128)(2,1)S(1)}, u32[]{:S(2)}, u32[]{:S(2)}) collective-permute-start(bf16[2,256,128]{2,1,0:T(8,128)(2,1)} %get-tuple-element.75), channel_id=1, source_target_pairs={{1,2},{3,4},{5,6},{7,8},{9,10},{11,12},{13,14},{2,1},{4,3},{6,5},{... | collective-permute-start | bytes 393224 | tf_op jit(solution)/shard_map/ppermute | solution.py:497
  107.3 7.8 %copy-start.9 = (bf16[2,256,128]{2,1,0:T(8,128)(2,1)}, bf16[2,256,128]{2,1,0:T(8,128)(2,1)S(1)}, u32[]{:S(2)}) copy-start(bf16[2,256,128]{2,1,0:T(8,128)(2,1)S(1)} %collective-permute-done.7._.refs_4_) | copy-start | bytes 393220
  107.3 7.8 %copy-start.10 = (bf16[2,256,128]{2,1,0:T(8,128)(2,1)}, bf16[2,256,128]{2,1,0:T(8,128)(2,1)S(1)}, u32[]{:S(2)}) copy-start(bf16[2,256,128]{2,1,0:T(8,128)(2,1)S(1)} %collective-permute-done.8.__.refs_5_) | copy-start | bytes 393220
  116.1 13.5 %all-to-all-start.5 = ((bf16[16,128,128]{2,1,0:T(8,128)(2,1)}), bf16[16,128,128]{2,1,0:T(8,128)(2,1)S(1)}, u32[]{:S(2)}, u32[]{:S(2)}) async-start(bf16[16,128,128]{2,1,0:T(8,128)(2,1)} %get-tuple-element.76), calls=%async_computation.5 | async-start | bytes 1048576 | tf_op jit(solution)/shard_map/all_to_all | solution.py:482
  119.7 3.4 %collective-permute-start.9 = (bf16[256,128]{1,0:T(8,128)(2,1)S(1)}, bf16[256,128]{1,0:T(8,128)(2,1)S(1)}, u32[]{:S(2)}, u32[]{:S(2)}) collective-permute-start(bf16[256,128]{1,0:T(8,128)(2,1)S(1)} %copy-done.16), channel_id=1, source_target_pairs={{0,16},{16,0},{32,48},{48,32},{64,80},{80,64},{96,112},{112,96},{1... | collective-permute-start | bytes 196616 | tf_op jit(solution)/shard_map/ppermute | solution.py:494
  121.0 5.9 %collective-permute-start.10 = (bf16[256,128]{1,0:T(8,128)(2,1)S(1)}, bf16[256,128]{1,0:T(8,128)(2,1)S(1)}, u32[]{:S(2)}, u32[]{:S(2)}) collective-permute-start(bf16[256,128]{1,0:T(8,128)(2,1)S(1)} %copy-done.15), channel_id=1, source_target_pairs={{16,32},{48,64},{80,96},{112,128},{144,160},{176,192},{208,224},{3... | collective-permute-start | bytes 196616 | tf_op jit(solution)/shard_map/ppermute | solution.py:495
  123.1 6.5 %copy-start.11 = (bf16[256,128]{1,0:T(8,128)(2,1)}, bf16[256,128]{1,0:T(8,128)(2,1)S(1)}, u32[]{:S(2)}) copy-start(bf16[256,128]{1,0:T(8,128)(2,1)S(1)} %collective-permute-done.9._.refs_2_) | copy-start | bytes 196612
  129.6 30.0 %copy-start = (f32[2,1024,128]{2,1,0:T(8,128)S(1)}, f32[2,1024,128]{2,1,0:T(8,128)}, u32[]{:S(2)}) copy-start(f32[2,1024,128]{2,1,0:T(8,128)} %get-tuple-element.94.search) | copy-start | bytes 3145732
  129.6 30.0 %copy-start.1 = (f32[2,1024,128]{2,1,0:T(8,128)S(1)}, f32[2,1024,128]{2,1,0:T(8,128)}, u32[]{:S(2)}) copy-start(f32[2,1024,128]{2,1,0:T(8,128)} %get-tuple-element.95.prod) | copy-start | bytes 3145732
  129.7 4.4 %collective-permute-start.11 = (bf16[2048,128]{1,0:T(8,128)(2,1)S(1)}, bf16[2048,128]{1,0:T(8,128)(2,1)S(1)}, u32[]{:S(2)}, u32[]{:S(2)}) collective-permute-start(bf16[2048,128]{1,0:T(8,128)(2,1)S(1)} %bitcast.9), channel_id=1, source_target_pairs={{0,16},{16,0},{1,17},{17,1},{2,18},{18,2},{3,19},{19,3},{4,20},{20... | collective-permute-start | bytes 1572872 | tf_op jit(solution)/shard_map/ppermute | solution.py:486
  (3 other events, 7.7 us)

commit v5 on v4

--- a/solution.py
+++ b/solution.py
@@ -506,12 +506,12 @@
     pay, stats = call(
         z_sum_kernel,
         [((SY, HALF, K), BF16), ((8, K), F32)],
-        [VM, HB, HB],
+        [VM, AN, AN],
         [HB, VM],
         [((HALF, K), BF16), sems(SY)],
     )(rec, *arrived[2:])
     sol = all_to_all(pay, ("x", "y"))
-    (sol,) = call(tie_kernel, [((SY, HALF, K), BF16)], [AN] + [HB] * 2, [AN], aliases={0: 0})(sol, *arrived[:2])
+    (sol,) = call(tie_kernel, [((SY, HALF, K), BF16)], [AN] * 3, [AN], aliases={0: 0})(sol, *arrived[:2])
     kinds = [(a.shape, a.dtype) for a in needed]
     needed = call(preload_kernel, kinds, [AN] + [HB] * len(kinds), [VM] * len(kinds), [sems(len(kinds))])(sol, *needed)
     sol = sol.reshape(SY * HALF, K)
@@ -557,14 +557,14 @@
         [VM, VM, HB],
         [((E, NC), BF16), ((E, B), BF16), ((NC, B), BF16), sems(2)],
     )(rec, coarse_inv, gram)
-    sol_own, sol_other, _, needed = coarse_solution(own, snd, arrived, [inter, gram, *arrived])
+    sol_own, sol_other, _, needed = coarse_solution(own, snd, arrived, [inter, gram])
     jump0, prod, half1, pay = call(
         second_kernel,
         [whole, whole, halved, payload],
         [SM] + [VM] * 8 + [HB] * 4,
         [HB] * 4,
         [whole, square, square, ((2, CORN, B), BF16), whole, whole, halved, block, sems(24 + SY)],
-    )(sizes, sol_own, sol_other, *needed, res, pre, factor, half)
+    )(sizes, sol_own, sol_other, *needed, *arrived, res, pre, factor, half)
     rec = all_to_all(pay, ("x", "y"))
     slim = edges_of(K)
     inter1, *edges = call(
@@ -576,14 +576,14 @@
     )(sizes, half1, factor)
     arrived1 = exchange(*edges)
     own, snd = call(coarse_next_kernel, sent, [VM] * 2 + [HB], [VM] * 2)(rec, picked_inv, inter1)
-    sol_own, sol_other, stats, needed = coarse_solution(own, snd, arrived1, [inter1, gram, *arrived1, *arrived])
+    sol_own, sol_other, stats, needed = coarse_solution(own, snd, arrived1, [inter1, gram, *arrived])
     res1, jump1, pay = call(
         third_kernel,
         [whole] * 2 + [((CS * YS, 8, K), F32)],
         [SM] + [VM] * 13 + [HB] * 2,
         [VM] * 3,
         [whole, whole, sems(2)],
-    )(sizes, sol_own, sol_other, stats, *needed, res, jump0)
+    )(sizes, sol_own, sol_other, stats, *needed[:2], *arrived1, *needed[2:], res, jump0)
     rec = all_to_all(pay, ("core", "y"))
     (pay,) = call(partial_kernel, [((ZS * XS, 8, K), F32)], [VM], [VM])(rec)
     rec = all_to_all(pay, ("z", "x"))

time: 162 us -> 160 us (0.988)
  starting transfers between devices: 54.5 us -> 51 us
  waiting for transfers between devices: 42.7 us -> 45.1 us
    all_to_all x6, waiting for transfers between devices: 23.3 us -> 25.3 us  [all_to_all(): return lax.all_to_all(value, axes, split_axis=0, concat_axis=0)]
    ppermute x4, starting transfers between devices: 10.6 us -> 8.92 us  [swap(): return lax.ppermute(value, 'core', [(0, 1), (1, 0)])]
  transfers between devices with their start and end apart: 18 -> 18, of which waited for: 12 -> 13; matrix products, arithmetic and copies ran while one was open for 0% -> 0% of each run, Pallas kernels for 8% -> 7%
where the time goes in v5:
time: 160 us; the launch traced here: 159 us
  starting transfers between devices  51 us (32%)
  waiting for transfers between devices  45.1 us (28%)
  Pallas kernels  40.3 us (25%)
  blocking collectives  21.2 us (13%)
    pallas_call x17, Pallas kernels, placed(): run(*[pltpu.with_memory_space_constraint(a, pltpu.HBM) if spec is HB else...  40.3 us
    all_to_all x6, starting transfers between devices, all_to_all(): return lax.all_to_all(value, axes, split_axis=0, concat_axis=0)  32.9 us
    all_to_all x6, waiting for transfers between devices, all_to_all(): return lax.all_to_all(value, axes, split_axis=0, concat_axis=0)  25.3 us
    all_to_all x2, blocking collectives, all_to_all(): return lax.all_to_all(value, axes, split_axis=0, concat_axis=0)  21.2 us
    ppermute x2, waiting for transfers between devices, exchange(): lax.ppermute(near, cols, even)  10.5 us
    ppermute x4, starting transfers between devices, swap(): return lax.ppermute(value, 'core', [(0, 1), (1, 0)])  8.92 us
    ppermute x2, waiting for transfers between devices, exchange(): lax.ppermute(far, rows, odd)  7.31 us
    ppermute x2, starting transfers between devices, exchange(): lax.ppermute(far, rows, odd)  5.09 us
  transfers between devices with their start and end apart: 18, of which 13 were waited for; matrix products, arithmetic and copies ran while one was open for 0% of the time, Pallas kernels for 7%

profile of v5, /device:TPU:1, one launch (start us, length us, event | category | flops | bytes accessed | tf_op | source)
XLA Modules:
  0.0 158.7 jit_solution(6639074094868274118)
XLA Ops:
  0.7 6.9 %shard_map.86 = (f32[2,1024,128]{2,1,0:T(8,128)}, f32[2,1024,128]{2,1,0:T(8,128)}, bf16[2,160,1024]{2,1,0:T(8,128)(2,1)}, bf16[16,80,128]{2,1,0:T(8,128)(2,1)}) custom-call(s32[2]{0:T(128)} %bitcast.13, s32[2,1,1024]{2,1,0:T(1,128)} %snow_hbm.1, s32[2,1,32]{2,1,0:T(1,128)} %cmap.1, bf16[2,1,1024,128]{3,2,1,0:T(8,128)(2,1)} %press_hbm.1, ...), custom_call_target="tpu_custom_call" | custom-call | tf_op jit(solution)/shard_map/pallas_call | solution.py:57
  7.5 7.6 %all-to-all-start = ((bf16[16,80,128]{2,1,0:T(8,128)(2,1)}), bf16[16,80,128]{2,1,0:T(8,128)(2,1)S(1)}, u32[]{:S(2)}, u32[]{:S(2)}) async-start(bf16[16,80,128]{2,1,0:T(8,128)(2,1)} %get-tuple-element.42), calls=%async_computation | async-start | bytes 655360 | tf_op jit(solution)/shard_map/all_to_all | solution.py:482
  15.1 4.7 %shard_map.87 = (f32[2,1024,128]{2,1,0:T(8,128)}, bf16[2,1024,128]{2,1,0:T(8,128)(2,1)}, bf16[256,256]{1,0:T(8,128)(2,1)}, bf16[256,256]{1,0:T(8,128)(2,1)}, bf1...) custom-call(s32[2]{0:T(128)S(1)} %bitcast.14, s32[2,1,32]{2,1,0:T(1,128)S(1)} %copy-done.8, ...), custom_call_target="tpu_custom_call" | custom-call | tf_op jit(solution)/shard_map/pallas_call | solution.py:57
  19.9 3.0 %all-to-all-done.rec = bf16[16,80,128]{2,1,0:T(8,128)(2,1)S(1)} async-done(((bf16[16,80,128]{2,1,0:T(8,128)(2,1)}), bf16[16,80,128]{2,1,0:T(8,128)(2,1)S(1)}, u32[]{:S(2)}, u32[]{:S(2)}) %all-to-all-start) | async-done | bytes 327712 | tf_op jit(solution)/shard_map/all_to_all | solution.py:482
  22.9 4.7 %shard_map.88 = (f32[136,128]{1,0:T(8,128)S(1)}, f32[136,128]{1,0:T(8,128)S(1)}, bf16[256,1024]{1,0:T(8,128)(2,1)}) custom-call(bf16[16,80,128]{2,1,0:T(8,128)(2,1)S(1)} %all-to-all-done.rec, bf16[256,4096]{1,0:T(8,128)(2,1)} %coarse_hbm.1, bf16[2,1024,128]{2,1,0:T(8,128)(2,1)} %get-tuple-element.44._.refs_1_), custom_call_target="tpu_custom_call" | custom-call | tf_op jit(solution)/shard_map/pallas_call | solution.py:57
  27.7 2.4 %collective-permute-start = (f32[136,128]{1,0:T(8,128)S(1)}, f32[136,128]{1,0:T(8,128)S(1)}, u32[]{:S(2)}, u32[]{:S(2)}) collective-permute-start(f32[136,128]{1,0:T(8,128)S(1)} %get-tuple-element.46), channel_id=1, source_target_pairs={{0,16},{16,0},{1,17},{17,1},{2,18},{18,2},{3,19},{19,3},{4,20},{20... | collective-permute-start | bytes 208904 | tf_op jit(solution)/shard_map/ppermute | solution.py:486
  31.8 8.2 %all-to-all-start.1 = ((bf16[8,144,128]{2,1,0:T(8,128)(2,1)}), bf16[8,144,128]{2,1,0:T(8,128)(2,1)S(1)}, u32[]{:S(2)}, u32[]{:S(2)}) async-start(bf16[8,144,128]{2,1,0:T(8,128)(2,1)} %shard_map.89), calls=%async_computation.1 | async-start | bytes 589824 | tf_op jit(solution)/shard_map/all_to_all | solution.py:482
  40.8 6.6 %collective-permute-done.1._.near.refs_4_ = bf16[2,256,256]{2,1,0:T(8,128)(2,1)S(1)} collective-permute-done((bf16[2,256,256]{2,1,0:T(8,128)(2,1)}, bf16[2,256,256]{2,1,0:T(8,128)(2,1)S(1)}, u32[]{:S(2)}, u32[]{:S(2)}) %collective-permute-start.1) | collective-permute-done | bytes 262176 | tf_op jit(solution)/shard_map/ppermute | solution.py:496
  47.4 5.0 %all-to-all-done.1.rec = bf16[8,144,128]{2,1,0:T(8,128)(2,1)S(1)} async-done(((bf16[8,144,128]{2,1,0:T(8,128)(2,1)}), bf16[8,144,128]{2,1,0:T(8,128)(2,1)S(1)}, u32[]{:S(2)}, u32[]{:S(2)}) %all-to-all-start.1) | async-done | bytes 294944 | tf_op jit(solution)/shard_map/all_to_all | solution.py:482
  52.4 1.6 %shard_map.90 = (bf16[16,128,128]{2,1,0:T(8,128)(2,1)}, f32[8,128]{1,0:T(8,128)}) custom-call(bf16[8,144,128]{2,1,0:T(8,128)(2,1)S(1)} %all-to-all-done.1.rec, bf16[2,256,256]{2,1,0:T(8,128)(2,1)S(1)} %collective-permute-done.1._.near.refs_4_, bf16[2,256,256]{2,1,0:T(8,128)(2,1)S(1)} %collective-permute-done.2.__.other.refs_5_), custom_call_target="tpu_custom_call" | custom-call | tf_op jit(solution)/shard_map/pallas_call | solution.py:57
  54.1 3.6 %all-to-all-start.2 = ((bf16[16,128,128]{2,1,0:T(8,128)(2,1)}), bf16[16,128,128]{2,1,0:T(8,128)(2,1)S(1)}, u32[]{:S(2)}, u32[]{:S(2)}) async-start(bf16[16,128,128]{2,1,0:T(8,128)(2,1)} %get-tuple-element.49), calls=%async_computation.2 | async-start | bytes 1048576 | tf_op jit(solution)/shard_map/all_to_all | solution.py:482
  58.9 3.0 %collective-permute-start.4 = (bf16[256,256]{1,0:T(8,128)(2,1)S(1)}, bf16[256,256]{1,0:T(8,128)(2,1)S(1)}, u32[]{:S(2)}, u32[]{:S(2)}) collective-permute-start(bf16[256,256]{1,0:T(8,128)(2,1)S(1)} %copy-done.9), channel_id=1, source_target_pairs={{16,32},{48,64},{80,96},{112,128},{144,160},{176,192},{208,224},{3... | collective-permute-start | bytes 393224 | tf_op jit(solution)/shard_map/ppermute | solution.py:495
  62.0 3.6 %collective-permute-done.4.__.far.refs_3_ = bf16[256,256]{1,0:T(8,128)(2,1)S(1)} collective-permute-done((bf16[256,256]{1,0:T(8,128)(2,1)S(1)}, bf16[256,256]{1,0:T(8,128)(2,1)S(1)}, u32[]{:S(2)}, u32[]{:S(2)}) %collective-permute-start.4) | collective-permute-done | bytes 131104 | tf_op jit(solution)/shard_map/ppermute | solution.py:495
  65.5 2.0 %all-to-all-done.2.source = bf16[16,128,128]{2,1,0:T(8,128)(2,1)S(1)} async-done(((bf16[16,128,128]{2,1,0:T(8,128)(2,1)}), bf16[16,128,128]{2,1,0:T(8,128)(2,1)S(1)}, u32[]{:S(2)}, u32[]{:S(2)}) %all-to-all-start.2) | async-done | bytes 524320 | tf_op jit(solution)/shard_map/all_to_all | solution.py:482
  67.5 2.5 %collective-permute-start.5 = (bf16[2048,128]{1,0:T(8,128)(2,1)S(1)}, bf16[2048,128]{1,0:T(8,128)(2,1)S(1)}, u32[]{:S(2)}, u32[]{:S(2)}) collective-permute-start(bf16[2048,128]{1,0:T(8,128)(2,1)S(1)} %bitcast.11), channel_id=1, source_target_pairs={{0,16},{16,0},{1,17},{17,1},{2,18},{18,2},{3,19},{19,3},{4,20},{20... | collective-permute-start | bytes 1572872 | tf_op jit(solution)/shard_map/ppermute | solution.py:486
  71.6 7.6 %shard_map.93 = (f32[2,1024,128]{2,1,0:T(8,128)}, f32[2,1024,128]{2,1,0:T(8,128)}, bf16[2,128,1024]{2,1,0:T(8,128)(2,1)}, bf16[16,80,128]{2,1,0:T(8,128)(2,1)}) custom-call(s32[2]{0:T(128)S(1)} %bitcast.15, bf16[2048,128]{1,0:T(8,128)(2,1)S(1)} %bitcast.12, bf16[2048,128]{1,0:T(8,128)(2,1)S(1)} %collective-permute-done.5.sol_other, ...), custom_call_target="tpu_custom_call" | custom-call | tf_op jit(solution)/shard_map/pallas_call | solution.py:57
  79.3 3.7 %all-to-all-start.3 = ((bf16[16,80,128]{2,1,0:T(8,128)(2,1)}), bf16[16,80,128]{2,1,0:T(8,128)(2,1)S(1)}, u32[]{:S(2)}, u32[]{:S(2)}) async-start(bf16[16,80,128]{2,1,0:T(8,128)(2,1)} %get-tuple-element.56), calls=%async_computation.3 | async-start | bytes 655360 | tf_op jit(solution)/shard_map/all_to_all | solution.py:482
  82.9 4.0 %shard_map.94 = (f32[2,1024,128]{2,1,0:T(8,128)}, bf16[256,128]{1,0:T(8,128)(2,1)}, bf16[256,128]{1,0:T(8,128)(2,1)}, bf16[2,256,128]{2,1,0:T(8,128)(2,1)}, bf16[2,256,128]{2,1,0:T(8,128)(2,1)}) custom-call(s32[2]{0:T(128)S(1)} %bitcast.16, bf16[2,128,1024]{2,1,0:T(8,128)(2,1)} %get-tuple-element.58.half_hbm, bf16[2,1,1024,1024]{3,2,1,0:T(8,128)(2,1)} %fac_hbm.7), custom_call_target="tpu_custom_call" | custom-call | tf_op jit(solution)/shard_map/pallas_call | solution.py:57
  86.9 4.6 %all-to-all-done.3.rec = bf16[16,80,128]{2,1,0:T(8,128)(2,1)S(1)} async-done(((bf16[16,80,128]{2,1,0:T(8,128)(2,1)}), bf16[16,80,128]{2,1,0:T(8,128)(2,1)S(1)}, u32[]{:S(2)}, u32[]{:S(2)}) %all-to-all-start.3) | async-done | bytes 327712 | tf_op jit(solution)/shard_map/all_to_all | solution.py:482
  91.9 1.5 collective-permute-start.6
  95.1 6.2 %all-to-all-start.4 = ((bf16[8,144,128]{2,1,0:T(8,128)(2,1)}), bf16[8,144,128]{2,1,0:T(8,128)(2,1)S(1)}, u32[]{:S(2)}, u32[]{:S(2)}) async-start(bf16[8,144,128]{2,1,0:T(8,128)(2,1)} %shard_map.96), calls=%async_computation.4 | async-start | bytes 589824 | tf_op jit(solution)/shard_map/all_to_all | solution.py:482
  102.1 3.9 %collective-permute-done.7._.near = bf16[2,256,128]{2,1,0:T(8,128)(2,1)S(1)} collective-permute-done((bf16[2,256,128]{2,1,0:T(8,128)(2,1)}, bf16[2,256,128]{2,1,0:T(8,128)(2,1)S(1)}, u32[]{:S(2)}, u32[]{:S(2)}) %collective-permute-start.7) | collective-permute-done | bytes 131104 | tf_op jit(solution)/shard_map/ppermute | solution.py:496
  106.0 7.8 %all-to-all-done.4.rec = bf16[8,144,128]{2,1,0:T(8,128)(2,1)S(1)} async-done(((bf16[8,144,128]{2,1,0:T(8,128)(2,1)}), bf16[8,144,128]{2,1,0:T(8,128)(2,1)S(1)}, u32[]{:S(2)}, u32[]{:S(2)}) %all-to-all-start.4) | async-done | bytes 294944 | tf_op jit(solution)/shard_map/all_to_all | solution.py:482
  114.8 3.6 %all-to-all-start.5 = ((bf16[16,128,128]{2,1,0:T(8,128)(2,1)}), bf16[16,128,128]{2,1,0:T(8,128)(2,1)S(1)}, u32[]{:S(2)}, u32[]{:S(2)}) async-start(bf16[16,128,128]{2,1,0:T(8,128)(2,1)} %get-tuple-element.64), calls=%async_computation.5 | async-start | bytes 1048576 | tf_op jit(solution)/shard_map/all_to_all | solution.py:482
  119.6 2.1 %collective-permute-start.10 = (bf16[256,128]{1,0:T(8,128)(2,1)S(1)}, bf16[256,128]{1,0:T(8,128)(2,1)S(1)}, u32[]{:S(2)}, u32[]{:S(2)}) collective-permute-start(bf16[256,128]{1,0:T(8,128)(2,1)S(1)} %copy-done.11), channel_id=1, source_target_pairs={{16,32},{48,64},{80,96},{112,128},{144,160},{176,192},{208,224},{3... | collective-permute-start | bytes 196616 | tf_op jit(solution)/shard_map/ppermute | solution.py:495
  121.8 3.8 %collective-permute-done.10.__.far = bf16[256,128]{1,0:T(8,128)(2,1)S(1)} collective-permute-done((bf16[256,128]{1,0:T(8,128)(2,1)S(1)}, bf16[256,128]{1,0:T(8,128)(2,1)S(1)}, u32[]{:S(2)}, u32[]{:S(2)}) %collective-permute-start.10) | collective-permute-done | bytes 65568 | tf_op jit(solution)/shard_map/ppermute | solution.py:495
  125.5 2.8 %all-to-all-done.5.source = bf16[16,128,128]{2,1,0:T(8,128)(2,1)S(1)} async-done(((bf16[16,128,128]{2,1,0:T(8,128)(2,1)}), bf16[16,128,128]{2,1,0:T(8,128)(2,1)S(1)}, u32[]{:S(2)}, u32[]{:S(2)}) %all-to-all-start.5) | async-done | bytes 524320 | tf_op jit(solution)/shard_map/all_to_all | solution.py:482
  128.3 2.5 %collective-permute-start.11 = (bf16[2048,128]{1,0:T(8,128)(2,1)S(1)}, bf16[2048,128]{1,0:T(8,128)(2,1)S(1)}, u32[]{:S(2)}, u32[]{:S(2)}) collective-permute-start(bf16[2048,128]{1,0:T(8,128)(2,1)S(1)} %bitcast.9), channel_id=1, source_target_pairs={{0,16},{16,0},{1,17},{17,1},{2,18},{18,2},{3,19},{19,3},{4,20},{20... | collective-permute-start | bytes 1572872 | tf_op jit(solution)/shard_map/ppermute | solution.py:486
  130.8 1.6 %shard_map.99 = (f32[2,1024,128]{2,1,0:T(8,128)S(1)}, bf16[2,1024,128]{2,1,0:T(8,128)(2,1)S(1)}, bf16[256,256]{1,0:T(8,128)(2,1)S(1)}, bf16[256,256]{1,0:T(8,128...) custom-call(bf16[16,128,128]{2,1,0:T(8,128)(2,1)S(1)} %shard_map.98._, ...), custom_call_target="tpu_custom_call" | custom-call | tf_op jit(solution)/shard_map/pallas_call | solution.py:57
  132.4 3.4 %shard_map.100 = (f32[2,1024,128]{2,1,0:T(8,128)S(1)}, f32[2,1024,128]{2,1,0:T(8,128)S(1)}, f32[8,8,128]{2,1,0:T(8,128)S(1)}) custom-call(s32[2]{0:T(128)S(1)} %bitcast.17, bf16[2048,128]{1,0:T(8,128)(2,1)S(1)} %bitcast.10, bf16[2048,128]{1,0:T(8,128)(2,1)S(1)} %collective-permute-done.11.sol_other, f32[8,128]{1,0:T(8,128)S(1)} %get-tuple-element.67.stats, ...), custom_call_target="tpu_custom_call" | custom-call | tf_op jit(solution)/shard_map/pallas_call | solution.py:57
  135.9 7.5 %all_to_all.40.rec = f32[8,8,128]{2,1,0:T(8,128)S(1)} all-to-all(f32[8,8,128]{2,1,0:T(8,128)S(1)} %get-tuple-element.75), channel_id=1, replica_groups=mesh['z'=8,'core'=2,'x'=4,'y'=4] {'core','y'}, dimensions={0} | all-to-all | bytes 65536 | tf_op jit(solution)/shard_map/all_to_all | solution.py:482
  143.4 13.6 %all_to_all.41.rec = f32[32,8,128]{2,1,0:T(8,128)S(1)} all-to-all(f32[32,8,128]{2,1,0:T(8,128)S(1)} %shard_map.101), channel_id=1, replica_groups=mesh['z'=8,'core'=2,'x'=4,'y'=4] {'z','x'}, dimensions={0} | all-to-all | bytes 262144 | tf_op jit(solution)/shard_map/all_to_all | solution.py:482
  (49 shorter events, 11.9 us)
Async XLA Ops:
  0.6 14.5 %copy-start.7 = (s32[2,1]{0,1:T(1,128)S(1)}, s32[2,1]{0,1:T(1,128)}, u32[]{:S(2)}) copy-start(s32[2,1]{0,1:T(1,128)} %param.10) | copy-start | bytes 28
  0.6 14.5 %copy-start.8 = (s32[2,1,32]{2,1,0:T(1,128)S(1)}, s32[2,1,32]{2,1,0:T(1,128)}, u32[]{:S(2)}) copy-start(s32[2,1,32]{2,1,0:T(1,128)} %cmap.1) | copy-start | bytes 772
  7.5 15.4 %all-to-all-start = ((bf16[16,80,128]{2,1,0:T(8,128)(2,1)}), bf16[16,80,128]{2,1,0:T(8,128)(2,1)S(1)}, u32[]{:S(2)}, u32[]{:S(2)}) async-start(bf16[16,80,128]{2,1,0:T(8,128)(2,1)} %get-tuple-element.42), calls=%async_computation | async-start | bytes 655360 | tf_op jit(solution)/shard_map/all_to_all | solution.py:482
  19.9 37.8 %copy-start.10 = (bf16[256,256]{1,0:T(8,128)(2,1)S(1)}, bf16[256,256]{1,0:T(8,128)(2,1)}, u32[]{:S(2)}) copy-start(bf16[256,256]{1,0:T(8,128)(2,1)} %get-tuple-element.50) | copy-start | bytes 393220
  19.9 39.1 %copy-start.9 = (bf16[256,256]{1,0:T(8,128)(2,1)S(1)}, bf16[256,256]{1,0:T(8,128)(2,1)}, u32[]{:S(2)}) copy-start(bf16[256,256]{1,0:T(8,128)(2,1)} %get-tuple-element.51) | copy-start | bytes 393220
  27.7 3.3 %collective-permute-start = (f32[136,128]{1,0:T(8,128)S(1)}, f32[136,128]{1,0:T(8,128)S(1)}, u32[]{:S(2)}, u32[]{:S(2)}) collective-permute-start(f32[136,128]{1,0:T(8,128)S(1)} %get-tuple-element.46), channel_id=1, source_target_pairs={{0,16},{16,0},{1,17},{17,1},{2,18},{18,2},{3,19},{19,3},{4,20},{20... | collective-permute-start | bytes 208904 | tf_op jit(solution)/shard_map/ppermute | solution.py:486
  31.8 20.6 %all-to-all-start.1 = ((bf16[8,144,128]{2,1,0:T(8,128)(2,1)}), bf16[8,144,128]{2,1,0:T(8,128)(2,1)S(1)}, u32[]{:S(2)}, u32[]{:S(2)}) async-start(bf16[8,144,128]{2,1,0:T(8,128)(2,1)} %shard_map.89), calls=%async_computation.1 | async-start | bytes 589824 | tf_op jit(solution)/shard_map/all_to_all | solution.py:482
  40.0 7.4 %collective-permute-start.1 = (bf16[2,256,256]{2,1,0:T(8,128)(2,1)}, bf16[2,256,256]{2,1,0:T(8,128)(2,1)S(1)}, u32[]{:S(2)}, u32[]{:S(2)}) collective-permute-start(bf16[2,256,256]{2,1,0:T(8,128)(2,1)} %get-tuple-element.47), channel_id=1, source_target_pairs={{0,1},{1,0},{2,3},{3,2},{4,5},{5,4},{6,7},{7,6},{8,9},{9,8},{10,11... | collective-permute-start | bytes 786440 | tf_op jit(solution)/shard_map/ppermute | solution.py:496
  40.1 7.3 %collective-permute-start.2 = (bf16[2,256,256]{2,1,0:T(8,128)(2,1)}, bf16[2,256,256]{2,1,0:T(8,128)(2,1)S(1)}, u32[]{:S(2)}, u32[]{:S(2)}) collective-permute-start(bf16[2,256,256]{2,1,0:T(8,128)(2,1)} %get-tuple-element.48), channel_id=1, source_target_pairs={{1,2},{3,4},{5,6},{7,8},{9,10},{11,12},{13,14},{2,1},{4,3},{6,5},{... | collective-permute-start | bytes 786440 | tf_op jit(solution)/shard_map/ppermute | solution.py:497
  47.4 31.8 %copy-start = (bf16[2,256,256]{2,1,0:T(8,128)(2,1)}, bf16[2,256,256]{2,1,0:T(8,128)(2,1)S(1)}, u32[]{:S(2)}) copy-start(bf16[2,256,256]{2,1,0:T(8,128)(2,1)S(1)} %collective-permute-done.1._.near.refs_4_) | copy-start | bytes 786436
  47.4 31.8 %copy-start.1 = (bf16[2,256,256]{2,1,0:T(8,128)(2,1)}, bf16[2,256,256]{2,1,0:T(8,128)(2,1)S(1)}, u32[]{:S(2)}) copy-start(bf16[2,256,256]{2,1,0:T(8,128)(2,1)S(1)} %collective-permute-done.2.__.other.refs_5_) | copy-start | bytes 786436
  54.1 13.5 %all-to-all-start.2 = ((bf16[16,128,128]{2,1,0:T(8,128)(2,1)}), bf16[16,128,128]{2,1,0:T(8,128)(2,1)S(1)}, u32[]{:S(2)}, u32[]{:S(2)}) async-start(bf16[16,128,128]{2,1,0:T(8,128)(2,1)} %get-tuple-element.49), calls=%async_computation.2 | async-start | bytes 1048576 | tf_op jit(solution)/shard_map/all_to_all | solution.py:482
  57.7 4.3 %collective-permute-start.3 = (bf16[256,256]{1,0:T(8,128)(2,1)S(1)}, bf16[256,256]{1,0:T(8,128)(2,1)S(1)}, u32[]{:S(2)}, u32[]{:S(2)}) collective-permute-start(bf16[256,256]{1,0:T(8,128)(2,1)S(1)} %copy-done.10), channel_id=1, source_target_pairs={{0,16},{16,0},{32,48},{48,32},{64,80},{80,64},{96,112},{112,96},{1... | collective-permute-start | bytes 393224 | tf_op jit(solution)/shard_map/ppermute | solution.py:494
  58.9 6.6 %collective-permute-start.4 = (bf16[256,256]{1,0:T(8,128)(2,1)S(1)}, bf16[256,256]{1,0:T(8,128)(2,1)S(1)}, u32[]{:S(2)}, u32[]{:S(2)}) collective-permute-start(bf16[256,256]{1,0:T(8,128)(2,1)S(1)} %copy-done.9), channel_id=1, source_target_pairs={{16,32},{48,64},{80,96},{112,128},{144,160},{176,192},{208,224},{3... | collective-permute-start | bytes 393224 | tf_op jit(solution)/shard_map/ppermute | solution.py:495
  61.9 17.3 %copy-start.2 = (bf16[256,256]{1,0:T(8,128)(2,1)}, bf16[256,256]{1,0:T(8,128)(2,1)S(1)}, u32[]{:S(2)}) copy-start(bf16[256,256]{1,0:T(8,128)(2,1)S(1)} %collective-permute-done.3._.chip.refs_2_) | copy-start | bytes 393220
  65.5 13.7 %copy-start.3 = (bf16[256,256]{1,0:T(8,128)(2,1)}, bf16[256,256]{1,0:T(8,128)(2,1)S(1)}, u32[]{:S(2)}) copy-start(bf16[256,256]{1,0:T(8,128)(2,1)S(1)} %collective-permute-done.4.__.far.refs_3_) | copy-start | bytes 393220
  67.5 4.0 %collective-permute-start.5 = (bf16[2048,128]{1,0:T(8,128)(2,1)S(1)}, bf16[2048,128]{1,0:T(8,128)(2,1)S(1)}, u32[]{:S(2)}, u32[]{:S(2)}) collective-permute-start(bf16[2048,128]{1,0:T(8,128)(2,1)S(1)} %bitcast.11), channel_id=1, source_target_pairs={{0,16},{16,0},{1,17},{17,1},{2,18},{18,2},{3,19},{19,3},{4,20},{20... | collective-permute-start | bytes 1572872 | tf_op jit(solution)/shard_map/ppermute | solution.py:486
  79.2 12.3 %copy-start.6 = (bf16[256,1024]{1,0:T(8,128)(2,1)S(1)}, bf16[256,1024]{1,0:T(8,128)(2,1)}, u32[]{:S(2)}) copy-start(bf16[256,1024]{1,0:T(8,128)(2,1)} %get-tuple-element.57.picked_inv) | copy-start | bytes 1572868
  79.3 12.3 %all-to-all-start.3 = ((bf16[16,80,128]{2,1,0:T(8,128)(2,1)}), bf16[16,80,128]{2,1,0:T(8,128)(2,1)S(1)}, u32[]{:S(2)}, u32[]{:S(2)}) async-start(bf16[16,80,128]{2,1,0:T(8,128)(2,1)} %get-tuple-element.56), calls=%async_computation.3 | async-start | bytes 655360 | tf_op jit(solution)/shard_map/all_to_all | solution.py:482
  86.9 31.4 %copy-start.12 = (bf16[256,128]{1,0:T(8,128)(2,1)S(1)}, bf16[256,128]{1,0:T(8,128)(2,1)}, u32[]{:S(2)}) copy-start(bf16[256,128]{1,0:T(8,128)(2,1)} %get-tuple-element.65) | copy-start | bytes 196612
  86.9 32.7 %copy-start.11 = (bf16[256,128]{1,0:T(8,128)(2,1)S(1)}, bf16[256,128]{1,0:T(8,128)(2,1)}, u32[]{:S(2)}) copy-start(bf16[256,128]{1,0:T(8,128)(2,1)} %get-tuple-element.66) | copy-start | bytes 196612
  91.9 2.4 %collective-permute-start.6 = (f32[136,128]{1,0:T(8,128)S(1)}, f32[136,128]{1,0:T(8,128)S(1)}, u32[]{:S(2)}, u32[]{:S(2)}) collective-permute-start(f32[136,128]{1,0:T(8,128)S(1)} %get-tuple-element.61), channel_id=1, source_target_pairs={{0,16},{16,0},{1,17},{17,1},{2,18},{18,2},{3,19},{19,3},{4,20},{20... | collective-permute-start | bytes 208904 | tf_op jit(solution)/shard_map/ppermute | solution.py:486
  95.1 18.7 %all-to-all-start.4 = ((bf16[8,144,128]{2,1,0:T(8,128)(2,1)}), bf16[8,144,128]{2,1,0:T(8,128)(2,1)S(1)}, u32[]{:S(2)}, u32[]{:S(2)}) async-start(bf16[8,144,128]{2,1,0:T(8,128)(2,1)} %shard_map.96), calls=%async_computation.4 | async-start | bytes 589824 | tf_op jit(solution)/shard_map/all_to_all | solution.py:482
  101.3 4.6 %collective-permute-start.7 = (bf16[2,256,128]{2,1,0:T(8,128)(2,1)}, bf16[2,256,128]{2,1,0:T(8,128)(2,1)S(1)}, u32[]{:S(2)}, u32[]{:S(2)}) collective-permute-start(bf16[2,256,128]{2,1,0:T(8,128)(2,1)} %get-tuple-element.62), channel_id=1, source_target_pairs={{0,1},{1,0},{2,3},{3,2},{4,5},{5,4},{6,7},{7,6},{8,9},{9,8},{10,11... | collective-permute-start | bytes 393224 | tf_op jit(solution)/shard_map/ppermute | solution.py:496
  101.4 4.6 %collective-permute-start.8 = (bf16[2,256,128]{2,1,0:T(8,128)(2,1)}, bf16[2,256,128]{2,1,0:T(8,128)(2,1)S(1)}, u32[]{:S(2)}, u32[]{:S(2)}) collective-permute-start(bf16[2,256,128]{2,1,0:T(8,128)(2,1)} %get-tuple-element.63), channel_id=1, source_target_pairs={{1,2},{3,4},{5,6},{7,8},{9,10},{11,12},{13,14},{2,1},{4,3},{6,5},{... | collective-permute-start | bytes 393224 | tf_op jit(solution)/shard_map/ppermute | solution.py:497
  114.8 13.5 %all-to-all-start.5 = ((bf16[16,128,128]{2,1,0:T(8,128)(2,1)}), bf16[16,128,128]{2,1,0:T(8,128)(2,1)S(1)}, u32[]{:S(2)}, u32[]{:S(2)}) async-start(bf16[16,128,128]{2,1,0:T(8,128)(2,1)} %get-tuple-element.64), calls=%async_computation.5 | async-start | bytes 1048576 | tf_op jit(solution)/shard_map/all_to_all | solution.py:482
  118.4 3.4 %collective-permute-start.9 = (bf16[256,128]{1,0:T(8,128)(2,1)S(1)}, bf16[256,128]{1,0:T(8,128)(2,1)S(1)}, u32[]{:S(2)}, u32[]{:S(2)}) collective-permute-start(bf16[256,128]{1,0:T(8,128)(2,1)S(1)} %copy-done.12), channel_id=1, source_target_pairs={{0,16},{16,0},{32,48},{48,32},{64,80},{80,64},{96,112},{112,96},{1... | collective-permute-start | bytes 196616 | tf_op jit(solution)/shard_map/ppermute | solution.py:494
  119.6 5.9 %collective-permute-start.10 = (bf16[256,128]{1,0:T(8,128)(2,1)S(1)}, bf16[256,128]{1,0:T(8,128)(2,1)S(1)}, u32[]{:S(2)}, u32[]{:S(2)}) collective-permute-start(bf16[256,128]{1,0:T(8,128)(2,1)S(1)} %copy-done.11), channel_id=1, source_target_pairs={{16,32},{48,64},{80,96},{112,128},{144,160},{176,192},{208,224},{3... | collective-permute-start | bytes 196616 | tf_op jit(solution)/shard_map/ppermute | solution.py:495
  128.3 28.8 %copy-start.4 = (f32[2,1024,128]{2,1,0:T(8,128)S(1)}, f32[2,1024,128]{2,1,0:T(8,128)}, u32[]{:S(2)}) copy-start(f32[2,1024,128]{2,1,0:T(8,128)} %get-tuple-element.78.search) | copy-start | bytes 3145732
  128.3 28.8 %copy-start.5 = (f32[2,1024,128]{2,1,0:T(8,128)S(1)}, f32[2,1024,128]{2,1,0:T(8,128)}, u32[]{:S(2)}) copy-start(f32[2,1024,128]{2,1,0:T(8,128)} %get-tuple-element.79.prod) | copy-start | bytes 3145732
  128.3 4.1 %collective-permute-start.11 = (bf16[2048,128]{1,0:T(8,128)(2,1)S(1)}, bf16[2048,128]{1,0:T(8,128)(2,1)S(1)}, u32[]{:S(2)}, u32[]{:S(2)}) collective-permute-start(bf16[2048,128]{1,0:T(8,128)(2,1)S(1)} %bitcast.9), channel_id=1, source_target_pairs={{0,16},{16,0},{1,17},{17,1},{2,18},{18,2},{3,19},{19,3},{4,20},{20... | collective-permute-start | bytes 1572872 | tf_op jit(solution)/shard_map/ppermute | solution.py:486

commit v6 on v5

--- a/solution.py
+++ b/solution.py
@@ -455,19 +455,19 @@
         cross += jnp.sum(before * jumped, axis=0, keepdims=True)
         energy += jnp.sum(jumped * jumped, axis=0, keepdims=True)
     block = rows_of((8, K), [cross, energy])
-    for dest in range(CS * YS):
+    for dest in range(CS * SY):
         pay[dest] = block
 
 
 def partial_kernel(rec, pay):
-    total = sum(rec[b] for b in range(CS * YS))
-    for dest in range(ZS * XS):
+    total = sum(rec[b] for b in range(CS * SY))
+    for dest in range(ZS):
         pay[dest] = total
 
 
 def last_kernel(rec, stats, res1, jump1, search, prod, mult, res, multv, resv, sem):
     copies = Copies(sem)
-    total = sum(rec[b] for b in range(ZS * XS))
+    total = sum(rec[b] for b in range(ZS))
     first = stats[0:1] / (stats[1:2] + 1e-06)
     step = total[0:1] / (total[1:2] + 1e-06)
     for s in range(2):
@@ -579,14 +579,14 @@
     sol_own, sol_other, stats, needed = coarse_solution(own, snd, arrived1, [inter1, gram, *arrived])
     res1, jump1, pay = call(
         third_kernel,
-        [whole] * 2 + [((CS * YS, 8, K), F32)],
+        [whole] * 2 + [((CS * SY, 8, K), F32)],
         [SM] + [VM] * 13 + [HB] * 2,
         [VM] * 3,
         [whole, whole, sems(2)],
     )(sizes, sol_own, sol_other, stats, *needed[:2], *arrived1, *needed[2:], res, jump0)
-    rec = all_to_all(pay, ("core", "y"))
-    (pay,) = call(partial_kernel, [((ZS * XS, 8, K), F32)], [VM], [VM])(rec)
-    rec = all_to_all(pay, ("z", "x"))
+    rec = all_to_all(pay, ("core", "x", "y"))
+    (pay,) = call(partial_kernel, [((ZS, 8, K), F32)], [VM], [VM])(rec)
+    rec = all_to_all(pay, "z")
     mult, res = call(last_kernel, [whole] * 2, [VM] * 6, [HB] * 2, [whole, whole, sems(4)])(
         rec, stats, res1, jump1, search, prod
     )

time: 160 us -> 160 us (level)
  no operation moved by 1% of the time
where the time goes in v6:
time: 160 us; the launch traced here: 159 us
  starting transfers between devices  51 us (32%)
  waiting for transfers between devices  45.1 us (28%)
  Pallas kernels  40.3 us (25%)
  blocking collectives  21.1 us (13%)
    pallas_call x17, Pallas kernels, placed(): run(*[pltpu.with_memory_space_constraint(a, pltpu.HBM) if spec is HB else...  40.3 us
    all_to_all x6, starting transfers between devices, all_to_all(): return lax.all_to_all(value, axes, split_axis=0, concat_axis=0)  32.9 us
    all_to_all x6, waiting for transfers between devices, all_to_all(): return lax.all_to_all(value, axes, split_axis=0, concat_axis=0)  25.3 us
    all_to_all x2, blocking collectives, all_to_all(): return lax.all_to_all(value, axes, split_axis=0, concat_axis=0)  21.1 us
    ppermute x2, waiting for transfers between devices, exchange(): lax.ppermute(near, cols, even)  10.5 us
    ppermute x4, starting transfers between devices, swap(): return lax.ppermute(value, 'core', [(0, 1), (1, 0)])  8.92 us
    ppermute x2, waiting for transfers between devices, exchange(): lax.ppermute(far, rows, odd)  7.31 us
    ppermute x2, starting transfers between devices, exchange(): lax.ppermute(far, rows, odd)  5.09 us
  transfers between devices with their start and end apart: 18, of which 13 were waited for; matrix products, arithmetic and copies ran while one was open for 0% of the time, Pallas kernels for 7%

profile of v6, /device:TPU:1, one launch (start us, length us, event | category | flops | bytes accessed | tf_op | source)
XLA Modules:
  0.0 158.6 jit_solution(816437886324714464)
XLA Ops:
  0.7 6.9 %shard_map.86 = (f32[2,1024,128]{2,1,0:T(8,128)}, f32[2,1024,128]{2,1,0:T(8,128)}, bf16[2,160,1024]{2,1,0:T(8,128)(2,1)}, bf16[16,80,128]{2,1,0:T(8,128)(2,1)}) custom-call(s32[2]{0:T(128)} %bitcast.13, s32[2,1,1024]{2,1,0:T(1,128)} %snow_hbm.1, s32[2,1,32]{2,1,0:T(1,128)} %cmap.1, bf16[2,1,1024,128]{3,2,1,0:T(8,128)(2,1)} %press_hbm.1, ...), custom_call_target="tpu_custom_call" | custom-call | tf_op jit(solution)/shard_map/pallas_call | solution.py:57
  7.5 7.6 %all-to-all-start = ((bf16[16,80,128]{2,1,0:T(8,128)(2,1)}), bf16[16,80,128]{2,1,0:T(8,128)(2,1)S(1)}, u32[]{:S(2)}, u32[]{:S(2)}) async-start(bf16[16,80,128]{2,1,0:T(8,128)(2,1)} %get-tuple-element.42), calls=%async_computation | async-start | bytes 655360 | tf_op jit(solution)/shard_map/all_to_all | solution.py:482
  15.1 4.7 %shard_map.87 = (f32[2,1024,128]{2,1,0:T(8,128)}, bf16[2,1024,128]{2,1,0:T(8,128)(2,1)}, bf16[256,256]{1,0:T(8,128)(2,1)}, bf16[256,256]{1,0:T(8,128)(2,1)}, bf1...) custom-call(s32[2]{0:T(128)S(1)} %bitcast.14, s32[2,1,32]{2,1,0:T(1,128)S(1)} %copy-done.8, ...), custom_call_target="tpu_custom_call" | custom-call | tf_op jit(solution)/shard_map/pallas_call | solution.py:57
  19.9 3.0 %all-to-all-done.rec = bf16[16,80,128]{2,1,0:T(8,128)(2,1)S(1)} async-done(((bf16[16,80,128]{2,1,0:T(8,128)(2,1)}), bf16[16,80,128]{2,1,0:T(8,128)(2,1)S(1)}, u32[]{:S(2)}, u32[]{:S(2)}) %all-to-all-start) | async-done | bytes 327712 | tf_op jit(solution)/shard_map/all_to_all | solution.py:482
  22.9 4.7 %shard_map.88 = (f32[136,128]{1,0:T(8,128)S(1)}, f32[136,128]{1,0:T(8,128)S(1)}, bf16[256,1024]{1,0:T(8,128)(2,1)}) custom-call(bf16[16,80,128]{2,1,0:T(8,128)(2,1)S(1)} %all-to-all-done.rec, bf16[256,4096]{1,0:T(8,128)(2,1)} %coarse_hbm.1, bf16[2,1024,128]{2,1,0:T(8,128)(2,1)} %get-tuple-element.44._.refs_1_), custom_call_target="tpu_custom_call" | custom-call | tf_op jit(solution)/shard_map/pallas_call | solution.py:57
  27.7 2.4 %collective-permute-start = (f32[136,128]{1,0:T(8,128)S(1)}, f32[136,128]{1,0:T(8,128)S(1)}, u32[]{:S(2)}, u32[]{:S(2)}) collective-permute-start(f32[136,128]{1,0:T(8,128)S(1)} %get-tuple-element.46), channel_id=1, source_target_pairs={{0,16},{16,0},{1,17},{17,1},{2,18},{18,2},{3,19},{19,3},{4,20},{20... | collective-permute-start | bytes 208904 | tf_op jit(solution)/shard_map/ppermute | solution.py:486
  31.8 8.2 %all-to-all-start.1 = ((bf16[8,144,128]{2,1,0:T(8,128)(2,1)}), bf16[8,144,128]{2,1,0:T(8,128)(2,1)S(1)}, u32[]{:S(2)}, u32[]{:S(2)}) async-start(bf16[8,144,128]{2,1,0:T(8,128)(2,1)} %shard_map.89), calls=%async_computation.1 | async-start | bytes 589824 | tf_op jit(solution)/shard_map/all_to_all | solution.py:482
  40.8 6.6 %collective-permute-done.1._.near.refs_4_ = bf16[2,256,256]{2,1,0:T(8,128)(2,1)S(1)} collective-permute-done((bf16[2,256,256]{2,1,0:T(8,128)(2,1)}, bf16[2,256,256]{2,1,0:T(8,128)(2,1)S(1)}, u32[]{:S(2)}, u32[]{:S(2)}) %collective-permute-start.1) | collective-permute-done | bytes 262176 | tf_op jit(solution)/shard_map/ppermute | solution.py:496
  47.4 5.0 %all-to-all-done.1.rec = bf16[8,144,128]{2,1,0:T(8,128)(2,1)S(1)} async-done(((bf16[8,144,128]{2,1,0:T(8,128)(2,1)}), bf16[8,144,128]{2,1,0:T(8,128)(2,1)S(1)}, u32[]{:S(2)}, u32[]{:S(2)}) %all-to-all-start.1) | async-done | bytes 294944 | tf_op jit(solution)/shard_map/all_to_all | solution.py:482
  52.4 1.6 %shard_map.90 = (bf16[16,128,128]{2,1,0:T(8,128)(2,1)}, f32[8,128]{1,0:T(8,128)}) custom-call(bf16[8,144,128]{2,1,0:T(8,128)(2,1)S(1)} %all-to-all-done.1.rec, bf16[2,256,256]{2,1,0:T(8,128)(2,1)S(1)} %collective-permute-done.1._.near.refs_4_, bf16[2,256,256]{2,1,0:T(8,128)(2,1)S(1)} %collective-permute-done.2.__.other.refs_5_), custom_call_target="tpu_custom_call" | custom-call | tf_op jit(solution)/shard_map/pallas_call | solution.py:57
  54.1 3.6 %all-to-all-start.2 = ((bf16[16,128,128]{2,1,0:T(8,128)(2,1)}), bf16[16,128,128]{2,1,0:T(8,128)(2,1)S(1)}, u32[]{:S(2)}, u32[]{:S(2)}) async-start(bf16[16,128,128]{2,1,0:T(8,128)(2,1)} %get-tuple-element.49), calls=%async_computation.2 | async-start | bytes 1048576 | tf_op jit(solution)/shard_map/all_to_all | solution.py:482
  58.9 3.0 %collective-permute-start.4 = (bf16[256,256]{1,0:T(8,128)(2,1)S(1)}, bf16[256,256]{1,0:T(8,128)(2,1)S(1)}, u32[]{:S(2)}, u32[]{:S(2)}) collective-permute-start(bf16[256,256]{1,0:T(8,128)(2,1)S(1)} %copy-done.9), channel_id=1, source_target_pairs={{16,32},{48,64},{80,96},{112,128},{144,160},{176,192},{208,224},{3... | collective-permute-start | bytes 393224 | tf_op jit(solution)/shard_map/ppermute | solution.py:495
  62.0 3.6 %collective-permute-done.4.__.far.refs_3_ = bf16[256,256]{1,0:T(8,128)(2,1)S(1)} collective-permute-done((bf16[256,256]{1,0:T(8,128)(2,1)S(1)}, bf16[256,256]{1,0:T(8,128)(2,1)S(1)}, u32[]{:S(2)}, u32[]{:S(2)}) %collective-permute-start.4) | collective-permute-done | bytes 131104 | tf_op jit(solution)/shard_map/ppermute | solution.py:495
  65.5 2.0 %all-to-all-done.2.source = bf16[16,128,128]{2,1,0:T(8,128)(2,1)S(1)} async-done(((bf16[16,128,128]{2,1,0:T(8,128)(2,1)}), bf16[16,128,128]{2,1,0:T(8,128)(2,1)S(1)}, u32[]{:S(2)}, u32[]{:S(2)}) %all-to-all-start.2) | async-done | bytes 524320 | tf_op jit(solution)/shard_map/all_to_all | solution.py:482
  67.5 2.5 %collective-permute-start.5 = (bf16[2048,128]{1,0:T(8,128)(2,1)S(1)}, bf16[2048,128]{1,0:T(8,128)(2,1)S(1)}, u32[]{:S(2)}, u32[]{:S(2)}) collective-permute-start(bf16[2048,128]{1,0:T(8,128)(2,1)S(1)} %bitcast.11), channel_id=1, source_target_pairs={{0,16},{16,0},{1,17},{17,1},{2,18},{18,2},{3,19},{19,3},{4,20},{20... | collective-permute-start | bytes 1572872 | tf_op jit(solution)/shard_map/ppermute | solution.py:486
  71.6 7.6 %shard_map.93 = (f32[2,1024,128]{2,1,0:T(8,128)}, f32[2,1024,128]{2,1,0:T(8,128)}, bf16[2,128,1024]{2,1,0:T(8,128)(2,1)}, bf16[16,80,128]{2,1,0:T(8,128)(2,1)}) custom-call(s32[2]{0:T(128)S(1)} %bitcast.15, bf16[2048,128]{1,0:T(8,128)(2,1)S(1)} %bitcast.12, bf16[2048,128]{1,0:T(8,128)(2,1)S(1)} %collective-permute-done.5.sol_other, ...), custom_call_target="tpu_custom_call" | custom-call | tf_op jit(solution)/shard_map/pallas_call | solution.py:57
  79.3 3.7 %all-to-all-start.3 = ((bf16[16,80,128]{2,1,0:T(8,128)(2,1)}), bf16[16,80,128]{2,1,0:T(8,128)(2,1)S(1)}, u32[]{:S(2)}, u32[]{:S(2)}) async-start(bf16[16,80,128]{2,1,0:T(8,128)(2,1)} %get-tuple-element.56), calls=%async_computation.3 | async-start | bytes 655360 | tf_op jit(solution)/shard_map/all_to_all | solution.py:482
  82.9 4.0 %shard_map.94 = (f32[2,1024,128]{2,1,0:T(8,128)}, bf16[256,128]{1,0:T(8,128)(2,1)}, bf16[256,128]{1,0:T(8,128)(2,1)}, bf16[2,256,128]{2,1,0:T(8,128)(2,1)}, bf16[2,256,128]{2,1,0:T(8,128)(2,1)}) custom-call(s32[2]{0:T(128)S(1)} %bitcast.16, bf16[2,128,1024]{2,1,0:T(8,128)(2,1)} %get-tuple-element.58.half_hbm, bf16[2,1,1024,1024]{3,2,1,0:T(8,128)(2,1)} %fac_hbm.7), custom_call_target="tpu_custom_call" | custom-call | tf_op jit(solution)/shard_map/pallas_call | solution.py:57
  86.9 4.6 %all-to-all-done.3.rec = bf16[16,80,128]{2,1,0:T(8,128)(2,1)S(1)} async-done(((bf16[16,80,128]{2,1,0:T(8,128)(2,1)}), bf16[16,80,128]{2,1,0:T(8,128)(2,1)S(1)}, u32[]{:S(2)}, u32[]{:S(2)}) %all-to-all-start.3) | async-done | bytes 327712 | tf_op jit(solution)/shard_map/all_to_all | solution.py:482
  91.9 1.5 collective-permute-start.6
  95.1 6.2 %all-to-all-start.4 = ((bf16[8,144,128]{2,1,0:T(8,128)(2,1)}), bf16[8,144,128]{2,1,0:T(8,128)(2,1)S(1)}, u32[]{:S(2)}, u32[]{:S(2)}) async-start(bf16[8,144,128]{2,1,0:T(8,128)(2,1)} %shard_map.96), calls=%async_computation.4 | async-start | bytes 589824 | tf_op jit(solution)/shard_map/all_to_all | solution.py:482
  102.1 3.9 %collective-permute-done.7._.near = bf16[2,256,128]{2,1,0:T(8,128)(2,1)S(1)} collective-permute-done((bf16[2,256,128]{2,1,0:T(8,128)(2,1)}, bf16[2,256,128]{2,1,0:T(8,128)(2,1)S(1)}, u32[]{:S(2)}, u32[]{:S(2)}) %collective-permute-start.7) | collective-permute-done | bytes 131104 | tf_op jit(solution)/shard_map/ppermute | solution.py:496
  106.0 7.8 %all-to-all-done.4.rec = bf16[8,144,128]{2,1,0:T(8,128)(2,1)S(1)} async-done(((bf16[8,144,128]{2,1,0:T(8,128)(2,1)}), bf16[8,144,128]{2,1,0:T(8,128)(2,1)S(1)}, u32[]{:S(2)}, u32[]{:S(2)}) %all-to-all-start.4) | async-done | bytes 294944 | tf_op jit(solution)/shard_map/all_to_all | solution.py:482
  114.8 3.6 %all-to-all-start.5 = ((bf16[16,128,128]{2,1,0:T(8,128)(2,1)}), bf16[16,128,128]{2,1,0:T(8,128)(2,1)S(1)}, u32[]{:S(2)}, u32[]{:S(2)}) async-start(bf16[16,128,128]{2,1,0:T(8,128)(2,1)} %get-tuple-element.64), calls=%async_computation.5 | async-start | bytes 1048576 | tf_op jit(solution)/shard_map/all_to_all | solution.py:482
  119.6 2.1 %collective-permute-start.10 = (bf16[256,128]{1,0:T(8,128)(2,1)S(1)}, bf16[256,128]{1,0:T(8,128)(2,1)S(1)}, u32[]{:S(2)}, u32[]{:S(2)}) collective-permute-start(bf16[256,128]{1,0:T(8,128)(2,1)S(1)} %copy-done.11), channel_id=1, source_target_pairs={{16,32},{48,64},{80,96},{112,128},{144,160},{176,192},{208,224},{3... | collective-permute-start | bytes 196616 | tf_op jit(solution)/shard_map/ppermute | solution.py:495
  121.8 3.8 %collective-permute-done.10.__.far = bf16[256,128]{1,0:T(8,128)(2,1)S(1)} collective-permute-done((bf16[256,128]{1,0:T(8,128)(2,1)S(1)}, bf16[256,128]{1,0:T(8,128)(2,1)S(1)}, u32[]{:S(2)}, u32[]{:S(2)}) %collective-permute-start.10) | collective-permute-done | bytes 65568 | tf_op jit(solution)/shard_map/ppermute | solution.py:495
  125.5 2.8 %all-to-all-done.5.source = bf16[16,128,128]{2,1,0:T(8,128)(2,1)S(1)} async-done(((bf16[16,128,128]{2,1,0:T(8,128)(2,1)}), bf16[16,128,128]{2,1,0:T(8,128)(2,1)S(1)}, u32[]{:S(2)}, u32[]{:S(2)}) %all-to-all-start.5) | async-done | bytes 524320 | tf_op jit(solution)/shard_map/all_to_all | solution.py:482
  128.3 2.5 %collective-permute-start.11 = (bf16[2048,128]{1,0:T(8,128)(2,1)S(1)}, bf16[2048,128]{1,0:T(8,128)(2,1)S(1)}, u32[]{:S(2)}, u32[]{:S(2)}) collective-permute-start(bf16[2048,128]{1,0:T(8,128)(2,1)S(1)} %bitcast.9), channel_id=1, source_target_pairs={{0,16},{16,0},{1,17},{17,1},{2,18},{18,2},{3,19},{19,3},{4,20},{20... | collective-permute-start | bytes 1572872 | tf_op jit(solution)/shard_map/ppermute | solution.py:486
  130.8 1.6 %shard_map.99 = (f32[2,1024,128]{2,1,0:T(8,128)S(1)}, bf16[2,1024,128]{2,1,0:T(8,128)(2,1)S(1)}, bf16[256,256]{1,0:T(8,128)(2,1)S(1)}, bf16[256,256]{1,0:T(8,128...) custom-call(bf16[16,128,128]{2,1,0:T(8,128)(2,1)S(1)} %shard_map.98._, ...), custom_call_target="tpu_custom_call" | custom-call | tf_op jit(solution)/shard_map/pallas_call | solution.py:57
  132.4 3.4 %shard_map.100 = (f32[2,1024,128]{2,1,0:T(8,128)S(1)}, f32[2,1024,128]{2,1,0:T(8,128)S(1)}, f32[32,8,128]{2,1,0:T(8,128)S(1)}) custom-call(s32[2]{0:T(128)S(1)} %bitcast.17, bf16[2048,128]{1,0:T(8,128)(2,1)S(1)} %bitcast.10, bf16[2048,128]{1,0:T(8,128)(2,1)S(1)} %collective-permute-done.11.sol_other, f32[8,128]{1,0:T(8,128)S(1)} %get-tuple-element.67.stats, ...), custom_call_target="tpu_custom_call" | custom-call | tf_op jit(solution)/shard_map/pallas_call | solution.py:57
  135.9 11.1 %all_to_all.40.rec = f32[32,8,128]{2,1,0:T(8,128)S(1)} all-to-all(f32[32,8,128]{2,1,0:T(8,128)S(1)} %get-tuple-element.75), channel_id=1, replica_groups=mesh['z'=8,'core'=2,'x'=4,'y'=4] {'core','x','y'}, dimensions={0} | all-to-all | bytes 262144 | tf_op jit(solution)/shard_map/all_to_all | solution.py:482
  147.0 9.9 %all_to_all.41.rec = f32[8,8,128]{2,1,0:T(8,128)S(1)} all-to-all(f32[8,8,128]{2,1,0:T(8,128)S(1)} %shard_map.101), channel_id=1, replica_groups=mesh['z'=8,'core'=2,'x'=4,'y'=4] {'z'}, dimensions={0} | all-to-all | bytes 65536 | tf_op jit(solution)/shard_map/all_to_all | solution.py:482
  (49 shorter events, 11.9 us)
Async XLA Ops:
  0.6 14.5 %copy-start.7 = (s32[2,1]{0,1:T(1,128)S(1)}, s32[2,1]{0,1:T(1,128)}, u32[]{:S(2)}) copy-start(s32[2,1]{0,1:T(1,128)} %param.10) | copy-start | bytes 28
  0.6 14.5 %copy-start.8 = (s32[2,1,32]{2,1,0:T(1,128)S(1)}, s32[2,1,32]{2,1,0:T(1,128)}, u32[]{:S(2)}) copy-start(s32[2,1,32]{2,1,0:T(1,128)} %cmap.1) | copy-start | bytes 772
  7.5 15.4 %all-to-all-start = ((bf16[16,80,128]{2,1,0:T(8,128)(2,1)}), bf16[16,80,128]{2,1,0:T(8,128)(2,1)S(1)}, u32[]{:S(2)}, u32[]{:S(2)}) async-start(bf16[16,80,128]{2,1,0:T(8,128)(2,1)} %get-tuple-element.42), calls=%async_computation | async-start | bytes 655360 | tf_op jit(solution)/shard_map/all_to_all | solution.py:482
  19.9 37.8 %copy-start.10 = (bf16[256,256]{1,0:T(8,128)(2,1)S(1)}, bf16[256,256]{1,0:T(8,128)(2,1)}, u32[]{:S(2)}) copy-start(bf16[256,256]{1,0:T(8,128)(2,1)} %get-tuple-element.50) | copy-start | bytes 393220
  19.9 39.1 %copy-start.9 = (bf16[256,256]{1,0:T(8,128)(2,1)S(1)}, bf16[256,256]{1,0:T(8,128)(2,1)}, u32[]{:S(2)}) copy-start(bf16[256,256]{1,0:T(8,128)(2,1)} %get-tuple-element.51) | copy-start | bytes 393220
  27.7 3.3 %collective-permute-start = (f32[136,128]{1,0:T(8,128)S(1)}, f32[136,128]{1,0:T(8,128)S(1)}, u32[]{:S(2)}, u32[]{:S(2)}) collective-permute-start(f32[136,128]{1,0:T(8,128)S(1)} %get-tuple-element.46), channel_id=1, source_target_pairs={{0,16},{16,0},{1,17},{17,1},{2,18},{18,2},{3,19},{19,3},{4,20},{20... | collective-permute-start | bytes 208904 | tf_op jit(solution)/shard_map/ppermute | solution.py:486
  31.8 20.6 %all-to-all-start.1 = ((bf16[8,144,128]{2,1,0:T(8,128)(2,1)}), bf16[8,144,128]{2,1,0:T(8,128)(2,1)S(1)}, u32[]{:S(2)}, u32[]{:S(2)}) async-start(bf16[8,144,128]{2,1,0:T(8,128)(2,1)} %shard_map.89), calls=%async_computation.1 | async-start | bytes 589824 | tf_op jit(solution)/shard_map/all_to_all | solution.py:482
  40.0 7.4 %collective-permute-start.1 = (bf16[2,256,256]{2,1,0:T(8,128)(2,1)}, bf16[2,256,256]{2,1,0:T(8,128)(2,1)S(1)}, u32[]{:S(2)}, u32[]{:S(2)}) collective-permute-start(bf16[2,256,256]{2,1,0:T(8,128)(2,1)} %get-tuple-element.47), channel_id=1, source_target_pairs={{0,1},{1,0},{2,3},{3,2},{4,5},{5,4},{6,7},{7,6},{8,9},{9,8},{10,11... | collective-permute-start | bytes 786440 | tf_op jit(solution)/shard_map/ppermute | solution.py:496
  40.1 7.3 %collective-permute-start.2 = (bf16[2,256,256]{2,1,0:T(8,128)(2,1)}, bf16[2,256,256]{2,1,0:T(8,128)(2,1)S(1)}, u32[]{:S(2)}, u32[]{:S(2)}) collective-permute-start(bf16[2,256,256]{2,1,0:T(8,128)(2,1)} %get-tuple-element.48), channel_id=1, source_target_pairs={{1,2},{3,4},{5,6},{7,8},{9,10},{11,12},{13,14},{2,1},{4,3},{6,5},{... | collective-permute-start | bytes 786440 | tf_op jit(solution)/shard_map/ppermute | solution.py:497
  47.4 31.8 %copy-start = (bf16[2,256,256]{2,1,0:T(8,128)(2,1)}, bf16[2,256,256]{2,1,0:T(8,128)(2,1)S(1)}, u32[]{:S(2)}) copy-start(bf16[2,256,256]{2,1,0:T(8,128)(2,1)S(1)} %collective-permute-done.1._.near.refs_4_) | copy-start | bytes 786436
  47.4 31.8 %copy-start.1 = (bf16[2,256,256]{2,1,0:T(8,128)(2,1)}, bf16[2,256,256]{2,1,0:T(8,128)(2,1)S(1)}, u32[]{:S(2)}) copy-start(bf16[2,256,256]{2,1,0:T(8,128)(2,1)S(1)} %collective-permute-done.2.__.other.refs_5_) | copy-start | bytes 786436
  54.1 13.5 %all-to-all-start.2 = ((bf16[16,128,128]{2,1,0:T(8,128)(2,1)}), bf16[16,128,128]{2,1,0:T(8,128)(2,1)S(1)}, u32[]{:S(2)}, u32[]{:S(2)}) async-start(bf16[16,128,128]{2,1,0:T(8,128)(2,1)} %get-tuple-element.49), calls=%async_computation.2 | async-start | bytes 1048576 | tf_op jit(solution)/shard_map/all_to_all | solution.py:482
  57.7 4.3 %collective-permute-start.3 = (bf16[256,256]{1,0:T(8,128)(2,1)S(1)}, bf16[256,256]{1,0:T(8,128)(2,1)S(1)}, u32[]{:S(2)}, u32[]{:S(2)}) collective-permute-start(bf16[256,256]{1,0:T(8,128)(2,1)S(1)} %copy-done.10), channel_id=1, source_target_pairs={{0,16},{16,0},{32,48},{48,32},{64,80},{80,64},{96,112},{112,96},{1... | collective-permute-start | bytes 393224 | tf_op jit(solution)/shard_map/ppermute | solution.py:494
  58.9 6.6 %collective-permute-start.4 = (bf16[256,256]{1,0:T(8,128)(2,1)S(1)}, bf16[256,256]{1,0:T(8,128)(2,1)S(1)}, u32[]{:S(2)}, u32[]{:S(2)}) collective-permute-start(bf16[256,256]{1,0:T(8,128)(2,1)S(1)} %copy-done.9), channel_id=1, source_target_pairs={{16,32},{48,64},{80,96},{112,128},{144,160},{176,192},{208,224},{3... | collective-permute-start | bytes 393224 | tf_op jit(solution)/shard_map/ppermute | solution.py:495
  61.9 17.3 %copy-start.2 = (bf16[256,256]{1,0:T(8,128)(2,1)}, bf16[256,256]{1,0:T(8,128)(2,1)S(1)}, u32[]{:S(2)}) copy-start(bf16[256,256]{1,0:T(8,128)(2,1)S(1)} %collective-permute-done.3._.chip.refs_2_) | copy-start | bytes 393220
  65.5 13.7 %copy-start.3 = (bf16[256,256]{1,0:T(8,128)(2,1)}, bf16[256,256]{1,0:T(8,128)(2,1)S(1)}, u32[]{:S(2)}) copy-start(bf16[256,256]{1,0:T(8,128)(2,1)S(1)} %collective-permute-done.4.__.far.refs_3_) | copy-start | bytes 393220
  67.5 4.0 %collective-permute-start.5 = (bf16[2048,128]{1,0:T(8,128)(2,1)S(1)}, bf16[2048,128]{1,0:T(8,128)(2,1)S(1)}, u32[]{:S(2)}, u32[]{:S(2)}) collective-permute-start(bf16[2048,128]{1,0:T(8,128)(2,1)S(1)} %bitcast.11), channel_id=1, source_target_pairs={{0,16},{16,0},{1,17},{17,1},{2,18},{18,2},{3,19},{19,3},{4,20},{20... | collective-permute-start | bytes 1572872 | tf_op jit(solution)/shard_map/ppermute | solution.py:486
  79.2 12.3 %copy-start.6 = (bf16[256,1024]{1,0:T(8,128)(2,1)S(1)}, bf16[256,1024]{1,0:T(8,128)(2,1)}, u32[]{:S(2)}) copy-start(bf16[256,1024]{1,0:T(8,128)(2,1)} %get-tuple-element.57.picked_inv) | copy-start | bytes 1572868
  79.3 12.3 %all-to-all-start.3 = ((bf16[16,80,128]{2,1,0:T(8,128)(2,1)}), bf16[16,80,128]{2,1,0:T(8,128)(2,1)S(1)}, u32[]{:S(2)}, u32[]{:S(2)}) async-start(bf16[16,80,128]{2,1,0:T(8,128)(2,1)} %get-tuple-element.56), calls=%async_computation.3 | async-start | bytes 655360 | tf_op jit(solution)/shard_map/all_to_all | solution.py:482
  86.9 31.4 %copy-start.12 = (bf16[256,128]{1,0:T(8,128)(2,1)S(1)}, bf16[256,128]{1,0:T(8,128)(2,1)}, u32[]{:S(2)}) copy-start(bf16[256,128]{1,0:T(8,128)(2,1)} %get-tuple-element.65) | copy-start | bytes 196612
  86.9 32.7 %copy-start.11 = (bf16[256,128]{1,0:T(8,128)(2,1)S(1)}, bf16[256,128]{1,0:T(8,128)(2,1)}, u32[]{:S(2)}) copy-start(bf16[256,128]{1,0:T(8,128)(2,1)} %get-tuple-element.66) | copy-start | bytes 196612
  91.9 2.4 %collective-permute-start.6 = (f32[136,128]{1,0:T(8,128)S(1)}, f32[136,128]{1,0:T(8,128)S(1)}, u32[]{:S(2)}, u32[]{:S(2)}) collective-permute-start(f32[136,128]{1,0:T(8,128)S(1)} %get-tuple-element.61), channel_id=1, source_target_pairs={{0,16},{16,0},{1,17},{17,1},{2,18},{18,2},{3,19},{19,3},{4,20},{20... | collective-permute-start | bytes 208904 | tf_op jit(solution)/shard_map/ppermute | solution.py:486
  95.1 18.7 %all-to-all-start.4 = ((bf16[8,144,128]{2,1,0:T(8,128)(2,1)}), bf16[8,144,128]{2,1,0:T(8,128)(2,1)S(1)}, u32[]{:S(2)}, u32[]{:S(2)}) async-start(bf16[8,144,128]{2,1,0:T(8,128)(2,1)} %shard_map.96), calls=%async_computation.4 | async-start | bytes 589824 | tf_op jit(solution)/shard_map/all_to_all | solution.py:482
  101.3 4.6 %collective-permute-start.7 = (bf16[2,256,128]{2,1,0:T(8,128)(2,1)}, bf16[2,256,128]{2,1,0:T(8,128)(2,1)S(1)}, u32[]{:S(2)}, u32[]{:S(2)}) collective-permute-start(bf16[2,256,128]{2,1,0:T(8,128)(2,1)} %get-tuple-element.62), channel_id=1, source_target_pairs={{0,1},{1,0},{2,3},{3,2},{4,5},{5,4},{6,7},{7,6},{8,9},{9,8},{10,11... | collective-permute-start | bytes 393224 | tf_op jit(solution)/shard_map/ppermute | solution.py:496
  101.4 4.6 %collective-permute-start.8 = (bf16[2,256,128]{2,1,0:T(8,128)(2,1)}, bf16[2,256,128]{2,1,0:T(8,128)(2,1)S(1)}, u32[]{:S(2)}, u32[]{:S(2)}) collective-permute-start(bf16[2,256,128]{2,1,0:T(8,128)(2,1)} %get-tuple-element.63), channel_id=1, source_target_pairs={{1,2},{3,4},{5,6},{7,8},{9,10},{11,12},{13,14},{2,1},{4,3},{6,5},{... | collective-permute-start | bytes 393224 | tf_op jit(solution)/shard_map/ppermute | solution.py:497
  114.8 13.5 %all-to-all-start.5 = ((bf16[16,128,128]{2,1,0:T(8,128)(2,1)}), bf16[16,128,128]{2,1,0:T(8,128)(2,1)S(1)}, u32[]{:S(2)}, u32[]{:S(2)}) async-start(bf16[16,128,128]{2,1,0:T(8,128)(2,1)} %get-tuple-element.64), calls=%async_computation.5 | async-start | bytes 1048576 | tf_op jit(solution)/shard_map/all_to_all | solution.py:482
  118.4 3.4 %collective-permute-start.9 = (bf16[256,128]{1,0:T(8,128)(2,1)S(1)}, bf16[256,128]{1,0:T(8,128)(2,1)S(1)}, u32[]{:S(2)}, u32[]{:S(2)}) collective-permute-start(bf16[256,128]{1,0:T(8,128)(2,1)S(1)} %copy-done.12), channel_id=1, source_target_pairs={{0,16},{16,0},{32,48},{48,32},{64,80},{80,64},{96,112},{112,96},{1... | collective-permute-start | bytes 196616 | tf_op jit(solution)/shard_map/ppermute | solution.py:494
  119.6 5.9 %collective-permute-start.10 = (bf16[256,128]{1,0:T(8,128)(2,1)S(1)}, bf16[256,128]{1,0:T(8,128)(2,1)S(1)}, u32[]{:S(2)}, u32[]{:S(2)}) collective-permute-start(bf16[256,128]{1,0:T(8,128)(2,1)S(1)} %copy-done.11), channel_id=1, source_target_pairs={{16,32},{48,64},{80,96},{112,128},{144,160},{176,192},{208,224},{3... | collective-permute-start | bytes 196616 | tf_op jit(solution)/shard_map/ppermute | solution.py:495
  128.3 28.7 %copy-start.4 = (f32[2,1024,128]{2,1,0:T(8,128)S(1)}, f32[2,1024,128]{2,1,0:T(8,128)}, u32[]{:S(2)}) copy-start(f32[2,1024,128]{2,1,0:T(8,128)} %get-tuple-element.78.search) | copy-start | bytes 3145732
  128.3 28.7 %copy-start.5 = (f32[2,1024,128]{2,1,0:T(8,128)S(1)}, f32[2,1024,128]{2,1,0:T(8,128)}, u32[]{:S(2)}) copy-start(f32[2,1024,128]{2,1,0:T(8,128)} %get-tuple-element.79.prod) | copy-start | bytes 3145732
  128.3 4.1 %collective-permute-start.11 = (bf16[2048,128]{1,0:T(8,128)(2,1)S(1)}, bf16[2048,128]{1,0:T(8,128)(2,1)S(1)}, u32[]{:S(2)}, u32[]{:S(2)}) collective-permute-start(bf16[2048,128]{1,0:T(8,128)(2,1)S(1)} %bitcast.9), channel_id=1, source_target_pairs={{0,16},{16,0},{1,17},{17,1},{2,18},{18,2},{3,19},{19,3},{4,20},{20... | collective-permute-start | bytes 1572872 | tf_op jit(solution)/shard_map/ppermute | solution.py:486
